TPU v7x, 512 devices: a whole 4x8x8 slice. The times are simulated.
512 devices in a mesh: ctx: 16 (over x, z_hi, core), ch: 32 (over z_lo, y).
Axes of the slice: x: 4, y: 8, z: 8 (z_hi: 2, z_lo: 4; z = z_hi * 4 + z_lo), core: 2. Of those that a mesh axis runs over, the one named last changes fastest.
Arguments:
- tokens: bfloat16 [16384, 4096], P('ctx', 'ch'), may hold values from -6 to 6
- in_weights: bfloat16 [3, 4096, 4096], P(None, None, 'ch'), may hold values from -0.09375 to 0.09375
- short_taps: float32 [3, 7, 4096], P(None, None, 'ch'), may hold values from -2 to 2
- residues: float32 [4096, 16], P('ch'), may hold values from -4 to 4
- decays: float32 [4096, 16], P('ch'), may hold values from 3.0517578e-05 to 0.03125
- skip_gain: float32 [4096], P('ch'), may hold values from 0.5 to 1.5
Outputs:
- mixed: float32 [16384, 4096], P('ctx', 'ch')
All inputs are finite; a program needn't handle non-finite values.
Results may differ from a plain program's by a relative error of at most 0.0003.
Values may be sent and summed in bfloat16 or wider, within the bound.
No kernel may reach another device: no remote copies, remote signals or barrier semaphores. Data moves between devices by JAX's collectives and lax.ppermute only.
A program may use at most 64 MiB of HBM per device.

v0:
```python
import math

import jax
import jax.numpy as jnp
from jax import lax
from jax.sharding import PartitionSpec as P

MODES = 16
TAPS = 7


def passed_along(block, axis, distance):
    devices = range(lax.axis_size(axis))
    route = [(i - distance, i) for i in devices if i - distance in devices]
    return lax.ppermute(block, axis, route)


def precise(form, left, right):
    return jnp.einsum(form, left, right, precision=lax.Precision.HIGHEST)


def split_length(length_all):
    chosen = 1
    for candidate in range(1, math.isqrt(length_all) + 1):
        if length_all % candidate == 0:
            chosen = candidate
    return chosen


def angle_table(row_count, col_count, period, col_start):
    row_ids = jnp.arange(row_count, dtype=jnp.int32)[:, None]
    col_ids = jnp.arange(col_count, dtype=jnp.int32)[None, :] + col_start
    product_mod = row_ids * col_ids % period
    angles = product_mod.astype(jnp.float32) * (2.0 * math.pi / period)
    return (jnp.cos(angles), jnp.sin(angles))


def forward_dft(real_in, imag_in, outer_len, inner_len):
    batch_len = real_in.shape[0]
    rows_in = real_in.shape[1] // inner_len
    cos_outer, sin_outer = angle_table(outer_len, rows_in, outer_len, 0)
    real_grid = real_in.reshape(batch_len, rows_in, inner_len)
    first_re = precise("kn,bnm->bkm", cos_outer, real_grid)
    first_im = -precise("kn,bnm->bkm", sin_outer, real_grid)
    imag_grid = imag_in.reshape(batch_len, rows_in, inner_len)
    first_re = first_re + precise("kn,bnm->bkm", sin_outer, imag_grid)
    first_im = first_im + precise("kn,bnm->bkm", cos_outer, imag_grid)
    cos_twist, sin_twist = angle_table(outer_len, inner_len, outer_len * inner_len, 0)
    turned_re = cos_twist * first_re + sin_twist * first_im
    turned_im = cos_twist * first_im - sin_twist * first_re
    cos_inner, sin_inner = angle_table(inner_len, inner_len, inner_len, 0)
    final_re = precise("bkm,jm->bkj", turned_re, cos_inner) + precise(
        "bkm,jm->bkj", turned_im, sin_inner
    )
    final_im = precise("bkm,jm->bkj", turned_im, cos_inner) - precise(
        "bkm,jm->bkj", turned_re, sin_inner
    )
    return (final_re, final_im)


def inverse_dft(spec_re, spec_im, keep_rows):
    batch_len, outer_len, inner_len = spec_re.shape
    cos_inner, sin_inner = angle_table(inner_len, inner_len, inner_len, 0)
    back_re = precise("bkj,mj->bkm", spec_re, cos_inner) - precise(
        "bkj,mj->bkm", spec_im, sin_inner
    )
    back_im = precise("bkj,mj->bkm", spec_im, cos_inner) + precise(
        "bkj,mj->bkm", spec_re, sin_inner
    )
    cos_twist, sin_twist = angle_table(outer_len, inner_len, outer_len * inner_len, 0)
    turned_re = cos_twist * back_re - sin_twist * back_im
    turned_im = cos_twist * back_im + sin_twist * back_re
    cos_outer, sin_outer = angle_table(keep_rows, outer_len, outer_len, 0)
    result_re = precise("nk,bkm->bnm", cos_outer, turned_re) - precise(
        "nk,bkm->bnm", sin_outer, turned_im
    )
    result_re = result_re.reshape(batch_len, keep_rows * inner_len)
    result_im = precise("nk,bkm->bnm", cos_outer, turned_im) + precise(
        "nk,bkm->bnm", sin_outer, turned_re
    )
    return (result_re, result_im.reshape(batch_len, keep_rows * inner_len))


def modal_filter(weights, decays, first_step, count):
    positions = (jnp.arange(count, dtype=jnp.int32) + first_step).astype(jnp.float32)[:, None]
    total = jnp.zeros((count, weights.shape[0]), jnp.float32)
    for which_mode in range(weights.shape[1]):
        total = total + weights[:, which_mode][None, :] * jnp.exp(
            -decays[:, which_mode][None, :] * positions
        )
    return total


def spread_conv(gated, weights, decays):
    devices = lax.axis_size("ctx")
    position = lax.axis_index("ctx")
    seq_dev, width = gated.shape
    slab_len = seq_dev // devices
    length_all = 2 * devices * seq_dev
    local_filter = modal_filter(weights, decays, position * seq_dev, seq_dev)
    signal, kernel = (
        lax.all_to_all(
            gated.reshape(1, seq_dev, width), "ctx", split_axis=1, concat_axis=0, tiled=True
        ),
        lax.all_to_all(
            local_filter.reshape(1, seq_dev, width), "ctx", split_axis=1, concat_axis=0, tiled=True
        ),
    )
    cos_block, sin_block = angle_table(2 * devices, devices, 2 * devices, 0)
    cos_twist, sin_twist = angle_table(2 * devices, slab_len, length_all, position * slab_len)
    cos_twist = cos_twist[:, :, None]
    sin_twist = sin_twist[:, :, None]

    def across(field):
        part_re = precise("rp,ptc->rtc", cos_block, field)
        part_im = -precise("rp,ptc->rtc", sin_block, field)
        return (
            cos_twist * part_re + sin_twist * part_im,
            cos_twist * part_im - sin_twist * part_re,
        )

    sig_re, sig_im = across(signal)
    ker_re, ker_im = across(kernel)
    sig_re, sig_im, ker_re, ker_im = (
        lax.all_to_all(sig_re, "ctx", split_axis=0, concat_axis=1, tiled=True),
        lax.all_to_all(sig_im, "ctx", split_axis=0, concat_axis=1, tiled=True),
        lax.all_to_all(ker_re, "ctx", split_axis=0, concat_axis=1, tiled=True),
        lax.all_to_all(ker_im, "ctx", split_axis=0, concat_axis=1, tiled=True),
    )
    outer_len = split_length(seq_dev)
    inner_len = seq_dev // outer_len

    def along(field_re, field_im):
        flat_re = field_re.transpose(0, 2, 1).reshape(2 * width, seq_dev)
        flat_im = field_im.transpose(0, 2, 1).reshape(2 * width, seq_dev)
        return forward_dft(flat_re, flat_im, outer_len, inner_len)

    zed_re, zed_im = along(sig_re, sig_im)
    hat_re, hat_im = along(ker_re, ker_im)
    prod_re = zed_re * hat_re - zed_im * hat_im
    prod_im = zed_re * hat_im + zed_im * hat_re
    inv_re, inv_im = inverse_dft(prod_re, prod_im, outer_len)
    inv_re = inv_re.reshape(2, width, seq_dev).transpose(0, 2, 1)
    inv_im = inv_im.reshape(2, width, seq_dev).transpose(0, 2, 1)
    back_re, back_im = (
        lax.all_to_all(inv_re, "ctx", split_axis=1, concat_axis=0, tiled=True),
        lax.all_to_all(inv_im, "ctx", split_axis=1, concat_axis=0, tiled=True),
    )
    reverted_re = cos_twist * back_re - sin_twist * back_im
    reverted_im = cos_twist * back_im + sin_twist * back_re
    cos_final, sin_final = angle_table(devices, 2 * devices, 2 * devices, 0)
    blocks = (
        precise("pr,rtc->ptc", cos_final, reverted_re)
        - precise("pr,rtc->ptc", sin_final, reverted_im)
    ) / length_all
    result = lax.all_to_all(blocks, "ctx", split_axis=0, concat_axis=1, tiled=True)
    return result.reshape(seq_dev, width)


def per_device(tokens, in_weights, short_taps, residues, decays, skip_gain):
    seq_dev = tokens.shape[0]
    projected = jnp.einsum(
        "td,sdc->stc",
        lax.all_gather(tokens, "ch", axis=1, tiled=True),
        in_weights,
        preferred_element_type=jnp.float32,
    )
    previous = passed_along(projected[:, seq_dev - (TAPS - 1) :, :], "ctx", 1)
    padded = jnp.concatenate([previous, projected], axis=1)
    filtered = jnp.zeros_like(projected)
    for offset in range(TAPS):
        filtered = (
            filtered + short_taps[:, offset][:, None, :] * padded[:, offset : offset + seq_dev, :]
        )
    gated = filtered[1] * filtered[2]
    weights = residues * jnp.sqrt(2.0 * decays / MODES)
    convolved = spread_conv(gated, weights, decays)
    return filtered[0] * (convolved + skip_gain[None, :] * gated)


def solution(mesh):
    return jax.shard_map(
        per_device,
        mesh=mesh,
        in_specs=(
            P("ctx", "ch"),
            P(None, None, "ch"),
            P(None, None, "ch"),
            P("ch", None),
            P("ch", None),
            P("ch"),
        ),
        out_specs=P("ctx", "ch"),
        check_vma=False,
    )
```

profile of v0, /device:TPU:81, one launch (start us, length us, event | category | flops | bytes accessed | tf_op | source)
XLA Modules:
  0.0 523.2 jit_solution(14387236667966034876)
XLA Ops:
  11.3 12.5 %all-to-all-start.3 = ((f32[1,1024,128]{2,0,1:T(1,128)}), f32[1,1024,128]{2,0,1:T(1,128)}, u32[]{:S(2)}, u32[]{:S(2)}) async-start(f32[1,1024,128]{2,0,1:T(1,128)} %bitcast.253), calls=%async_computation.3 | async-start | bytes 1048576 | tf_op jit(solution)/shard_map/all_to_all | solution.py:105
  23.9 143.5 %all-gather.2.cloned.1.call-done = bf16[1024,4096]{1,0:T(8,128)(2,1)} async-done(((bf16[1024,128]{1,0:T(8,128)(2,1)}), bf16[1024,4096]{1,0:T(8,128)(2,1)}) %all-gather.2.cloned.1.call-update) | async-done | bytes 8388624 | tf_op jit(solution)/shard_map/all_gather | solution.py:164
  167.4 5.9 %fusion.19 = f32[3,1024,128]{1,2,0:T(8,128)S(1)} fusion(bf16[3,4096,128]{2,1,0:T(8,128)(2,1)S(1)} %copy-done, bf16[1024,4096]{1,0:T(8,128)(2,1)} %all-gather.2.cloned.1.call-done), kind=kOutput, calls=%fused_computation.30 | convolution fusion | flops 3221225472 | bytes 13107200 | tf_op jit(solution)/shard_map/td,sdc->stc/dot_general | solution.py:162
  173.4 24.7 %collective-permute-start = (f32[3,6,128]{1,2,0:T(8,128)S(1)}, f32[3,6,128]{1,2,0:T(8,128)S(1)}, u32[]{:S(2)}, u32[]{:S(2)}) collective-permute-start(f32[3,6,128]{1,2,0:T(8,128)S(1)} %slice.196), channel_id=1, source_target_pairs={{0,32},{32,64},{64,96},{96,128},{128,160},{160,192},{192,224},{224... | collective-permute-start | bytes 27656 | tf_op jit(solution)/shard_map/ppermute | solution.py:15
  198.1 3.6 collective-permute-done
  201.7 3.4 fusion.6
  206.4 12.1 %all-to-all-start = ((f32[1,1024,128]{2,0,1:T(1,128)}), f32[1,1024,128]{2,0,1:T(1,128)S(1)}, u32[]{:S(2)}, u32[]{:S(2)}) async-start(f32[1,1024,128]{2,0,1:T(1,128)} %copy.167), calls=%async_computation | async-start | bytes 1048576 | tf_op jit(solution)/shard_map/all_to_all | solution.py:102
  218.7 3.2 convolution_negate_fusion
  221.9 16.5 %all-to-all-done = f32[1,1024,128]{2,0,1:T(1,128)S(1)} async-done(((f32[1,1024,128]{2,0,1:T(1,128)}), f32[1,1024,128]{2,0,1:T(1,128)S(1)}, u32[]{:S(2)}, u32[]{:S(2)}) %all-to-all-start) | async-done | bytes 524320 | tf_op jit(solution)/shard_map/all_to_all | solution.py:102
  240.8 4.0 multiply_subtract_fusion.3
  246.4 5.3 %all-to-all-start.4 = ((f32[32,64,128]{2,1,0:T(8,128)}), f32[32,64,128]{2,1,0:T(8,128)}, u32[]{:S(2)}, u32[]{:S(2)}) async-start(f32[32,64,128]{2,1,0:T(8,128)} %copy.186), calls=%async_computation.4 | async-start | bytes 2097152 | tf_op jit(solution)/shard_map/all_to_all | solution.py:127
  253.3 26.2 %all-to-all-done.4 = f32[32,64,128]{2,1,0:T(8,128)} async-done(((f32[32,64,128]{2,1,0:T(8,128)}), f32[32,64,128]{2,1,0:T(8,128)}, u32[]{:S(2)}, u32[]{:S(2)}) %all-to-all-start.4) | async-done | bytes 1048608 | tf_op jit(solution)/shard_map/all_to_all | solution.py:127
  279.5 4.6 all-to-all-start.5
  285.7 26.9 %all-to-all-done.5 = f32[32,64,128]{2,1,0:T(8,128)} async-done(((f32[32,64,128]{2,1,0:T(8,128)}), f32[32,64,128]{2,1,0:T(8,128)}, u32[]{:S(2)}, u32[]{:S(2)}) %all-to-all-start.5) | async-done | bytes 1048608 | tf_op jit(solution)/shard_map/all_to_all | solution.py:128
  312.5 3.9 all-to-all-start.1
  318.1 27.4 %all-to-all-done.1 = f32[32,64,128]{2,1,0:T(8,128)S(1)} async-done(((f32[32,64,128]{2,1,0:T(8,128)}), f32[32,64,128]{2,1,0:T(8,128)S(1)}, u32[]{:S(2)}, u32[]{:S(2)}) %all-to-all-start.1) | async-done | bytes 1048608 | tf_op jit(solution)/shard_map/all_to_all | solution.py:125
  345.5 4.6 all-to-all-start.2
  372.6 6.0 %all-to-all-done.2 = f32[32,64,128]{2,1,0:T(8,128)} async-done(((f32[32,64,128]{2,1,0:T(8,128)}), f32[32,64,128]{2,1,0:T(8,128)}, u32[]{:S(2)}, u32[]{:S(2)}) %all-to-all-start.2) | async-done | bytes 1048608 | tf_op jit(solution)/shard_map/all_to_all | solution.py:126
  383.7 3.1 fusion.27
  418.4 4.9 all-to-all-start.7
  427.6 24.0 %all-to-all-done.7 = f32[2,1024,128]{2,0,1:T(2,128)} async-done(((f32[2,1024,128]{2,0,1:T(2,128)}), f32[2,1024,128]{2,0,1:T(2,128)}, u32[]{:S(2)}, u32[]{:S(2)}) %all-to-all-start.7) | async-done | bytes 1048608 | tf_op jit(solution)/shard_map/all_to_all | solution.py:147
  451.6 3.9 all-to-all-start.6
  457.7 26.9 %all-to-all-done.6 = f32[2,1024,128]{2,0,1:T(2,128)S(1)} async-done(((f32[2,1024,128]{2,0,1:T(2,128)}), f32[2,1024,128]{2,0,1:T(2,128)S(1)}, u32[]{:S(2)}, u32[]{:S(2)}) %all-to-all-start.6) | async-done | bytes 1048608 | tf_op jit(solution)/shard_map/all_to_all | solution.py:146
  487.9 21.6 %all_to_all.141 = f32[16,64,128]{2,1,0:T(8,128)} all-to-all(f32[16,64,128]{2,1,0:T(8,128)S(1)} %copy.212), channel_id=1, replica_groups=mesh['ctx'=16,'ch'=32] {'ctx'}, dimensions={0} | all-to-all | bytes 1048576 | tf_op jit(solution)/shard_map/all_to_all | solution.py:156
  (102 shorter events, 90.7 us)
Async XLA Ops:
  6.5 160.9 %copy-start = (bf16[3,4096,128]{2,1,0:T(8,128)(2,1)S(1)}, bf16[3,4096,128]{2,1,0:T(8,128)(2,1)}, u32[]{:S(2)}) copy-start(bf16[3,4096,128]{2,1,0:T(8,128)(2,1)} %param.7) | copy-start | bytes 9437188
  6.5 160.8 %all-gather.2.cloned.1.call-start = ((), (), s32[]{:S(2)}) async-start(), calls=%async_computation.9 | async-start | bytes 8650752 | tf_op jit(solution)/shard_map/all_gather | solution.py:164
  9.1 14.8 %copy-start.10 = (f32[3,7,128]{2,1,0:T(8,128)S(1)}, f32[3,7,128]{2,1,0:T(8,128)}, u32[]{:S(2)}) copy-start(f32[3,7,128]{2,1,0:T(8,128)} %param.8) | copy-start | bytes 32260
  11.3 195.0 %all-to-all-start.3 = ((f32[1,1024,128]{2,0,1:T(1,128)}), f32[1,1024,128]{2,0,1:T(1,128)}, u32[]{:S(2)}, u32[]{:S(2)}) async-start(f32[1,1024,128]{2,0,1:T(1,128)} %bitcast.253), calls=%async_computation.3 | async-start | bytes 1048576 | tf_op jit(solution)/shard_map/all_to_all | solution.py:105
  173.4 28.3 %collective-permute-start = (f32[3,6,128]{1,2,0:T(8,128)S(1)}, f32[3,6,128]{1,2,0:T(8,128)S(1)}, u32[]{:S(2)}, u32[]{:S(2)}) collective-permute-start(f32[3,6,128]{1,2,0:T(8,128)S(1)} %slice.196), channel_id=1, source_target_pairs={{0,32},{32,64},{64,96},{96,128},{128,160},{160,192},{192,224},{224... | collective-permute-start | bytes 27656 | tf_op jit(solution)/shard_map/ppermute | solution.py:15
  205.1 39.8 %copy-start.2 = (f32[3,1024,128]{1,2,0:T(8,128)}, f32[3,1024,128]{1,2,0:T(8,128)S(1)}, u32[]{:S(2)}) copy-start(f32[3,1024,128]{1,2,0:T(8,128)S(1)} %fusion.6) | copy-start | bytes 4718596
  206.4 32.0 %all-to-all-start = ((f32[1,1024,128]{2,0,1:T(1,128)}), f32[1,1024,128]{2,0,1:T(1,128)S(1)}, u32[]{:S(2)}, u32[]{:S(2)}) async-start(f32[1,1024,128]{2,0,1:T(1,128)} %copy.167), calls=%async_computation | async-start | bytes 1048576 | tf_op jit(solution)/shard_map/all_to_all | solution.py:102
  238.4 2.5 copy-start.6
  246.4 5.3 %copy-start.7 = (f32[32,64,128]{2,0,1:T(8,128)S(1)}, f32[32,64,128]{2,0,1:T(8,128)}, u32[]{:S(2)}) copy-start(f32[32,64,128]{2,0,1:T(8,128)} %get-tuple-element.9) | copy-start | bytes 3145732
  246.4 33.1 %all-to-all-start.4 = ((f32[32,64,128]{2,1,0:T(8,128)}), f32[32,64,128]{2,1,0:T(8,128)}, u32[]{:S(2)}, u32[]{:S(2)}) async-start(f32[32,64,128]{2,1,0:T(8,128)} %copy.186), calls=%async_computation.4 | async-start | bytes 2097152 | tf_op jit(solution)/shard_map/all_to_all | solution.py:127
  253.3 30.8 %copy-start.3 = (f32[32,64,128]{2,0,1:T(8,128)S(1)}, f32[32,64,128]{2,0,1:T(8,128)}, u32[]{:S(2)}) copy-start(f32[32,64,128]{2,0,1:T(8,128)} %get-tuple-element.17) | copy-start | bytes 3145732
  279.5 33.0 %all-to-all-start.5 = ((f32[32,64,128]{2,1,0:T(8,128)}), f32[32,64,128]{2,1,0:T(8,128)}, u32[]{:S(2)}, u32[]{:S(2)}) async-start(f32[32,64,128]{2,1,0:T(8,128)} %copy.190), calls=%async_computation.5 | async-start | bytes 2097152 | tf_op jit(solution)/shard_map/all_to_all | solution.py:128
  312.5 32.9 %all-to-all-start.1 = ((f32[32,64,128]{2,1,0:T(8,128)}), f32[32,64,128]{2,1,0:T(8,128)S(1)}, u32[]{:S(2)}, u32[]{:S(2)}) async-start(f32[32,64,128]{2,1,0:T(8,128)} %copy.170), calls=%async_computation.1 | async-start | bytes 2097152 | tf_op jit(solution)/shard_map/all_to_all | solution.py:125
  345.5 6.2 %copy-start.8 = (f32[32,64,128]{2,1,0:T(8,128)}, f32[32,64,128]{2,1,0:T(8,128)S(1)}, u32[]{:S(2)}) copy-start(f32[32,64,128]{2,1,0:T(8,128)S(1)} %all-to-all-done.1) | copy-start | bytes 3145732
  345.5 33.1 %all-to-all-start.2 = ((f32[32,64,128]{2,1,0:T(8,128)}), f32[32,64,128]{2,1,0:T(8,128)}, u32[]{:S(2)}, u32[]{:S(2)}) async-start(f32[32,64,128]{2,1,0:T(8,128)} %copy.174), calls=%async_computation.2 | async-start | bytes 2097152 | tf_op jit(solution)/shard_map/all_to_all | solution.py:126
  356.5 2.2 copy-start.9
  383.7 3.1 copy-start.5
  388.6 1.8 copy-start.4
  418.4 33.2 %all-to-all-start.7 = ((f32[2,1024,128]{2,0,1:T(2,128)}), f32[2,1024,128]{2,0,1:T(2,128)}, u32[]{:S(2)}, u32[]{:S(2)}) async-start(f32[2,1024,128]{2,0,1:T(2,128)} %bitcast.69), calls=%async_computation.7 | async-start | bytes 2097152 | tf_op jit(solution)/shard_map/all_to_all | solution.py:147
  451.6 32.9 %all-to-all-start.6 = ((f32[2,1024,128]{2,0,1:T(2,128)}), f32[2,1024,128]{2,0,1:T(2,128)S(1)}, u32[]{:S(2)}, u32[]{:S(2)}) async-start(f32[2,1024,128]{2,0,1:T(2,128)} %bitcast.64), calls=%async_computation.6 | async-start | bytes 2097152 | tf_op jit(solution)/shard_map/all_to_all | solution.py:146
  487.7 24.0 %copy-start.11 = (f32[128]{0:T(128)S(1)}, f32[128]{0:T(128)}, u32[]{:S(2)}) copy-start(f32[128]{0:T(128)} %param.11) | copy-start | bytes 1540
  509.5 6.7 %copy-start.1 = (bf16[3,4096,128]{2,1,0:T(8,128)(2,1)S(1)}, bf16[3,4096,128]{2,1,0:T(8,128)(2,1)}, u32[]{:S(2)}) copy-start(bf16[3,4096,128]{2,1,0:T(8,128)(2,1)} %param.7) | copy-start | bytes 9437188
Sparse Core Ops, SparseCore 0:
  9.4 157.9 all-gather.1
where the time goes:
time: 533 us; the launch traced here: 523 us
  waiting for transfers between devices  302 us (57%)
  starting transfers between devices  76.4 us (14%)
  matrix products  60 us (11%)
  local copies, waits for them, and re-layouts  36.9 us (7%)
  blocking collectives  21.6 us (4%)
  between operations  14.1 us (3%)
  other arithmetic  12.7 us (2%)
    all_gather x1, waiting for transfers between devices, per_device(): lax.all_gather(tokens, 'ch', axis=1, tiled=True)  143 us
    dot_general x30, matrix products, precise(): return jnp.einsum(form, left, right, precision=lax.Precision.HIGHEST)  54.1 us
    all_to_all x1, waiting for transfers between devices, spread_conv(): lax.all_to_all(sig_re, 'ctx', split_axis=0, concat_axis=1, tiled=True)  27.4 us
    all_to_all x1, waiting for transfers between devices, spread_conv(): lax.all_to_all(inv_re, 'ctx', split_axis=1, concat_axis=0, tiled=True)  26.9 us
    all_to_all x1, waiting for transfers between devices, spread_conv(): lax.all_to_all(ker_im, 'ctx', split_axis=0, concat_axis=1, tiled=True)  26.9 us
    all_to_all x1, waiting for transfers between devices, spread_conv(): lax.all_to_all(ker_re, 'ctx', split_axis=0, concat_axis=1, tiled=True)  26.2 us
    ppermute x1, starting transfers between devices, passed_along(): return lax.ppermute(block, axis, route)  24.7 us
    all_to_all x1, waiting for transfers between devices, spread_conv(): lax.all_to_all(inv_im, 'ctx', split_axis=1, concat_axis=0, tiled=True)  24 us
  transfers between devices with their start and end apart: 10, of which 9 were waited for; matrix products, arithmetic and copies ran while one was open for 10% of the time, Pallas kernels for 0%

commit v1 on v0

v1 whole, which is shorter than its diff:
```python
import functools

import jax
import jax.numpy as jnp
from jax import lax
from jax.experimental import pallas as pl
from jax.experimental.pallas import tpu as pltpu
from jax.sharding import PartitionSpec as P

MODES = 16
TAPS = 7
HALO = 8
CHUNKS = 8
UNROLL = 8
LANES = 128


def wide(row):
    return jnp.broadcast_to(row, (CHUNKS, LANES))


def local_kernel(length, proj, taps, weights, decays, skip, first, direct, starts, last, ends):
    poles = [wide(jnp.exp(-decays[m : m + 1, :])) for m in range(MODES)]
    gains = [wide(weights[m : m + 1, :]) for m in range(MODES)]
    skip_row = wide(skip[0:1, :])

    def steps(at, states):
        states = list(states)
        at = at * UNROLL
        rows = [
            [
                proj[s, pl.ds(at + HALO - (TAPS - 1) + k, CHUNKS, stride=length), :]
                for k in range(UNROLL + TAPS - 1)
            ]
            for s in range(3)
        ]
        coef = [[wide(taps[s, j : j + 1, :]) for j in range(TAPS)] for s in range(3)]
        for u in range(UNROLL):
            filtered = [sum(coef[s][j] * rows[s][u + j] for j in range(TAPS)) for s in range(3)]
            gated = filtered[1] * filtered[2]
            total = skip_row * gated
            for m in range(MODES):
                states[m] = poles[m] * states[m] + gated
                total = total + gains[m] * states[m]
            here = pl.ds(pl.multiple_of((at + u) * CHUNKS, CHUNKS), CHUNKS)
            first[here, :] = filtered[0]
            direct[here, :] = filtered[0] * total
        return tuple(states)

    zero = jnp.zeros((CHUNKS, LANES), jnp.float32)
    states = lax.fori_loop(0, length // UNROLL, steps, (zero,) * MODES)
    for m in range(MODES):
        ends[m * CHUNKS : (m + 1) * CHUNKS, :] = states[m]
    over = jnp.exp(-decays[...] * float(length))
    carry = jnp.zeros((MODES, LANES), jnp.float32)
    for c in range(CHUNKS):
        starts[c] = carry
        carry = over * carry + ends[pl.ds(c, MODES, stride=CHUNKS), :]
    last[...] = carry


def local_part(proj, taps, weights, decays, skip):
    rows = proj.shape[1] - HALO
    width = proj.shape[2]
    flat = jax.ShapeDtypeStruct((rows, width), jnp.float32)
    column = lambda n: pl.BlockSpec((n, LANES), lambda i: (0, i))
    return pl.pallas_call(
        functools.partial(local_kernel, rows // CHUNKS),
        grid=(width // LANES,),
        in_specs=[
            pl.BlockSpec((3, rows + HALO, LANES), lambda i: (0, 0, i)),
            pl.BlockSpec((3, TAPS, LANES), lambda i: (0, 0, i)),
            column(MODES),
            column(MODES),
            column(1),
        ],
        out_specs=[
            column(rows),
            column(rows),
            pl.BlockSpec((CHUNKS, MODES, LANES), lambda i: (0, 0, i)),
            column(MODES),
        ],
        out_shape=[
            flat,
            flat,
            jax.ShapeDtypeStruct((CHUNKS, MODES, width), jnp.float32),
            jax.ShapeDtypeStruct((MODES, width), jnp.float32),
        ],
        scratch_shapes=[pltpu.VMEM((MODES * CHUNKS, LANES), jnp.float32)],
        compiler_params=pltpu.CompilerParams(vmem_limit_bytes=32 * 2**20),
        cost_estimate=pl.CostEstimate(
            flops=rows * width * 110, bytes_accessed=rows * width * 20, transcendentals=0
        ),
    )(proj, taps, weights, decays, skip)


def final_kernel(length, carried, first, direct, starts, weights, decays, out, begins):
    over = jnp.exp(-decays[...] * float(length))
    reach = jnp.ones_like(over)
    for c in range(CHUNKS):
        begins[pl.ds(c, MODES, stride=CHUNKS), :] = weights[...] * (starts[c] + reach * carried[...])
        reach = reach * over
    poles = [wide(jnp.exp(-decays[m : m + 1, :])) for m in range(MODES)]

    def steps(at, terms):
        terms = list(terms)
        at = at * UNROLL
        for u in range(UNROLL):
            terms = [poles[m] * terms[m] for m in range(MODES)]
            sums = terms
            while len(sums) > 1:
                sums = [sums[i] + sums[i + 1] for i in range(0, len(sums), 2)]
            here = pl.ds(pl.multiple_of((at + u) * CHUNKS, CHUNKS), CHUNKS)
            out[pl.ds(at + u, CHUNKS, stride=length), :] = direct[here, :] + first[here, :] * sums[0]
        return tuple(terms)

    terms = tuple(begins[m * CHUNKS : (m + 1) * CHUNKS, :] for m in range(MODES))
    lax.fori_loop(0, length // UNROLL, steps, terms)


def final_part(carried, first, direct, starts, weights, decays):
    rows, width = first.shape
    column = lambda n: pl.BlockSpec((n, LANES), lambda i: (0, i))
    return pl.pallas_call(
        functools.partial(final_kernel, rows // CHUNKS),
        grid=(width // LANES,),
        in_specs=[
            column(MODES),
            column(rows),
            column(rows),
            pl.BlockSpec((CHUNKS, MODES, LANES), lambda i: (0, 0, i)),
            column(MODES),
            column(MODES),
        ],
        out_specs=column(rows),
        out_shape=jax.ShapeDtypeStruct((rows, width), jnp.float32),
        scratch_shapes=[pltpu.VMEM((MODES * CHUNKS, LANES), jnp.float32)],
        compiler_params=pltpu.CompilerParams(vmem_limit_bytes=32 * 2**20),
        cost_estimate=pl.CostEstimate(
            flops=rows * width * 36, bytes_accessed=rows * width * 12, transcendentals=0
        ),
    )(carried, first, direct, starts, weights, decays)


def per_device(tokens, in_weights, short_taps, residues, decays, skip_gain):
    rows = tokens.shape[0]
    blocks = lax.axis_size("ctx")
    mine = lax.axis_index("ctx")
    weights = (residues * jnp.sqrt(2.0 * decays / MODES)).T
    rates = decays.T
    projected = jnp.einsum(
        "td,sdc->stc",
        lax.all_gather(tokens, "ch", axis=1, tiled=True),
        in_weights,
        preferred_element_type=jnp.float32,
    )
    previous = lax.ppermute(
        projected[:, rows - HALO :, :], "ctx", [(i, i + 1) for i in range(blocks - 1)]
    )
    padded = jnp.concatenate([previous, projected], axis=1)
    first, direct, starts, last = local_part(
        padded, short_taps, weights, rates, skip_gain[None, :]
    )
    ahead = jnp.arange(blocks) - mine - 1
    ahead = ahead[:, None, None]
    worth = jnp.where(
        ahead >= 0, jnp.exp(-rates[None] * (rows * jnp.maximum(ahead, 0)).astype(jnp.float32)), 0.0
    )
    arrived = lax.all_to_all(worth * last[None], "ctx", split_axis=0, concat_axis=0, tiled=True)
    return final_part(jnp.sum(arrived, axis=0), first, direct, starts, weights, rates)


def solution(mesh):
    return jax.shard_map(
        per_device,
        mesh=mesh,
        in_specs=(
            P("ctx", "ch"),
            P(None, None, "ch"),
            P(None, None, "ch"),
            P("ch", None),
            P("ch", None),
            P("ch"),
        ),
        out_specs=P("ctx", "ch"),
        check_vma=False,
    )
```

time: 533 us -> 239 us (0.45)
  the two profiles are of different devices: /device:TPU:81 before, /device:TPU:1 now
where the time goes in v1:
time: 239 us; the launch traced here: 238 us
  waiting for transfers between devices  162 us (68%)
  starting transfers between devices  26.9 us (11%)
  blocking collectives  18.8 us (8%)
  between operations  13.5 us (6%)
  matrix products  6.86 us (3%)
  Pallas kernels  5.07 us (2%)
  local copies, waits for them, and re-layouts  3.68 us (2%)
    all_gather x1, waiting for transfers between devices, per_device(): lax.all_gather(tokens, 'ch', axis=1, tiled=True)  160 us
    ppermute x1, starting transfers between devices, per_device(): lax.ppermute(projected[:, rows - HALO:, :], 'ctx', [(i, i + 1) for i in r...  26.9 us
    all_to_all x1, blocking collectives, per_device(): lax.all_to_all(worth * last[None], 'ctx', split_axis=0, concat_axis=0, ti...  18.8 us
    dot_general x1, matrix products, per_device(): jnp.einsum('td,sdc->stc', lax.all_gather(tokens, 'ch', axis=1, tiled=True...  6.86 us
  transfers between devices with their start and end apart: 2, of which 2 were waited for; matrix products, arithmetic and copies ran while one was open for 1% of the time, Pallas kernels for 0%

profile of v1, /device:TPU:1, one launch (start us, length us, event | category | flops | bytes accessed | tf_op | source)
XLA Modules:
  0.0 238.4 jit_solution(11011747318266028580)
XLA Ops:
  6.5 0.0 copy-start
  6.5 0.0 all-gather.2.cloned.1.call-start
  6.5 0.7 all-gather.2.cloned.1.call-update
  7.3 0.9 bitcast_negate_fusion
  8.2 0.7 multiply_bitcast_fusion.weights
  8.9 160.1 %all-gather.2.cloned.1.call-done = bf16[1024,4096]{1,0:T(8,128)(2,1)} async-done(((bf16[1024,128]{1,0:T(8,128)(2,1)}), bf16[1024,4096]{1,0:T(8,128)(2,1)}) %all-gather.2.cloned.1.call-update) | async-done | bytes 8388624 | tf_op jit(solution)/shard_map/all_gather | solution.py:153
  169.1 0.0 copy-done
  169.1 6.9 %fusion.2 = f32[3,1024,128]{2,1,0:T(8,128)S(1)} fusion(bf16[3,4096,128]{2,1,0:T(8,128)(2,1)S(1)} %copy-done, bf16[1024,4096]{1,0:T(8,128)(2,1)} %all-gather.2.cloned.1.call-done), kind=kOutput, calls=%fused_computation.3 | convolution fusion | flops 3221225472 | bytes 13107200 | tf_op jit(solution)/shard_map/td,sdc->stc/dot_general | solution.py:151
  175.9 0.0 copy-start.5
  175.9 0.0 copy-start.6
  175.9 0.0 copy-start.7
  176.0 26.9 %collective-permute-start = (f32[3,8,128]{2,1,0:T(8,128)S(1)}, f32[3,8,128]{2,1,0:T(8,128)S(1)}, u32[]{:S(2)}, u32[]{:S(2)}) collective-permute-start(f32[3,8,128]{2,1,0:T(8,128)S(1)} %slice.4), channel_id=1, source_target_pairs={{0,32},{32,64},{64,96},{96,128},{128,160},{160,192},{192,224},{224... | collective-permute-start | bytes 36872 | tf_op jit(solution)/shard_map/ppermute | solution.py:157
  202.9 0.8 collective-permute-done
  203.7 0.1 pad_maximum_fusion.proj
  203.9 3.5 %shard_map.64 = (f32[1024,128]{1,0:T(8,128)S(1)}, f32[1024,128]{1,0:T(8,128)S(1)}, f32[8,16,128]{2,1,0:T(8,128)S(1)}, f32[16,128]{1,0:T(8,128)S(1)}) custom-call(f32[3,1032,128]{2,1,0:T(8,128)S(1)} %pad_maximum_fusion.proj, f32[3,7,128]{2,1,0:T(8,128)S(1)} %copy-done.6, f32[16,128]{1,0:T(8,128)S(1)} %multiply_bitcast_fusion.weights, f32[16,128]{1,0:T(8,128)S(1)} %bitcast.13, ...), custom_call_target="tpu_custom_call" | custom-call | flops 14417920 | bytes 2621440 | tf_op jit(solution)/shard_map/pallas_call | solution.py:67
  207.4 0.0 copy-start.1
  207.4 0.8 copy-done.1
  208.2 0.8 copy-done.3
  209.0 0.1 select_multiply_fusion
  209.1 18.8 %all_to_all.5 = f32[16,16,128]{2,1,0:T(8,128)S(1)} all-to-all(f32[16,16,128]{2,1,0:T(8,128)S(1)} %select_multiply_fusion), channel_id=1, replica_groups=mesh['ctx'=16,'ch'=32] {'ctx'}, dimensions={0} | all-to-all | bytes 262144 | tf_op jit(solution)/shard_map/all_to_all | solution.py:169
  227.9 0.0 copy-start.2
  227.9 1.0 copy-done.2
  229.0 1.0 copy-done.4
  230.0 1.5 shard_map.65
  (9 shorter events, 0.1 us)
Async XLA Ops:
  6.5 162.5 %copy-start = (bf16[3,4096,128]{2,1,0:T(8,128)(2,1)S(1)}, bf16[3,4096,128]{2,1,0:T(8,128)(2,1)}, u32[]{:S(2)}) copy-start(bf16[3,4096,128]{2,1,0:T(8,128)(2,1)} %param.7) | copy-start | bytes 9437188
  6.5 162.5 %all-gather.2.cloned.1.call-start = ((), (), s32[]{:S(2)}) async-start(), calls=%async_computation.1 | async-start | bytes 8650752 | tf_op jit(solution)/shard_map/all_gather | solution.py:153
  175.9 27.9 %copy-start.5 = (f32[128,16]{0,1:T(8,128)S(1)}, f32[128,16]{0,1:T(8,128)}, u32[]{:S(2)}) copy-start(f32[128,16]{0,1:T(8,128)} %param.10) | copy-start | bytes 24580
  175.9 27.9 %copy-start.6 = (f32[3,7,128]{2,1,0:T(8,128)S(1)}, f32[3,7,128]{2,1,0:T(8,128)}, u32[]{:S(2)}) copy-start(f32[3,7,128]{2,1,0:T(8,128)} %taps.1) | copy-start | bytes 32260
  175.9 27.9 %copy-start.7 = (f32[128]{0:T(128)S(1)}, f32[128]{0:T(128)}, u32[]{:S(2)}) copy-start(f32[128]{0:T(128)} %param.11) | copy-start | bytes 1540
  176.0 27.8 %collective-permute-start = (f32[3,8,128]{2,1,0:T(8,128)S(1)}, f32[3,8,128]{2,1,0:T(8,128)S(1)}, u32[]{:S(2)}, u32[]{:S(2)}) collective-permute-start(f32[3,8,128]{2,1,0:T(8,128)S(1)} %slice.4), channel_id=1, source_target_pairs={{0,32},{32,64},{64,96},{96,128},{128,160},{160,192},{192,224},{224... | collective-permute-start | bytes 36872 | tf_op jit(solution)/shard_map/ppermute | solution.py:157
  207.4 0.8 copy-start.1
  208.2 0.8 copy-start.3
  227.9 1.0 copy-start.2
  229.0 1.0 copy-start.4
Sparse Core Ops, SparseCore 0:
  9.4 159.6 all-gather.1

commit v2 on v1

--- a/solution.py
+++ b/solution.py
@@ -2,6 +2,7 @@
 
 import jax
 import jax.numpy as jnp
+import numpy as np
 from jax import lax
 from jax.experimental import pallas as pl
 from jax.experimental.pallas import tpu as pltpu
@@ -9,7 +10,7 @@
 
 MODES = 16
 TAPS = 7
-HALO = 8
+HALO = 16
 CHUNKS = 8
 UNROLL = 8
 LANES = 128
@@ -142,27 +143,108 @@
     )(carried, first, direct, starts, weights, decays)
 
 
+def project_kernel(count, ids, *refs):
+    blocks, weights = refs[:count], refs[count : 5 * count]
+    sums, out = refs[5 * count : -1], refs[-1]
+    total = None
+    for b in range(count):
+        wide_weights = jnp.concatenate(
+            [
+                jnp.concatenate([weights[4 * b + z][s] for s in range(3)], axis=1)
+                for z in range(4)
+            ],
+            axis=0,
+        )
+        part = jnp.dot(blocks[b][...], wide_weights, preferred_element_type=jnp.float32)
+        total = part if total is None else total + part
+    for s in range(3):
+        here = total[:, s * LANES : (s + 1) * LANES]
+        out[s] = here + sums[0][s] if sums else here
+
+
+def project(sums, blocks, ids, at, in_weights):
+    rows, depth = blocks[0].shape
+    count = len(blocks)
+    tile = rows // 5 if rows % 80 == 0 else rows // 3
+    piece = lambda k: pl.BlockSpec((3, LANES, LANES), lambda i, ids: (0, ids[4 * at + k], 0))
+    total = pl.BlockSpec((3, tile, LANES), lambda i, ids: (0, i, 0))
+    extra = [] if sums is None else [sums]
+    return pl.pallas_call(
+        functools.partial(project_kernel, count),
+        grid_spec=pltpu.PrefetchScalarGridSpec(
+            num_scalar_prefetch=1,
+            grid=(rows // tile,),
+            in_specs=[pl.BlockSpec((tile, depth), lambda i, ids: (i, 0))] * count
+            + [piece(k) for k in range(4 * count)]
+            + [total] * len(extra),
+            out_specs=total,
+        ),
+        out_shape=jax.ShapeDtypeStruct((3, rows, LANES), jnp.float32),
+        input_output_aliases={1 + 5 * count: 0} if extra else {},
+        compiler_params=pltpu.CompilerParams(vmem_limit_bytes=32 * 2**20),
+        cost_estimate=pl.CostEstimate(
+            flops=rows * depth * count * 768, bytes_accessed=rows * 3000, transcendentals=0
+        ),
+    )(ids, *blocks, *[in_weights] * (4 * count), *extra)
+
+
 def per_device(tokens, in_weights, short_taps, residues, decays, skip_gain):
     rows = tokens.shape[0]
     blocks = lax.axis_size("ctx")
+    ring = 8
+    lines = lax.axis_size("ch") // ring
     mine = lax.axis_index("ctx")
     weights = (residues * jnp.sqrt(2.0 * decays / MODES)).T
     rates = decays.T
-    projected = jnp.einsum(
-        "td,sdc->stc",
-        lax.all_gather(tokens, "ch", axis=1, tiled=True),
-        in_weights,
-        preferred_element_type=jnp.float32,
+
+    def beside(block, step):
+        return lax.ppermute(
+            block, "ch", [(z * ring + y, (z ^ step) * ring + y) for z in range(lines) for y in range(ring)]
+        )
+
+    def onward(block, cross):
+        route = []
+        for i in range(blocks):
+            to = i ^ 1 if cross else i
+            way = 1 if to % 2 == 0 else -1
+            for z in range(lines):
+                for y in range(ring):
+                    route.append(
+                        ((i * lines + z) * ring + y, (to * lines + z) * ring + (y + way) % ring)
+                    )
+        return lax.ppermute(block, ("ctx", "ch"), route)
+
+    def other_core(block):
+        return lax.ppermute(block, "ctx", [(i, i ^ 1) for i in range(blocks)])
+
+    before = lax.ppermute(tokens[rows - HALO :], "ctx", [(i, i + 1) for i in range(blocks - 1)])
+    own = jnp.concatenate([before, tokens], axis=0)
+    block = jnp.concatenate([own] + [beside(own, k) for k in range(1, lines)], axis=1)
+    table = np.zeros((2, lines, ring, ring, lines), np.int32)
+    for c, z, y, k in np.ndindex(2, lines, ring, lines):
+        way = 1 - 2 * c
+        places = [y] + [y + way * d for step in range(1, ring // 2) for d in (-step, step)] + [y + ring // 2]
+        table[c, z, y, :, k] = (z ^ k) * ring + np.array(places) % ring
+    ids = lax.dynamic_index_in_dim(
+        jnp.asarray(table.reshape(2, lines * ring, -1)[np.arange(blocks) % 2].reshape(-1, ring * lines)),
+        mine * lines * ring + lax.axis_index("ch"), 0, keepdims=False,
     )
-    previous = lax.ppermute(
-        projected[:, rows - HALO :, :], "ctx", [(i, i + 1) for i in range(blocks - 1)]
-    )
-    padded = jnp.concatenate([previous, projected], axis=1)
-    first, direct, starts, last = local_part(
-        padded, short_taps, weights, rates, skip_gain[None, :]
-    )
-    ahead = jnp.arange(blocks) - mine - 1
-    ahead = ahead[:, None, None]
+    straight, crossed = onward(block, False), onward(block, True)
+    sums, waiting, at = None, [block], 0
+    for step in range(1, ring // 2):
+        swapped = other_core(crossed)
+        here, last_crossed = straight, crossed
+        straight = onward(straight, False)
+        if step < ring // 2 - 1:
+            crossed = onward(crossed, False)
+        sums = project(sums, waiting, ids, at, in_weights)
+        at += len(waiting)
+        waiting = [here, swapped]
+        straight, sums = lax.optimization_barrier((straight, sums))
+    sums = project(sums, waiting, ids, at, in_weights)
+    sums = project(sums, [straight], ids, ring - 1, in_weights)
+    first, direct, starts, last = local_part(sums, short_taps, weights, rates, skip_gain[None, :])
+    ahead = (jnp.arange(blocks) - mine - 1)[:, None, None]
     worth = jnp.where(
         ahead >= 0, jnp.exp(-rates[None] * (rows * jnp.maximum(ahead, 0)).astype(jnp.float32)), 0.0
     )

time: 239 us -> 161 us (0.67)
  waiting for transfers between devices: 162 us -> 54.9 us
  starting transfers between devices: 26.9 us -> 56.5 us
  Pallas kernels: 5.07 us -> 19 us
  between operations: 13.5 us -> 0.32 us
  matrix products: 6.86 us -> 0 us
  blocking collectives: 18.8 us -> 23.9 us
    all_gather x1 -> x0, waiting for transfers between devices: 160 us -> none  [per_device(): lax.all_gather(tokens, 'ch', axis=1, tiled=True)]
    ppermute x1 -> x14, waiting for transfers between devices: 0.79 us -> 54.9 us  [the longest x7 39.6 us: onward(): return lax.ppermute(block, ('ctx', 'ch'), route)]
    ppermute x1 -> x14, starting transfers between devices: 26.9 us -> 56.5 us  [the longest x7 29.5 us: onward(): return lax.ppermute(block, ('ctx', 'ch'), route)]
    pallas_call x0 -> x5, Pallas kernels: none -> 13.8 us  [project(): pl.pallas_call(functools.partial(project_kernel, count), grid_spec=pltpu....]
    dot_general x1 -> x0, matrix products: 6.86 us -> none  [per_device(): jnp.einsum('td,sdc->stc', lax.all_gather(tokens, 'ch', axis=1, tiled=True...]
    all_to_all x1, blocking collectives: 18.8 us -> 23.9 us  [per_device(): lax.all_to_all(worth * last[None], 'ctx', split_axis=0, concat_axis=0, ti...]
  transfers between devices with their start and end apart: 2 -> 14, of which waited for: 2 -> 9; matrix products, arithmetic and copies ran while one was open for 1% -> 0% of each run, Pallas kernels for 0% -> 5%
where the time goes in v2:
time: 161 us; the launch traced here: 159 us
  starting transfers between devices  56.5 us (35%)
  waiting for transfers between devices  54.9 us (34%)
  blocking collectives  23.9 us (15%)
  Pallas kernels  19 us (12%)
  local copies, waits for them, and re-layouts  4.29 us (3%)
    ppermute x7, waiting for transfers between devices, onward(): return lax.ppermute(block, ('ctx', 'ch'), route)  39.6 us
    ppermute x7, starting transfers between devices, onward(): return lax.ppermute(block, ('ctx', 'ch'), route)  29.5 us
    all_to_all x1, blocking collectives, per_device(): lax.all_to_all(worth * last[None], 'ctx', split_axis=0, concat_axis=0, ti...  23.9 us
    ppermute x3, waiting for transfers between devices, beside(): lax.ppermute(block, 'ch', [(z * ring + y, (z ^ step) * ring + y) for z in...  14.5 us
    pallas_call x5, Pallas kernels, project(): pl.pallas_call(functools.partial(project_kernel, count), grid_spec=pltpu....  13.8 us
    ppermute x1, starting transfers between devices, per_device(): lax.ppermute(tokens[rows - HALO:], 'ctx', [(i, i + 1) for i in range(bloc...  12 us
    ppermute x3, starting transfers between devices, beside(): lax.ppermute(block, 'ch', [(z * ring + y, (z ^ step) * ring + y) for z in...  9.27 us
    ppermute x3, starting transfers between devices, other_core(): return lax.ppermute(block, 'ctx', [(i, i ^ 1) for i in range(blocks)])  5.75 us
  transfers between devices with their start and end apart: 14, of which 9 were waited for; matrix products, arithmetic and copies ran while one was open for 0% of the time, Pallas kernels for 5%

profile of v2, /device:TPU:1, one launch (start us, length us, event | category | flops | bytes accessed | tf_op | source)
XLA Modules:
  0.0 159.1 jit_solution(12305967687671559841)
XLA Ops:
  0.7 12.0 %collective-permute-start = (bf16[16,128]{1,0:T(8,128)(2,1)S(1)}, bf16[16,128]{1,0:T(8,128)(2,1)S(1)}, u32[]{:S(2)}, u32[]{:S(2)}) collective-permute-start(bf16[16,128]{1,0:T(8,128)(2,1)S(1)} %slice.3), channel_id=1, source_target_pairs={{0,32},{32,64},{64,96},{96,128},{128,160},{160,192},{192,224},{224... | collective-permute-start | bytes 12296 | tf_op jit(solution)/shard_map/ppermute | solution.py:220
  14.4 3.1 %collective-permute-start.1 = (bf16[1040,128]{1,0:T(8,128)(2,1)S(1)}, bf16[1040,128]{1,0:T(8,128)(2,1)S(1)}, u32[]{:S(2)}, u32[]{:S(2)}) collective-permute-start(bf16[1040,128]{1,0:T(8,128)(2,1)S(1)} %constant_dynamic-update-slice_fusion), channel_id=1, source_target_pairs={{0,8},{1,9},{2,10},{3,11},{4,12},{5,13},{6,14},{7,15},{8,0},{9,1},... | collective-permute-start | bytes 798728 | tf_op jit(solution)/shard_map/ppermute | solution.py:201
  17.5 4.0 %collective-permute-start.2 = (bf16[1040,128]{1,0:T(8,128)(2,1)S(1)}, bf16[1040,128]{1,0:T(8,128)(2,1)S(1)}, u32[]{:S(2)}, u32[]{:S(2)}) collective-permute-start(bf16[1040,128]{1,0:T(8,128)(2,1)S(1)} %constant_dynamic-update-slice_fusion), channel_id=1, source_target_pairs={{0,16},{1,17},{2,18},{3,19},{4,20},{5,21},{6,22},{7,23},{8,24},{9,... | collective-permute-start | bytes 798728 | tf_op jit(solution)/shard_map/ppermute | solution.py:201
  21.6 2.2 %collective-permute-start.3 = (bf16[1040,128]{1,0:T(8,128)(2,1)S(1)}, bf16[1040,128]{1,0:T(8,128)(2,1)S(1)}, u32[]{:S(2)}, u32[]{:S(2)}) collective-permute-start(bf16[1040,128]{1,0:T(8,128)(2,1)S(1)} %constant_dynamic-update-slice_fusion), channel_id=1, source_target_pairs={{0,24},{1,25},{2,26},{3,27},{4,28},{5,29},{6,30},{7,31},{8,16},{9,... | collective-permute-start | bytes 798728 | tf_op jit(solution)/shard_map/ppermute | solution.py:201
  24.4 13.9 %collective-permute-done.2 = bf16[1040,128]{1,0:T(8,128)(2,1)S(1)} collective-permute-done((bf16[1040,128]{1,0:T(8,128)(2,1)S(1)}, bf16[1040,128]{1,0:T(8,128)(2,1)S(1)}, u32[]{:S(2)}, u32[]{:S(2)}) %collective-permute-start.2) | collective-permute-done | bytes 266272 | tf_op jit(solution)/shard_map/ppermute | solution.py:201
  38.4 3.8 %collective-permute-start.4 = (bf16[1040,512]{1,0:T(8,128)(2,1)S(1)}, bf16[1040,512]{1,0:T(8,128)(2,1)S(1)}, u32[]{:S(2)}, u32[]{:S(2)}) collective-permute-start(bf16[1040,512]{1,0:T(8,128)(2,1)S(1)} %pad_maximum_fusion.refs_0_), channel_id=1, source_target_pairs={{0,1},{1,2},{2,3},{3,4},{4,5},{5,6},{6,7},{7,0},{8,9},{9,10},{10,1... | collective-permute-start | bytes 3194888 | tf_op jit(solution)/shard_map/ppermute | solution.py:215
  42.2 1.9 %collective-permute-start.7 = (bf16[1040,512]{1,0:T(8,128)(2,1)S(1)}, bf16[1040,512]{1,0:T(8,128)(2,1)}, u32[]{:S(2)}, u32[]{:S(2)}) collective-permute-start(bf16[1040,512]{1,0:T(8,128)(2,1)S(1)} %pad_maximum_fusion.refs_0_), channel_id=1, source_target_pairs={{0,39},{1,32},{2,33},{3,34},{4,35},{5,36},{6,37},{7,38},{8,47},{9,... | collective-permute-start | bytes 3194888 | tf_op jit(solution)/shard_map/ppermute | solution.py:215
  44.1 17.7 %collective-permute-done.4.refs_0_ = bf16[1040,512]{1,0:T(8,128)(2,1)S(1)} collective-permute-done((bf16[1040,512]{1,0:T(8,128)(2,1)S(1)}, bf16[1040,512]{1,0:T(8,128)(2,1)S(1)}, u32[]{:S(2)}, u32[]{:S(2)}) %collective-permute-start.4) | collective-permute-done | bytes 1064992 | tf_op jit(solution)/shard_map/ppermute | solution.py:215
  61.9 5.0 %collective-permute-start.5 = (bf16[1040,512]{1,0:T(8,128)(2,1)S(1)}, bf16[1040,512]{1,0:T(8,128)(2,1)S(1)}, u32[]{:S(2)}, u32[]{:S(2)}) collective-permute-start(bf16[1040,512]{1,0:T(8,128)(2,1)S(1)} %collective-permute-done.4.refs_0_), channel_id=1, source_target_pairs={{0,1},{1,2},{2,3},{3,4},{4,5},{5,6},{6,7},{7,0},{8,9},{9,10},{10,1... | collective-permute-start | bytes 3194888 | tf_op jit(solution)/shard_map/ppermute | solution.py:215
  66.9 3.7 %collective-permute-start.10 = (bf16[1040,512]{1,0:T(8,128)(2,1)}, bf16[1040,512]{1,0:T(8,128)(2,1)}, u32[]{:S(2)}, u32[]{:S(2)}) collective-permute-start(bf16[1040,512]{1,0:T(8,128)(2,1)} %collective-permute-done.7), channel_id=1, source_target_pairs={{0,1},{1,2},{2,3},{3,4},{4,5},{5,6},{6,7},{7,0},{8,9},{9,10},{10,1... | collective-permute-start | bytes 3194888 | tf_op jit(solution)/shard_map/ppermute | solution.py:215
  70.6 1.9 %collective-permute-start.8 = (bf16[1040,512]{1,0:T(8,128)(2,1)}, bf16[1040,512]{1,0:T(8,128)(2,1)S(1)}, u32[]{:S(2)}, u32[]{:S(2)}) collective-permute-start(bf16[1040,512]{1,0:T(8,128)(2,1)} %collective-permute-done.7), channel_id=1, source_target_pairs={{0,32},{32,0},{64,96},{96,64},{128,160},{160,128},{192,224},{224,1... | collective-permute-start | bytes 3194888 | tf_op jit(solution)/shard_map/ppermute | solution.py:218
  75.2 2.2 %shard_map.73.refs_10_ = f32[3,1040,128]{2,1,0:T(8,128)S(1)} custom-call(s32[32]{0:T(128)S(1)} %dynamic-slice_bitcast_fusion.ids, bf16[1040,512]{1,0:T(8,128)(2,1)S(1)} %pad_maximum_fusion.refs_0_, bf16[3,4096,128]{2,1,0:T(8,128)(2,1)S(1)} %copy-done, bf16[3,4096,128]{2,1,0:T(8,128)(2,1)S(1)} %copy-done, bf16[3,4096,128]{2,1,0:T(8,128)(2,1)S(1)} %copy-done, ...), custom_call_target="tpu_custom_call" | custom-call | flops 408944640 | bytes 3120000 | tf_op jit(solution)/shard_map/pallas_call | solution.py:172
  78.8 5.0 %collective-permute-start.6 = (bf16[1040,512]{1,0:T(8,128)(2,1)S(1)}, bf16[1040,512]{1,0:T(8,128)(2,1)S(1)}, u32[]{:S(2)}, u32[]{:S(2)}) collective-permute-start(bf16[1040,512]{1,0:T(8,128)(2,1)S(1)} %collective-permute-done.5.refs_0_), channel_id=1, source_target_pairs={{0,1},{1,2},{2,3},{3,4},{4,5},{5,6},{6,7},{7,0},{8,9},{9,10},{10,1... | collective-permute-start | bytes 3194888 | tf_op jit(solution)/shard_map/ppermute | solution.py:215
  83.8 6.5 %collective-permute-done.10 = bf16[1040,512]{1,0:T(8,128)(2,1)} collective-permute-done((bf16[1040,512]{1,0:T(8,128)(2,1)}, bf16[1040,512]{1,0:T(8,128)(2,1)}, u32[]{:S(2)}, u32[]{:S(2)}) %collective-permute-start.10) | collective-permute-done | bytes 1064992 | tf_op jit(solution)/shard_map/ppermute | solution.py:215
  90.3 5.0 %collective-permute-start.12 = (bf16[1040,512]{1,0:T(8,128)(2,1)}, bf16[1040,512]{1,0:T(8,128)(2,1)S(1)}, u32[]{:S(2)}, u32[]{:S(2)}) collective-permute-start(bf16[1040,512]{1,0:T(8,128)(2,1)} %collective-permute-done.10), channel_id=1, source_target_pairs={{0,1},{1,2},{2,3},{3,4},{4,5},{5,6},{6,7},{7,0},{8,9},{9,10},{10,1... | collective-permute-start | bytes 3194888 | tf_op jit(solution)/shard_map/ppermute | solution.py:215
  97.3 3.1 %shard_map.74.refs_10_ = f32[3,1040,128]{2,1,0:T(8,128)S(1)} custom-call(s32[32]{0:T(128)S(1)} %dynamic-slice_bitcast_fusion.ids, bf16[1040,512]{1,0:T(8,128)(2,1)S(1)} %collective-permute-done.4.refs_0_, bf16[1040,512]{1,0:T(8,128)(2,1)S(1)} %collective-permute-done.8.refs_1_, bf16[3,4096,128]{2,1,0:T(8,128)(2,1)S(1)} %copy-done.1, ...), custom_call_target="tpu_custom_call", output_to_operand_aliasing={{}: (11, {})} | custom-call | flops 817889280 | bytes 3120000 | tf_op jit(solution)/shard_map/pallas_call | solution.py:172
  101.6 5.0 %collective-permute-start.9 = (bf16[1040,512]{1,0:T(8,128)(2,1)S(1)}, bf16[1040,512]{1,0:T(8,128)(2,1)S(1)}, u32[]{:S(2)}, u32[]{:S(2)}) collective-permute-start(bf16[1040,512]{1,0:T(8,128)(2,1)S(1)} %collective-permute-done.6.refs_0_), channel_id=1, source_target_pairs={{0,1},{1,2},{2,3},{3,4},{4,5},{5,6},{6,7},{7,0},{8,9},{9,10},{10,1... | collective-permute-start | bytes 3194888 | tf_op jit(solution)/shard_map/ppermute | solution.py:215
  106.6 6.5 %collective-permute-done.12 = bf16[1040,512]{1,0:T(8,128)(2,1)S(1)} collective-permute-done((bf16[1040,512]{1,0:T(8,128)(2,1)}, bf16[1040,512]{1,0:T(8,128)(2,1)S(1)}, u32[]{:S(2)}, u32[]{:S(2)}) %collective-permute-start.12) | collective-permute-done | bytes 1064992 | tf_op jit(solution)/shard_map/ppermute | solution.py:215
  115.1 3.1 %shard_map.75.refs_10_ = f32[3,1040,128]{2,1,0:T(8,128)S(1)} custom-call(s32[32]{0:T(128)S(1)} %dynamic-slice_bitcast_fusion.ids, bf16[1040,512]{1,0:T(8,128)(2,1)S(1)} %collective-permute-done.5.refs_0_, bf16[1040,512]{1,0:T(8,128)(2,1)S(1)} %collective-permute-done.11.refs_1_, ...), custom_call_target="tpu_custom_call", output_to_operand_aliasing={{}: (11, {})} | custom-call | flops 817889280 | bytes 3120000 | tf_op jit(solution)/shard_map/pallas_call | solution.py:172
  118.2 6.2 %collective-permute-done.9.refs_0_ = bf16[1040,512]{1,0:T(8,128)(2,1)S(1)} collective-permute-done((bf16[1040,512]{1,0:T(8,128)(2,1)S(1)}, bf16[1040,512]{1,0:T(8,128)(2,1)S(1)}, u32[]{:S(2)}, u32[]{:S(2)}) %collective-permute-start.9) | collective-permute-done | bytes 1064992 | tf_op jit(solution)/shard_map/ppermute | solution.py:215
  124.4 3.1 %shard_map.76.refs_5_ = f32[3,1040,128]{2,1,0:T(8,128)S(1)} custom-call(s32[32]{0:T(128)S(1)} %dynamic-slice_bitcast_fusion.ids, bf16[1040,512]{1,0:T(8,128)(2,1)S(1)} %collective-permute-done.6.refs_0_, bf16[1040,512]{1,0:T(8,128)(2,1)S(1)} %collective-permute-done.13.refs_1_, bf16[3,4096,128]{2,1,0:T(8,128)(2,1)S(1)} %copy-done.1, ...), custom_call_target="tpu_custom_call", output_to_operand_aliasing={{}: (11, {})} | custom-call | flops 817889280 | bytes 3120000 | tf_op jit(solution)/shard_map/pallas_call | solution.py:172
  127.6 2.3 %shard_map.77.proj = f32[3,1040,128]{2,1,0:T(8,128)S(1)} custom-call(s32[32]{0:T(128)S(1)} %dynamic-slice_bitcast_fusion.ids, bf16[1040,512]{1,0:T(8,128)(2,1)S(1)} %collective-permute-done.9.refs_0_, bf16[3,4096,128]{2,1,0:T(8,128)(2,1)S(1)} %copy-done.1, bf16[3,4096,128]{2,1,0:T(8,128)(2,1)S(1)} %copy-done.1, ...), custom_call_target="tpu_custom_call", output_to_operand_aliasing={{}: (6, {})} | custom-call | flops 408944640 | bytes 3120000 | tf_op jit(solution)/shard_map/pallas_call | solution.py:172
  129.9 3.6 %shard_map.78 = (f32[1024,128]{1,0:T(8,128)S(1)}, f32[1024,128]{1,0:T(8,128)S(1)}, f32[8,16,128]{2,1,0:T(8,128)S(1)}, f32[16,128]{1,0:T(8,128)S(1)}) custom-call(f32[3,1040,128]{2,1,0:T(8,128)S(1)} %shard_map.77.proj, f32[3,7,128]{2,1,0:T(8,128)S(1)} %copy-done.3, f32[16,128]{1,0:T(8,128)S(1)} %multiply_bitcast_fusion.weights, f32[16,128]{1,0:T(8,128)S(1)} %bitcast.7, ...), custom_call_target="tpu_custom_call" | custom-call | flops 14417920 | bytes 2621440 | tf_op jit(solution)/shard_map/pallas_call | solution.py:68
  133.7 23.9 %all_to_all.5 = f32[16,16,128]{2,1,0:T(8,128)S(1)} all-to-all(f32[16,16,128]{2,1,0:T(8,128)S(1)} %select_multiply_fusion), channel_id=1, replica_groups=mesh['ctx'=16,'ch'=32] {'ctx'}, dimensions={0} | all-to-all | bytes 262144 | tf_op jit(solution)/shard_map/all_to_all | solution.py:251
  (35 shorter events, 14.0 us)
Async XLA Ops:
  0.7 12.8 %collective-permute-start = (bf16[16,128]{1,0:T(8,128)(2,1)S(1)}, bf16[16,128]{1,0:T(8,128)(2,1)S(1)}, u32[]{:S(2)}, u32[]{:S(2)}) collective-permute-start(bf16[16,128]{1,0:T(8,128)(2,1)S(1)} %slice.3), channel_id=1, source_target_pairs={{0,32},{32,64},{64,96},{96,128},{128,160},{160,192},{192,224},{224... | collective-permute-start | bytes 12296 | tf_op jit(solution)/shard_map/ppermute | solution.py:220
  14.4 10.0 %collective-permute-start.1 = (bf16[1040,128]{1,0:T(8,128)(2,1)S(1)}, bf16[1040,128]{1,0:T(8,128)(2,1)S(1)}, u32[]{:S(2)}, u32[]{:S(2)}) collective-permute-start(bf16[1040,128]{1,0:T(8,128)(2,1)S(1)} %constant_dynamic-update-slice_fusion), channel_id=1, source_target_pairs={{0,8},{1,9},{2,10},{3,11},{4,12},{5,13},{6,14},{7,15},{8,0},{9,1},... | collective-permute-start | bytes 798728 | tf_op jit(solution)/shard_map/ppermute | solution.py:201
  17.5 20.7 %collective-permute-start.2 = (bf16[1040,128]{1,0:T(8,128)(2,1)S(1)}, bf16[1040,128]{1,0:T(8,128)(2,1)S(1)}, u32[]{:S(2)}, u32[]{:S(2)}) collective-permute-start(bf16[1040,128]{1,0:T(8,128)(2,1)S(1)} %constant_dynamic-update-slice_fusion), channel_id=1, source_target_pairs={{0,16},{1,17},{2,18},{3,19},{4,20},{5,21},{6,22},{7,23},{8,24},{9,... | collective-permute-start | bytes 798728 | tf_op jit(solution)/shard_map/ppermute | solution.py:201
  21.6 16.7 %collective-permute-start.3 = (bf16[1040,128]{1,0:T(8,128)(2,1)S(1)}, bf16[1040,128]{1,0:T(8,128)(2,1)S(1)}, u32[]{:S(2)}, u32[]{:S(2)}) collective-permute-start(bf16[1040,128]{1,0:T(8,128)(2,1)S(1)} %constant_dynamic-update-slice_fusion), channel_id=1, source_target_pairs={{0,24},{1,25},{2,26},{3,27},{4,28},{5,29},{6,30},{7,31},{8,16},{9,... | collective-permute-start | bytes 798728 | tf_op jit(solution)/shard_map/ppermute | solution.py:201
  38.4 23.5 %collective-permute-start.4 = (bf16[1040,512]{1,0:T(8,128)(2,1)S(1)}, bf16[1040,512]{1,0:T(8,128)(2,1)S(1)}, u32[]{:S(2)}, u32[]{:S(2)}) collective-permute-start(bf16[1040,512]{1,0:T(8,128)(2,1)S(1)} %pad_maximum_fusion.refs_0_), channel_id=1, source_target_pairs={{0,1},{1,2},{2,3},{3,4},{4,5},{5,6},{6,7},{7,0},{8,9},{9,10},{10,1... | collective-permute-start | bytes 3194888 | tf_op jit(solution)/shard_map/ppermute | solution.py:215
  42.2 24.7 %collective-permute-start.7 = (bf16[1040,512]{1,0:T(8,128)(2,1)S(1)}, bf16[1040,512]{1,0:T(8,128)(2,1)}, u32[]{:S(2)}, u32[]{:S(2)}) collective-permute-start(bf16[1040,512]{1,0:T(8,128)(2,1)S(1)} %pad_maximum_fusion.refs_0_), channel_id=1, source_target_pairs={{0,39},{1,32},{2,33},{3,34},{4,35},{5,36},{6,37},{7,38},{8,47},{9,... | collective-permute-start | bytes 3194888 | tf_op jit(solution)/shard_map/ppermute | solution.py:215
  61.9 16.9 %collective-permute-start.5 = (bf16[1040,512]{1,0:T(8,128)(2,1)S(1)}, bf16[1040,512]{1,0:T(8,128)(2,1)S(1)}, u32[]{:S(2)}, u32[]{:S(2)}) collective-permute-start(bf16[1040,512]{1,0:T(8,128)(2,1)S(1)} %collective-permute-done.4.refs_0_), channel_id=1, source_target_pairs={{0,1},{1,2},{2,3},{3,4},{4,5},{5,6},{6,7},{7,0},{8,9},{9,10},{10,1... | collective-permute-start | bytes 3194888 | tf_op jit(solution)/shard_map/ppermute | solution.py:215
  66.9 23.4 %collective-permute-start.10 = (bf16[1040,512]{1,0:T(8,128)(2,1)}, bf16[1040,512]{1,0:T(8,128)(2,1)}, u32[]{:S(2)}, u32[]{:S(2)}) collective-permute-start(bf16[1040,512]{1,0:T(8,128)(2,1)} %collective-permute-done.7), channel_id=1, source_target_pairs={{0,1},{1,2},{2,3},{3,4},{4,5},{5,6},{6,7},{7,0},{8,9},{9,10},{10,1... | collective-permute-start | bytes 3194888 | tf_op jit(solution)/shard_map/ppermute | solution.py:215
  70.6 26.6 %collective-permute-start.8 = (bf16[1040,512]{1,0:T(8,128)(2,1)}, bf16[1040,512]{1,0:T(8,128)(2,1)S(1)}, u32[]{:S(2)}, u32[]{:S(2)}) collective-permute-start(bf16[1040,512]{1,0:T(8,128)(2,1)} %collective-permute-done.7), channel_id=1, source_target_pairs={{0,32},{32,0},{64,96},{96,64},{128,160},{160,128},{192,224},{224,1... | collective-permute-start | bytes 3194888 | tf_op jit(solution)/shard_map/ppermute | solution.py:218
  73.3 1.9 %copy-start = (bf16[3,4096,128]{2,1,0:T(8,128)(2,1)S(1)}, bf16[3,4096,128]{2,1,0:T(8,128)(2,1)}, u32[]{:S(2)}) copy-start(bf16[3,4096,128]{2,1,0:T(8,128)(2,1)} %refs_4_.9) | copy-start | bytes 9437188
  75.2 22.1 %copy-start.1 = (bf16[3,4096,128]{2,1,0:T(8,128)(2,1)S(1)}, bf16[3,4096,128]{2,1,0:T(8,128)(2,1)}, u32[]{:S(2)}) copy-start(bf16[3,4096,128]{2,1,0:T(8,128)(2,1)} %refs_4_.9) | copy-start | bytes 9437188
  77.3 37.8 %copy-start.2 = (f32[128,16]{0,1:T(8,128)S(1)}, f32[128,16]{0,1:T(8,128)}, u32[]{:S(2)}) copy-start(f32[128,16]{0,1:T(8,128)} %param.11) | copy-start | bytes 24580
  77.3 37.8 %copy-start.5 = (f32[128,16]{0,1:T(8,128)S(1)}, f32[128,16]{0,1:T(8,128)}, u32[]{:S(2)}) copy-start(f32[128,16]{0,1:T(8,128)} %param.10) | copy-start | bytes 24580
  78.8 22.8 %collective-permute-start.6 = (bf16[1040,512]{1,0:T(8,128)(2,1)S(1)}, bf16[1040,512]{1,0:T(8,128)(2,1)S(1)}, u32[]{:S(2)}, u32[]{:S(2)}) collective-permute-start(bf16[1040,512]{1,0:T(8,128)(2,1)S(1)} %collective-permute-done.5.refs_0_), channel_id=1, source_target_pairs={{0,1},{1,2},{2,3},{3,4},{4,5},{5,6},{6,7},{7,0},{8,9},{9,10},{10,1... | collective-permute-start | bytes 3194888 | tf_op jit(solution)/shard_map/ppermute | solution.py:215
  90.3 22.8 %collective-permute-start.12 = (bf16[1040,512]{1,0:T(8,128)(2,1)}, bf16[1040,512]{1,0:T(8,128)(2,1)S(1)}, u32[]{:S(2)}, u32[]{:S(2)}) collective-permute-start(bf16[1040,512]{1,0:T(8,128)(2,1)} %collective-permute-done.10), channel_id=1, source_target_pairs={{0,1},{1,2},{2,3},{3,4},{4,5},{5,6},{6,7},{7,0},{8,9},{9,10},{10,1... | collective-permute-start | bytes 3194888 | tf_op jit(solution)/shard_map/ppermute | solution.py:215
  95.3 19.8 %collective-permute-start.11 = (bf16[1040,512]{1,0:T(8,128)(2,1)}, bf16[1040,512]{1,0:T(8,128)(2,1)S(1)}, u32[]{:S(2)}, u32[]{:S(2)}) collective-permute-start(bf16[1040,512]{1,0:T(8,128)(2,1)} %collective-permute-done.10), channel_id=1, source_target_pairs={{0,32},{32,0},{64,96},{96,64},{128,160},{160,128},{192,224},{224,1... | collective-permute-start | bytes 3194888 | tf_op jit(solution)/shard_map/ppermute | solution.py:218
  101.6 22.8 %collective-permute-start.9 = (bf16[1040,512]{1,0:T(8,128)(2,1)S(1)}, bf16[1040,512]{1,0:T(8,128)(2,1)S(1)}, u32[]{:S(2)}, u32[]{:S(2)}) collective-permute-start(bf16[1040,512]{1,0:T(8,128)(2,1)S(1)} %collective-permute-done.6.refs_0_), channel_id=1, source_target_pairs={{0,1},{1,2},{2,3},{3,4},{4,5},{5,6},{6,7},{7,0},{8,9},{9,10},{10,1... | collective-permute-start | bytes 3194888 | tf_op jit(solution)/shard_map/ppermute | solution.py:215
  113.1 11.3 %collective-permute-start.13 = (bf16[1040,512]{1,0:T(8,128)(2,1)S(1)}, bf16[1040,512]{1,0:T(8,128)(2,1)S(1)}, u32[]{:S(2)}, u32[]{:S(2)}) collective-permute-start(bf16[1040,512]{1,0:T(8,128)(2,1)S(1)} %collective-permute-done.12), channel_id=1, source_target_pairs={{0,32},{32,0},{64,96},{96,64},{128,160},{160,128},{192,224},{224,1... | collective-permute-start | bytes 3194888 | tf_op jit(solution)/shard_map/ppermute | solution.py:218
  127.5 2.4 %copy-start.3 = (f32[3,7,128]{2,1,0:T(8,128)S(1)}, f32[3,7,128]{2,1,0:T(8,128)}, u32[]{:S(2)}) copy-start(f32[3,7,128]{2,1,0:T(8,128)} %taps.1) | copy-start | bytes 32260
  127.6 2.4 %copy-start.4 = (f32[128]{0:T(128)S(1)}, f32[128]{0:T(128)}, u32[]{:S(2)}) copy-start(f32[128]{0:T(128)} %param.12) | copy-start | bytes 1540

commit v3 on v2

v3 whole, which is shorter than its diff:
```python
import functools

import jax
import jax.numpy as jnp
import numpy as np
from jax import lax
from jax.experimental import pallas as pl
from jax.experimental.pallas import tpu as pltpu
from jax.sharding import PartitionSpec as P

MODES = 16
TAPS = 7
HALO = 16
CHUNKS = 8
UNROLL = 8
LANES = 128


def wide(row):
    return jnp.broadcast_to(row, (CHUNKS, LANES))


def local_kernel(length, proj, taps, weights, decays, skip, pack, ends):
    rows = length * CHUNKS
    poles = [wide(jnp.exp(-decays[m : m + 1, :])) for m in range(MODES)]
    gains = [wide(weights[m : m + 1, :]) for m in range(MODES)]
    skip_row = wide(skip[0:1, :])

    def steps(at, states):
        states = list(states)
        at = at * UNROLL
        taken = [
            [
                proj[s, pl.ds(at + HALO - (TAPS - 1) + k, CHUNKS, stride=length), :]
                for k in range(UNROLL + TAPS - 1)
            ]
            for s in range(3)
        ]
        coef = [[wide(taps[s, j : j + 1, :]) for j in range(TAPS)] for s in range(3)]
        for u in range(UNROLL):
            filtered = [sum(coef[s][j] * taken[s][u + j] for j in range(TAPS)) for s in range(3)]
            gated = filtered[1] * filtered[2]
            total = skip_row * gated
            for m in range(MODES):
                states[m] = poles[m] * states[m] + gated
                total = total + gains[m] * states[m]
            here = pl.multiple_of((at + u) * CHUNKS, CHUNKS)
            pack[pl.ds(here, CHUNKS), :] = filtered[0]
            pack[pl.ds(rows + here, CHUNKS), :] = filtered[0] * total
        return tuple(states)

    zero = jnp.zeros((CHUNKS, LANES), jnp.float32)
    states = lax.fori_loop(0, length // UNROLL, steps, (zero,) * MODES)
    for m in range(MODES):
        ends[m * CHUNKS : (m + 1) * CHUNKS, :] = states[m]
    over = jnp.exp(-decays[...] * float(length))
    carry = jnp.zeros((MODES, LANES), jnp.float32)
    for c in range(CHUNKS):
        pack[2 * rows + c * MODES : 2 * rows + (c + 1) * MODES, :] = carry
        carry = over * carry + ends[pl.ds(c, MODES, stride=CHUNKS), :]
    pack[2 * rows + CHUNKS * MODES : 2 * rows + (CHUNKS + 1) * MODES, :] = carry


def local_part(proj, taps, weights, decays, skip):
    rows = proj.shape[1] - HALO
    return pl.pallas_call(
        functools.partial(local_kernel, rows // CHUNKS),
        out_shape=jax.ShapeDtypeStruct((2 * rows + (CHUNKS + 1) * MODES, LANES), jnp.float32),
        scratch_shapes=[pltpu.VMEM((MODES * CHUNKS, LANES), jnp.float32)],
        compiler_params=pltpu.CompilerParams(vmem_limit_bytes=32 * 2**20),
        cost_estimate=pl.CostEstimate(
            flops=rows * LANES * 110, bytes_accessed=rows * LANES * 20, transcendentals=0
        ),
    )(proj, taps, weights, decays, skip)


def final_kernel(rows, half, carried, mine, other, weights, decays, out, begins):
    length = rows // CHUNKS
    low = half[0] == 0
    end = slice(2 * rows + CHUNKS * MODES, 2 * rows + (CHUNKS + 1) * MODES)
    poles = [wide(jnp.exp(-decays[m : m + 1, :])) for m in range(MODES)]
    over = jnp.exp(-decays[...] * float(length))
    beyond = jnp.exp(-decays[...] * float(rows))
    early = carried[...]
    late = beyond * early + jnp.where(low, mine[end, :], other[end, :])
    for pack, begin, offset in (
        (mine, jnp.where(low, early, late), half[0] * rows),
        (other, jnp.where(low, late, early), (1 - half[0]) * rows),
    ):
        reach = jnp.ones_like(over)
        for c in range(CHUNKS):
            start = pack[2 * rows + c * MODES : 2 * rows + (c + 1) * MODES, :]
            begins[pl.ds(c, MODES, stride=CHUNKS), :] = weights[...] * (start + reach * begin)
            reach = reach * over

        def steps(at, terms, pack=pack, offset=offset):
            terms = list(terms)
            at = at * UNROLL
            for u in range(UNROLL):
                terms = [poles[m] * terms[m] for m in range(MODES)]
                sums = terms
                while len(sums) > 1:
                    sums = [sums[i] + sums[i + 1] for i in range(0, len(sums), 2)]
                here = pl.multiple_of((at + u) * CHUNKS, CHUNKS)
                out[pl.ds(offset + at + u, CHUNKS, stride=length), :] = (
                    pack[pl.ds(rows + here, CHUNKS), :] + pack[pl.ds(here, CHUNKS), :] * sums[0]
                )
            return tuple(terms)

        terms = tuple(begins[m * CHUNKS : (m + 1) * CHUNKS, :] for m in range(MODES))
        lax.fori_loop(0, length // UNROLL, steps, terms)


def final_part(half, carried, mine, other, weights, decays):
    rows = (mine.shape[0] - (CHUNKS + 1) * MODES) // 2
    vmem = pl.BlockSpec(memory_space=pltpu.VMEM)
    return pl.pallas_call(
        functools.partial(final_kernel, rows),
        in_specs=[pl.BlockSpec(memory_space=pltpu.SMEM)] + [vmem] * 5,
        out_specs=vmem,
        out_shape=jax.ShapeDtypeStruct((2 * rows, LANES), jnp.float32),
        scratch_shapes=[pltpu.VMEM((MODES * CHUNKS, LANES), jnp.float32)],
        compiler_params=pltpu.CompilerParams(vmem_limit_bytes=32 * 2**20),
        cost_estimate=pl.CostEstimate(
            flops=rows * LANES * 72, bytes_accessed=rows * LANES * 24, transcendentals=0
        ),
    )(half, carried, mine, other, weights, decays)


def project_kernel(count, ids, *refs):
    blocks, weights = refs[:count], refs[count : 5 * count]
    sums, out = refs[5 * count : -1], refs[-1]
    total = None
    for b in range(count):
        wide_weights = jnp.concatenate(
            [
                jnp.concatenate([weights[4 * b + z][s] for s in range(3)], axis=1)
                for z in range(4)
            ],
            axis=0,
        )
        part = jnp.dot(blocks[b][...], wide_weights, preferred_element_type=jnp.float32)
        total = part if total is None else total + part
    for s in range(3):
        here = total[:, s * LANES : (s + 1) * LANES]
        out[s] = here + sums[0][s] if sums else here


def project(sums, blocks, ids, at, in_weights):
    rows, depth = blocks[0].shape
    count = len(blocks)
    tile = rows
    piece = lambda k: pl.BlockSpec((3, LANES, LANES), lambda i, ids: (0, ids[4 * at + k], 0))
    total = pl.BlockSpec((3, tile, LANES), lambda i, ids: (0, i, 0))
    extra = [] if sums is None else [sums]
    return pl.pallas_call(
        functools.partial(project_kernel, count),
        grid_spec=pltpu.PrefetchScalarGridSpec(
            num_scalar_prefetch=1,
            grid=(rows // tile,),
            in_specs=[pl.BlockSpec((tile, depth), lambda i, ids: (i, 0))] * count
            + [piece(k) for k in range(4 * count)]
            + [total] * len(extra),
            out_specs=total,
        ),
        out_shape=jax.ShapeDtypeStruct((3, rows, LANES), jnp.float32),
        input_output_aliases={1 + 5 * count: 0} if extra else {},
        compiler_params=pltpu.CompilerParams(vmem_limit_bytes=32 * 2**20),
        cost_estimate=pl.CostEstimate(
            flops=rows, bytes_accessed=rows, transcendentals=0
        ),
    )(ids, *blocks, *[in_weights] * (4 * count), *extra)


def per_device(tokens, in_weights, short_taps, residues, decays, skip_gain):
    rows = tokens.shape[0]
    part = rows // 2
    blocks = lax.axis_size("ctx")
    ring = 8
    lines = lax.axis_size("ch") // ring
    mine = lax.axis_index("ctx")
    place = mine * lines * ring + lax.axis_index("ch")
    half = lax.axis_index("ch") // ring % 2
    weights = (residues * jnp.sqrt(2.0 * decays / MODES)).T
    rates = decays.T

    def beside(block, step):
        return lax.ppermute(
            block, "ch", [(z * ring + y, (z ^ step) * ring + y) for z in range(lines) for y in range(ring)]
        )

    def onward(block):
        route = []
        for i in range(blocks):
            for z in range(lines):
                for y in range(ring):
                    at = (i * lines + z) * ring
                    route.append((at + y, at + (y + 1 - i % 2 * 2) % ring))
        return lax.ppermute(block, ("ctx", "ch"), route)

    def other_core(block):
        return lax.ppermute(block, "ctx", [(i, i ^ 1) for i in range(blocks)])

    table = np.zeros((2, 2, lines, ring, ring, lines), np.int32)
    for c, z, y, k in np.ndindex(2, lines, ring, lines):
        way = 1 - 2 * c
        places = [y] + [y + way * d for step in range(1, ring // 2) for d in (-step, step)] + [y + ring // 2]
        ids = (z ^ k) * ring + np.array(places) % ring
        count = lines * ring // 2
        table[c, 0, z, y, :, k] = ids
        table[c, 1, z, y, :, k] = ids % count + count * (ids // count != c)
    table = table.transpose(0, 2, 3, 1, 4, 5).reshape(2, lines * ring, -1)[np.arange(blocks) % 2]
    ids = lax.dynamic_index_in_dim(
        jnp.asarray(table.reshape(-1, 2 * lines * ring)), place, 0, keepdims=False
    )

    before = lax.ppermute(tokens[rows - HALO :], "ctx", [(i, i + 1) for i in range(blocks - 1)])
    padded = jnp.concatenate([before, tokens], axis=0)
    kept = lax.dynamic_slice_in_dim(padded, half * part, part + HALO, 0)
    given = lax.dynamic_slice_in_dim(padded, (1 - half) * part, part + HALO, 0)
    block = jnp.concatenate([kept, beside(given, 1), beside(kept, 2), beside(given, 3)], axis=1)
    count = in_weights.shape[1] // 2
    half_weights = lax.dynamic_slice_in_dim(in_weights, mine % 2 * count, count, 1)
    half_weights, block = lax.optimization_barrier((half_weights, block))
    straight = onward(block)
    crossed = onward(other_core(block))
    half_weights = beside(half_weights, 1)

    sums, waiting, at = None, [block], 0
    arrived = [block]
    for step in range(1, ring // 2):
        swapped = other_core(crossed)
        if step == ring // 2 - 1:
            half_weights, straight = lax.optimization_barrier((half_weights, straight))
        here = straight
        straight = onward(straight)
        if step < ring // 2 - 1:
            crossed = onward(crossed)
        sums = project(sums, waiting, ids, at, in_weights)
        at += len(waiting)
        waiting = [here, swapped]
        arrived += waiting
        straight, sums = lax.optimization_barrier((straight, sums))
    their_weights = jnp.concatenate([half_weights, other_core(half_weights)], axis=1)
    sums = project(sums, waiting, ids, at, in_weights)
    theirs = project(None, arrived[:3], ids, ring, their_weights)
    theirs = project(theirs, arrived[3:], ids, ring + 3, their_weights)
    straight, sums, theirs = lax.optimization_barrier((straight, sums, theirs))
    theirs = project(theirs, [straight], ids, 2 * ring - 1, their_weights)
    sums = project(sums, [straight], ids, ring - 1, in_weights)

    own_values = (short_taps, weights, rates, skip_gain[None, :])
    packed = jnp.concatenate([short_taps.reshape(3 * TAPS, -1), weights, rates, skip_gain[None, :]], axis=0)
    packed = beside(packed, 1)
    their_values = (
        packed[: 3 * TAPS].reshape(3, TAPS, -1),
        packed[3 * TAPS : 3 * TAPS + MODES],
        packed[3 * TAPS + MODES : 3 * TAPS + 2 * MODES],
        packed[3 * TAPS + 2 * MODES :],
    )
    their_pack = local_part(theirs, *their_values)
    other = beside(their_pack, 1)
    pack = local_part(sums, *own_values)

    ahead = (jnp.arange(blocks) - mine - 1)[:, None, None]

    def worth(rate, state):
        distance = (rows * jnp.maximum(ahead, 0) + (1 - half) * part).astype(jnp.float32)
        return jnp.where(ahead >= 0, jnp.exp(-rate[None] * distance), 0.0) * state[None]

    to_own = worth(rates, pack[-MODES:])
    to_their = worth(their_values[2], their_pack[-MODES:])
    states = jnp.where(half == 0, jnp.stack([to_own, to_their], 1), jnp.stack([to_their, to_own], 1))
    groups = [
        [(i * lines + z + q) * ring + y for i in range(blocks) for q in range(2)]
        for z in range(0, lines, 2)
        for y in range(ring)
    ]
    states = lax.all_to_all(
        states.reshape(2 * blocks, MODES, LANES), ("ctx", "ch"), 0, 0, axis_index_groups=groups, tiled=True
    )
    return final_part(
        jnp.full((1,), half, jnp.int32), jnp.sum(states, axis=0), pack, other, weights, rates
    )


def solution(mesh):
    return jax.shard_map(
        per_device,
        mesh=mesh,
        in_specs=(
            P("ctx", "ch"),
            P(None, None, "ch"),
            P(None, None, "ch"),
            P("ch", None),
            P("ch", None),
            P("ch"),
        ),
        out_specs=P("ctx", "ch"),
        check_vma=False,
    )
```

time: 161 us -> 146 us (0.907)
  waiting for transfers between devices: 54.9 us -> 18.4 us
  starting transfers between devices: 56.5 us -> 65 us
  local copies, waits for them, and re-layouts: 4.29 us -> 11.9 us
  Pallas kernels: 19 us -> 25.5 us
    ppermute x7, waiting for transfers between devices: 39.6 us -> 4.96 us  [onward(): return lax.ppermute(block, ('ctx', 'ch'), route)]
    ppermute x3 -> x5, starting transfers between devices: 5.75 us -> 12 us  [other_core(): return lax.ppermute(block, 'ctx', [(i, i ^ 1) for i in range(blocks)])]
    ppermute x3 -> x6, starting transfers between devices: 9.27 us -> 15 us  [beside(): lax.ppermute(block, 'ch', [(z * ring + y, (z ^ step) * ring + y) for z in...]
    pallas_call x5 -> x8, Pallas kernels: 13.8 us -> 18.5 us  [project(): pl.pallas_call(functools.partial(project_kernel, count), grid_spec=pltpu....]
    ppermute x7, starting transfers between devices: 29.5 us -> 26 us  [onward(): return lax.ppermute(block, ('ctx', 'ch'), route)]
    dynamic_slice x0 -> x2, local copies, waits for them, and re-layouts: none -> 2.7 us  [the longest x1 2.67 us: per_device(): lax.dynamic_slice_in_dim(in_weights, mine % 2 * count, count, 1)]
    unnamed x13 -> x26, local copies, waits for them, and re-layouts: 1.92 us -> 4.39 us
    pallas_call x2 -> x3, Pallas kernels: 5.17 us -> 7.03 us  [the longest x2 4.39 us: local_part(): pl.pallas_call(functools.partial(local_kernel, rows // CHUNKS), out_shape...]
  transfers between devices with their start and end apart: 14 -> 19, of which waited for: 9 -> 6; matrix products, arithmetic and copies ran while one was open for 0% -> 5% of each run, Pallas kernels for 5% -> 8%
where the time goes in v3:
time: 146 us; the launch traced here: 145 us
  starting transfers between devices  65 us (45%)
  Pallas kernels  25.5 us (17%)
  blocking collectives  23.5 us (16%)
  waiting for transfers between devices  18.4 us (13%)
  local copies, waits for them, and re-layouts  11.9 us (8%)
    ppermute x7, starting transfers between devices, onward(): return lax.ppermute(block, ('ctx', 'ch'), route)  26 us
    all_to_all x1, blocking collectives, per_device(): lax.all_to_all(states.reshape(2 * blocks, MODES, LANES), ('ctx', 'ch'), 0...  23.5 us
    pallas_call x8, Pallas kernels, project(): pl.pallas_call(functools.partial(project_kernel, count), grid_spec=pltpu....  18.5 us
    ppermute x6, starting transfers between devices, beside(): lax.ppermute(block, 'ch', [(z * ring + y, (z ^ step) * ring + y) for z in...  15 us
    ppermute x6, waiting for transfers between devices, beside(): lax.ppermute(block, 'ch', [(z * ring + y, (z ^ step) * ring + y) for z in...  12.8 us
    ppermute x1, starting transfers between devices, per_device(): lax.ppermute(tokens[rows - HALO:], 'ctx', [(i, i + 1) for i in range(bloc...  12 us
    ppermute x5, starting transfers between devices, other_core(): return lax.ppermute(block, 'ctx', [(i, i ^ 1) for i in range(blocks)])  12 us
    ppermute x7, waiting for transfers between devices, onward(): return lax.ppermute(block, ('ctx', 'ch'), route)  4.96 us
  transfers between devices with their start and end apart: 19, of which 6 were waited for; matrix products, arithmetic and copies ran while one was open for 5% of the time, Pallas kernels for 8%

profile of v3, /device:TPU:1, one launch (start us, length us, event | category | flops | bytes accessed | tf_op | source)
XLA Modules:
  0.0 145.2 jit_solution(16933221321588427885)
XLA Ops:
  0.7 12.0 %collective-permute-start = (bf16[16,128]{1,0:T(8,128)(2,1)S(1)}, bf16[16,128]{1,0:T(8,128)(2,1)S(1)}, u32[]{:S(2)}, u32[]{:S(2)}) collective-permute-start(bf16[16,128]{1,0:T(8,128)(2,1)S(1)} %slice.21), channel_id=1, source_target_pairs={{0,32},{32,64},{64,96},{96,128},{128,160},{160,192},{192,224},{224... | collective-permute-start | bytes 12296 | tf_op jit(solution)/shard_map/ppermute | solution.py:217
  14.5 3.1 %collective-permute-start.1 = (bf16[528,128]{1,0:T(8,128)(2,1)S(1)}, bf16[528,128]{1,0:T(8,128)(2,1)S(1)}, u32[]{:S(2)}, u32[]{:S(2)}) collective-permute-start(bf16[528,128]{1,0:T(8,128)(2,1)S(1)} %get-tuple-element.32), channel_id=1, source_target_pairs={{0,8},{1,9},{2,10},{3,11},{4,12},{5,13},{6,14},{7,15},{8,0},{9,1},... | collective-permute-start | bytes 405512 | tf_op jit(solution)/shard_map/ppermute | solution.py:188
  17.6 4.0 %collective-permute-start.3 = (bf16[528,128]{1,0:T(8,128)(2,1)S(1)}, bf16[528,128]{1,0:T(8,128)(2,1)S(1)}, u32[]{:S(2)}, u32[]{:S(2)}) collective-permute-start(bf16[528,128]{1,0:T(8,128)(2,1)S(1)} %get-tuple-element.32), channel_id=1, source_target_pairs={{0,24},{1,25},{2,26},{3,27},{4,28},{5,29},{6,30},{7,31},{8,16},{9,... | collective-permute-start | bytes 405512 | tf_op jit(solution)/shard_map/ppermute | solution.py:188
  21.6 2.2 %collective-permute-start.2 = (bf16[528,128]{1,0:T(8,128)(2,1)S(1)}, bf16[528,128]{1,0:T(8,128)(2,1)S(1)}, u32[]{:S(2)}, u32[]{:S(2)}) collective-permute-start(bf16[528,128]{1,0:T(8,128)(2,1)S(1)} %get-tuple-element.31), channel_id=1, source_target_pairs={{0,16},{1,17},{2,18},{3,19},{4,20},{5,21},{6,22},{7,23},{8,24},{9,... | collective-permute-start | bytes 405512 | tf_op jit(solution)/shard_map/ppermute | solution.py:188
  23.8 2.7 %constant_dynamic-slice_fusion.2 = bf16[3,2048,128]{2,1,0:T(8,128)(2,1)} fusion(bf16[3,4096,128]{2,1,0:T(8,128)(2,1)} %refs_4_.9, s32[]{:T(128)S(6)} %select_n.67), kind=kLoop, calls=%fused_computation.12 | loop fusion | bytes 3145732 | tf_op jit(solution)/shard_map/dynamic_slice | solution.py:223
  26.5 3.9 %collective-permute-done.2 = bf16[528,128]{1,0:T(8,128)(2,1)S(1)} collective-permute-done((bf16[528,128]{1,0:T(8,128)(2,1)S(1)}, bf16[528,128]{1,0:T(8,128)(2,1)S(1)}, u32[]{:S(2)}, u32[]{:S(2)}) %collective-permute-start.2) | collective-permute-done | bytes 135200 | tf_op jit(solution)/shard_map/ppermute | solution.py:188
  32.4 4.9 %collective-permute-start.5 = (bf16[528,512]{1,0:T(8,128)(2,1)S(1)}, bf16[528,512]{1,0:T(8,128)(2,1)}, u32[]{:S(2)}, u32[]{:S(2)}) collective-permute-start(bf16[528,512]{1,0:T(8,128)(2,1)S(1)} %pad_maximum_fusion.refs_0_), channel_id=1, source_target_pairs={{0,1},{1,2},{2,3},{3,4},{4,5},{5,6},{6,7},{7,0},{8,9},{9,10},{10,1... | collective-permute-start | bytes 1622024 | tf_op jit(solution)/shard_map/ppermute | solution.py:199
  40.1 3.0 %collective-permute-start.9 = (bf16[528,512]{1,0:T(8,128)(2,1)}, bf16[528,512]{1,0:T(8,128)(2,1)}, u32[]{:S(2)}, u32[]{:S(2)}) collective-permute-start(bf16[528,512]{1,0:T(8,128)(2,1)} %collective-permute-done.8), channel_id=1, source_target_pairs={{0,1},{1,2},{2,3},{3,4},{4,5},{5,6},{6,7},{7,0},{8,9},{9,10},{10,1... | collective-permute-start | bytes 1622024 | tf_op jit(solution)/shard_map/ppermute | solution.py:199
  43.6 5.1 %collective-permute-start.6 = (bf16[528,512]{1,0:T(8,128)(2,1)}, bf16[528,512]{1,0:T(8,128)(2,1)}, u32[]{:S(2)}, u32[]{:S(2)}) collective-permute-start(bf16[528,512]{1,0:T(8,128)(2,1)} %collective-permute-done.5.refs_0_.refs_1_), channel_id=1, source_target_pairs={{0,1},{1,2},{2,3},{3,4},{4,5},{5,6},{6,7},{7,0},{8,9},{9,10},{10,1... | collective-permute-start | bytes 1622024 | tf_op jit(solution)/shard_map/ppermute | solution.py:199
  53.6 2.9 %collective-permute-done.6.refs_0_ = bf16[528,512]{1,0:T(8,128)(2,1)} collective-permute-done((bf16[528,512]{1,0:T(8,128)(2,1)}, bf16[528,512]{1,0:T(8,128)(2,1)}, u32[]{:S(2)}, u32[]{:S(2)}) %collective-permute-start.6) | collective-permute-done | bytes 540704 | tf_op jit(solution)/shard_map/ppermute | solution.py:199
  56.6 3.9 %collective-permute-start.7 = (bf16[528,512]{1,0:T(8,128)(2,1)}, bf16[528,512]{1,0:T(8,128)(2,1)}, u32[]{:S(2)}, u32[]{:S(2)}) collective-permute-start(bf16[528,512]{1,0:T(8,128)(2,1)} %collective-permute-done.6.refs_0_), channel_id=1, source_target_pairs={{0,1},{1,2},{2,3},{3,4},{4,5},{5,6},{6,7},{7,0},{8,9},{9,10},{10,1... | collective-permute-start | bytes 1622024 | tf_op jit(solution)/shard_map/ppermute | solution.py:199
  60.5 2.1 %collective-permute-start.12 = (bf16[528,512]{1,0:T(8,128)(2,1)}, bf16[528,512]{1,0:T(8,128)(2,1)}, u32[]{:S(2)}, u32[]{:S(2)}) collective-permute-start(bf16[528,512]{1,0:T(8,128)(2,1)} %collective-permute-done.9), channel_id=1, source_target_pairs={{0,1},{1,2},{2,3},{3,4},{4,5},{5,6},{6,7},{7,0},{8,9},{9,10},{10,1... | collective-permute-start | bytes 1622024 | tf_op jit(solution)/shard_map/ppermute | solution.py:199
  62.6 2.3 %shard_map.74.refs_10_ = f32[3,528,128]{2,1,0:T(8,128)S(1)} custom-call(s32[64]{0:T(128)S(1)} %fusion.ids, bf16[528,512]{1,0:T(8,128)(2,1)} %collective-permute-done.5.refs_0_.refs_1_, bf16[528,512]{1,0:T(8,128)(2,1)S(1)} %collective-permute-done.10.refs_1_.refs_2_, bf16[3,4096,128]{2,1,0:T(8,128)(2,1)S(1)} %copy-done, ...), custom_call_target="tpu_custom_call", output_to_operand_aliasing={{}: (11, {})} | custom-call | flops 528 | bytes 528 | tf_op jit(solution)/shard_map/pallas_call | solution.py:156
  67.3 8.8 %collective-permute-done.4 = bf16[3,2048,128]{2,1,0:T(8,128)(2,1)} collective-permute-done((bf16[3,2048,128]{2,1,0:T(8,128)(2,1)}, bf16[3,2048,128]{2,1,0:T(8,128)(2,1)}, u32[]{:S(2)}, u32[]{:S(2)}) %collective-permute-start.4) | collective-permute-done | bytes 1572896 | tf_op jit(solution)/shard_map/ppermute | solution.py:188
  78.1 3.8 %collective-permute-start.14 = (bf16[528,512]{1,0:T(8,128)(2,1)}, bf16[528,512]{1,0:T(8,128)(2,1)}, u32[]{:S(2)}, u32[]{:S(2)}) collective-permute-start(bf16[528,512]{1,0:T(8,128)(2,1)} %collective-permute-done.12), channel_id=1, source_target_pairs={{0,1},{1,2},{2,3},{3,4},{4,5},{5,6},{6,7},{7,0},{8,9},{9,10},{10,1... | collective-permute-start | bytes 1622024 | tf_op jit(solution)/shard_map/ppermute | solution.py:199
  83.9 3.2 %collective-permute-start.11 = (bf16[528,512]{1,0:T(8,128)(2,1)}, bf16[528,512]{1,0:T(8,128)(2,1)}, u32[]{:S(2)}, u32[]{:S(2)}) collective-permute-start(bf16[528,512]{1,0:T(8,128)(2,1)} %collective-permute-done.7.refs_0_.refs_2_), channel_id=1, source_target_pairs={{0,1},{1,2},{2,3},{3,4},{4,5},{5,6},{6,7},{7,0},{8,9},{9,10},{10,1... | collective-permute-start | bytes 1622024 | tf_op jit(solution)/shard_map/ppermute | solution.py:199
  89.1 4.2 %collective-permute-start.15 = (bf16[528,512]{1,0:T(8,128)(2,1)}, bf16[528,512]{1,0:T(8,128)(2,1)}, u32[]{:S(2)}, u32[]{:S(2)}) collective-permute-start(bf16[528,512]{1,0:T(8,128)(2,1)} %collective-permute-done.14), channel_id=1, source_target_pairs={{0,32},{32,0},{64,96},{96,64},{128,160},{160,128},{192,224},{224,1... | collective-permute-start | bytes 1622024 | tf_op jit(solution)/shard_map/ppermute | solution.py:202
  95.0 2.5 %shard_map.75.refs_10_ = f32[3,528,128]{2,1,0:T(8,128)S(1)} custom-call(s32[64]{0:T(128)S(1)} %fusion.ids, bf16[528,512]{1,0:T(8,128)(2,1)} %collective-permute-done.6.refs_0_, bf16[528,512]{1,0:T(8,128)(2,1)} %collective-permute-done.13.refs_1_, bf16[3,4096,128]{2,1,0:T(8,128)(2,1)S(1)} %copy-done, ...), custom_call_target="tpu_custom_call", output_to_operand_aliasing={{}: (11, {})} | custom-call | flops 528 | bytes 528 | tf_op jit(solution)/shard_map/pallas_call | solution.py:156
  99.2 2.6 %shard_map.77.refs_20_ = f32[3,528,128]{2,1,0:T(8,128)S(1)} custom-call(s32[64]{0:T(128)S(1)} %fusion.ids, bf16[528,512]{1,0:T(8,128)(2,1)S(1)} %copy-done.5, bf16[528,512]{1,0:T(8,128)(2,1)} %collective-permute-done.5.refs_0_.refs_1_, bf16[528,512]{1,0:T(8,128)(2,1)S(1)} %copy-done.7, ...), custom_call_target="tpu_custom_call" | custom-call | flops 528 | bytes 528 | tf_op jit(solution)/shard_map/pallas_call | solution.py:156
  101.8 2.5 %shard_map.76.refs_5_ = f32[3,528,128]{2,1,0:T(8,128)S(1)} custom-call(s32[64]{0:T(128)S(1)} %fusion.ids, bf16[528,512]{1,0:T(8,128)(2,1)} %collective-permute-done.7.refs_0_.refs_2_, bf16[528,512]{1,0:T(8,128)(2,1)} %collective-permute-done.15.refs_1_.refs_3_, bf16[3,4096,128]{2,1,0:T(8,128)(2,1)S(1)} %copy-done, ...), custom_call_target="tpu_custom_call", output_to_operand_aliasing={{}: (11, {})} | custom-call | flops 528 | bytes 528 | tf_op jit(solution)/shard_map/pallas_call | solution.py:156
  104.3 3.5 %shard_map.78.refs_5_ = f32[3,528,128]{2,1,0:T(8,128)S(1)} custom-call(s32[64]{0:T(128)S(1)} %fusion.ids, bf16[528,512]{1,0:T(8,128)(2,1)} %collective-permute-done.6.refs_0_, bf16[528,512]{1,0:T(8,128)(2,1)} %collective-permute-done.13.refs_1_, bf16[528,512]{1,0:T(8,128)(2,1)} %collective-permute-done.7.refs_0_.refs_2_, ...), custom_call_target="tpu_custom_call", output_to_operand_aliasing={{}: (21, {})} | custom-call | flops 528 | bytes 528 | tf_op jit(solution)/shard_map/pallas_call | solution.py:156
  109.8 2.6 %shard_map.82 = f32[1168,128]{1,0:T(8,128)} custom-call(f32[3,528,128]{2,1,0:T(8,128)S(1)} %shard_map.81.proj, f32[3,7,128]{2,1,0:T(8,128)S(1)} %reshape.59.taps, f32[16,128]{1,0:T(8,128)S(1)} %get-tuple-element.34.weights, f32[16,128]{1,0:T(8,128)S(1)} %get-tuple-element.35.decays, f32[1,128]{1,0:T(1,128)S(1)} %slice.32.skip), custom_call_target="tpu_custom_call" | custom-call | flops 7208960 | bytes 1310720 | tf_op jit(solution)/shard_map/pallas_call | solution.py:66
  119.1 23.5 %all_to_all.5 = f32[32,16,128]{2,1,0:T(8,128)S(1)} all-to-all(f32[32,16,128]{2,1,0:T(8,128)S(1)} %bitcast.14), channel_id=1, replica_groups={{0,8,32,40,64,72,96,104,128,136,160,168,192,200,224,232,256,264,288,296..., dimensions={0} | all-to-all | bytes 524288 | tf_op jit(solution)/shard_map/all_to_all | solution.py:279
  142.6 2.6 %shard_map.83 = f32[1024,128]{1,0:T(8,128)} custom-call(s32[1]{0:T(128)} %bitcast.half, f32[16,128]{1,0:T(8,128)S(1)} %reduce_sum.9.carried, f32[1168,128]{1,0:T(8,128)S(1)} %shard_map.80.mine, f32[1168,128]{1,0:T(8,128)} %collective-permute-done.18.other, f32[16,128]{1,0:T(8,128)S(1)} %multiply_bitcast_fusion.weights, f32[16,128]{1,0:T(8,128)S(1)} %bitcast.11), custom_call_target="tpu_custom_call" | custom-call | flops 4718592 | bytes 1572864 | tf_op jit(solution)/shard_map/pallas_call | solution.py:117
  (74 shorter events, 32.7 us)
Async XLA Ops:
  0.7 12.8 %collective-permute-start = (bf16[16,128]{1,0:T(8,128)(2,1)S(1)}, bf16[16,128]{1,0:T(8,128)(2,1)S(1)}, u32[]{:S(2)}, u32[]{:S(2)}) collective-permute-start(bf16[16,128]{1,0:T(8,128)(2,1)S(1)} %slice.21), channel_id=1, source_target_pairs={{0,32},{32,64},{64,96},{96,128},{128,160},{160,192},{192,224},{224... | collective-permute-start | bytes 12296 | tf_op jit(solution)/shard_map/ppermute | solution.py:217
  14.5 12.0 %collective-permute-start.1 = (bf16[528,128]{1,0:T(8,128)(2,1)S(1)}, bf16[528,128]{1,0:T(8,128)(2,1)S(1)}, u32[]{:S(2)}, u32[]{:S(2)}) collective-permute-start(bf16[528,128]{1,0:T(8,128)(2,1)S(1)} %get-tuple-element.32), channel_id=1, source_target_pairs={{0,8},{1,9},{2,10},{3,11},{4,12},{5,13},{6,14},{7,15},{8,0},{9,1},... | collective-permute-start | bytes 405512 | tf_op jit(solution)/shard_map/ppermute | solution.py:188
  17.6 12.8 %collective-permute-start.3 = (bf16[528,128]{1,0:T(8,128)(2,1)S(1)}, bf16[528,128]{1,0:T(8,128)(2,1)S(1)}, u32[]{:S(2)}, u32[]{:S(2)}) collective-permute-start(bf16[528,128]{1,0:T(8,128)(2,1)S(1)} %get-tuple-element.32), channel_id=1, source_target_pairs={{0,24},{1,25},{2,26},{3,27},{4,28},{5,29},{6,30},{7,31},{8,16},{9,... | collective-permute-start | bytes 405512 | tf_op jit(solution)/shard_map/ppermute | solution.py:188
  21.6 27.9 %copy-start = (bf16[3,4096,128]{2,1,0:T(8,128)(2,1)S(1)}, bf16[3,4096,128]{2,1,0:T(8,128)(2,1)}, u32[]{:S(2)}) copy-start(bf16[3,4096,128]{2,1,0:T(8,128)(2,1)} %refs_4_.9) | copy-start | bytes 9437188
  21.6 8.8 %collective-permute-start.2 = (bf16[528,128]{1,0:T(8,128)(2,1)S(1)}, bf16[528,128]{1,0:T(8,128)(2,1)S(1)}, u32[]{:S(2)}, u32[]{:S(2)}) collective-permute-start(bf16[528,128]{1,0:T(8,128)(2,1)S(1)} %get-tuple-element.31), channel_id=1, source_target_pairs={{0,16},{1,17},{2,18},{3,19},{4,20},{5,21},{6,22},{7,23},{8,24},{9,... | collective-permute-start | bytes 405512 | tf_op jit(solution)/shard_map/ppermute | solution.py:188
  30.5 9.6 %collective-permute-start.8 = (bf16[528,512]{1,0:T(8,128)(2,1)S(1)}, bf16[528,512]{1,0:T(8,128)(2,1)}, u32[]{:S(2)}, u32[]{:S(2)}) collective-permute-start(bf16[528,512]{1,0:T(8,128)(2,1)S(1)} %pad_maximum_fusion.refs_0_), channel_id=1, source_target_pairs={{0,32},{32,0},{64,96},{96,64},{128,160},{160,128},{192,224},{224,1... | collective-permute-start | bytes 1622024 | tf_op jit(solution)/shard_map/ppermute | solution.py:202
  32.4 11.2 %collective-permute-start.5 = (bf16[528,512]{1,0:T(8,128)(2,1)S(1)}, bf16[528,512]{1,0:T(8,128)(2,1)}, u32[]{:S(2)}, u32[]{:S(2)}) collective-permute-start(bf16[528,512]{1,0:T(8,128)(2,1)S(1)} %pad_maximum_fusion.refs_0_), channel_id=1, source_target_pairs={{0,1},{1,2},{2,3},{3,4},{4,5},{5,6},{6,7},{7,0},{8,9},{9,10},{10,1... | collective-permute-start | bytes 1622024 | tf_op jit(solution)/shard_map/ppermute | solution.py:199
  38.1 38.0 %collective-permute-start.4 = (bf16[3,2048,128]{2,1,0:T(8,128)(2,1)}, bf16[3,2048,128]{2,1,0:T(8,128)(2,1)}, u32[]{:S(2)}, u32[]{:S(2)}) collective-permute-start(bf16[3,2048,128]{2,1,0:T(8,128)(2,1)} %constant_dynamic-slice_fusion.2), channel_id=1, source_target_pairs={{0,8},{1,9},{2,10},{3,11},{4,12},{5,13},{6,14},{7,15},{8,0},{9,1},... | collective-permute-start | bytes 4718600 | tf_op jit(solution)/shard_map/ppermute | solution.py:188
  40.1 11.5 %collective-permute-start.9 = (bf16[528,512]{1,0:T(8,128)(2,1)}, bf16[528,512]{1,0:T(8,128)(2,1)}, u32[]{:S(2)}, u32[]{:S(2)}) collective-permute-start(bf16[528,512]{1,0:T(8,128)(2,1)} %collective-permute-done.8), channel_id=1, source_target_pairs={{0,1},{1,2},{2,3},{3,4},{4,5},{5,6},{6,7},{7,0},{8,9},{9,10},{10,1... | collective-permute-start | bytes 1622024 | tf_op jit(solution)/shard_map/ppermute | solution.py:199
  43.6 13.0 %collective-permute-start.6 = (bf16[528,512]{1,0:T(8,128)(2,1)}, bf16[528,512]{1,0:T(8,128)(2,1)}, u32[]{:S(2)}, u32[]{:S(2)}) collective-permute-start(bf16[528,512]{1,0:T(8,128)(2,1)} %collective-permute-done.5.refs_0_.refs_1_), channel_id=1, source_target_pairs={{0,1},{1,2},{2,3},{3,4},{4,5},{5,6},{6,7},{7,0},{8,9},{9,10},{10,1... | collective-permute-start | bytes 1622024 | tf_op jit(solution)/shard_map/ppermute | solution.py:199
  51.5 26.5 %copy-start.9 = (f32[3,7,128]{2,1,0:T(8,128)S(1)}, f32[3,7,128]{2,1,0:T(8,128)}, u32[]{:S(2)}) copy-start(f32[3,7,128]{2,1,0:T(8,128)} %taps.1) | copy-start | bytes 32260
  51.5 26.5 %copy-start.8 = (f32[128,16]{0,1:T(8,128)S(1)}, f32[128,16]{0,1:T(8,128)}, u32[]{:S(2)}) copy-start(f32[128,16]{0,1:T(8,128)} %param.11) | copy-start | bytes 24580
  51.5 26.5 %copy-start.11 = (f32[128,16]{0,1:T(8,128)S(1)}, f32[128,16]{0,1:T(8,128)}, u32[]{:S(2)}) copy-start(f32[128,16]{0,1:T(8,128)} %param.10) | copy-start | bytes 24580
  51.5 30.4 %copy-start.10 = (f32[128]{0:T(128)S(1)}, f32[128]{0:T(128)}, u32[]{:S(2)}) copy-start(f32[128]{0:T(128)} %param.12) | copy-start | bytes 1540
  51.6 11.0 %collective-permute-start.10 = (bf16[528,512]{1,0:T(8,128)(2,1)}, bf16[528,512]{1,0:T(8,128)(2,1)S(1)}, u32[]{:S(2)}, u32[]{:S(2)}) collective-permute-start(bf16[528,512]{1,0:T(8,128)(2,1)} %collective-permute-done.9), channel_id=1, source_target_pairs={{0,32},{32,0},{64,96},{96,64},{128,160},{160,128},{192,224},{224,1... | collective-permute-start | bytes 1622024 | tf_op jit(solution)/shard_map/ppermute | solution.py:202
  56.6 10.7 %collective-permute-start.7 = (bf16[528,512]{1,0:T(8,128)(2,1)}, bf16[528,512]{1,0:T(8,128)(2,1)}, u32[]{:S(2)}, u32[]{:S(2)}) collective-permute-start(bf16[528,512]{1,0:T(8,128)(2,1)} %collective-permute-done.6.refs_0_), channel_id=1, source_target_pairs={{0,1},{1,2},{2,3},{3,4},{4,5},{5,6},{6,7},{7,0},{8,9},{9,10},{10,1... | collective-permute-start | bytes 1622024 | tf_op jit(solution)/shard_map/ppermute | solution.py:199
  60.5 17.6 %collective-permute-start.12 = (bf16[528,512]{1,0:T(8,128)(2,1)}, bf16[528,512]{1,0:T(8,128)(2,1)}, u32[]{:S(2)}, u32[]{:S(2)}) collective-permute-start(bf16[528,512]{1,0:T(8,128)(2,1)} %collective-permute-done.9), channel_id=1, source_target_pairs={{0,1},{1,2},{2,3},{3,4},{4,5},{5,6},{6,7},{7,0},{8,9},{9,10},{10,1... | collective-permute-start | bytes 1622024 | tf_op jit(solution)/shard_map/ppermute | solution.py:199
  76.1 21.4 %collective-permute-start.16 = (bf16[3,2048,128]{2,1,0:T(8,128)(2,1)}, bf16[3,2048,128]{2,1,0:T(8,128)(2,1)}, u32[]{:S(2)}, u32[]{:S(2)}) collective-permute-start(bf16[3,2048,128]{2,1,0:T(8,128)(2,1)} %collective-permute-done.4), channel_id=1, source_target_pairs={{0,32},{32,0},{64,96},{96,64},{128,160},{160,128},{192,224},{224,1... | collective-permute-start | bytes 4718600 | tf_op jit(solution)/shard_map/ppermute | solution.py:202
  78.1 11.0 %collective-permute-start.14 = (bf16[528,512]{1,0:T(8,128)(2,1)}, bf16[528,512]{1,0:T(8,128)(2,1)}, u32[]{:S(2)}, u32[]{:S(2)}) collective-permute-start(bf16[528,512]{1,0:T(8,128)(2,1)} %collective-permute-done.12), channel_id=1, source_target_pairs={{0,1},{1,2},{2,3},{3,4},{4,5},{5,6},{6,7},{7,0},{8,9},{9,10},{10,1... | collective-permute-start | bytes 1622024 | tf_op jit(solution)/shard_map/ppermute | solution.py:199
  81.9 11.3 %collective-permute-start.17 = (f32[54,128]{1,0:T(8,128)S(1)}, f32[54,128]{1,0:T(8,128)S(1)}, u32[]{:S(2)}, u32[]{:S(2)}) collective-permute-start(f32[54,128]{1,0:T(8,128)S(1)} %pad_maximum_fusion.1), channel_id=1, source_target_pairs={{0,8},{1,9},{2,10},{3,11},{4,12},{5,13},{6,14},{7,15},{8,0},{9,1},... | collective-permute-start | bytes 82952 | tf_op jit(solution)/shard_map/ppermute | solution.py:188
  83.9 13.6 %collective-permute-start.11 = (bf16[528,512]{1,0:T(8,128)(2,1)}, bf16[528,512]{1,0:T(8,128)(2,1)}, u32[]{:S(2)}, u32[]{:S(2)}) collective-permute-start(bf16[528,512]{1,0:T(8,128)(2,1)} %collective-permute-done.7.refs_0_.refs_2_), channel_id=1, source_target_pairs={{0,1},{1,2},{2,3},{3,4},{4,5},{5,6},{6,7},{7,0},{8,9},{9,10},{10,1... | collective-permute-start | bytes 1622024 | tf_op jit(solution)/shard_map/ppermute | solution.py:199
  87.1 7.8 %collective-permute-start.13 = (bf16[528,512]{1,0:T(8,128)(2,1)}, bf16[528,512]{1,0:T(8,128)(2,1)}, u32[]{:S(2)}, u32[]{:S(2)}) collective-permute-start(bf16[528,512]{1,0:T(8,128)(2,1)} %collective-permute-done.12), channel_id=1, source_target_pairs={{0,32},{32,0},{64,96},{96,64},{128,160},{160,128},{192,224},{224,1... | collective-permute-start | bytes 1622024 | tf_op jit(solution)/shard_map/ppermute | solution.py:202
  89.1 12.7 %collective-permute-start.15 = (bf16[528,512]{1,0:T(8,128)(2,1)}, bf16[528,512]{1,0:T(8,128)(2,1)}, u32[]{:S(2)}, u32[]{:S(2)}) collective-permute-start(bf16[528,512]{1,0:T(8,128)(2,1)} %collective-permute-done.14), channel_id=1, source_target_pairs={{0,32},{32,0},{64,96},{96,64},{128,160},{160,128},{192,224},{224,1... | collective-permute-start | bytes 1622024 | tf_op jit(solution)/shard_map/ppermute | solution.py:202
  112.4 30.1 %collective-permute-start.18 = (f32[1168,128]{1,0:T(8,128)}, f32[1168,128]{1,0:T(8,128)}, u32[]{:S(2)}, u32[]{:S(2)}) collective-permute-start(f32[1168,128]{1,0:T(8,128)} %shard_map.82), channel_id=1, source_target_pairs={{0,8},{1,9},{2,10},{3,11},{4,12},{5,13},{6,14},{7,15},{8,0},{9,1},... | collective-permute-start | bytes 1794056 | tf_op jit(solution)/shard_map/ppermute | solution.py:188
  (7 other events, 10.2 us)

commit v4 on v3

v4 whole, which is shorter than its diff:
```python
import functools

import jax
import jax.numpy as jnp
import numpy as np
from jax import lax
from jax.experimental import pallas as pl
from jax.experimental.pallas import tpu as pltpu
from jax.sharding import PartitionSpec as P

MODES = 16
TAPS = 7
HALO = 16
CHUNKS = 8
UNROLL = 8
LANES = 128
RING = 8
LINES = 4
SMEM = pl.BlockSpec(memory_space=pltpu.SMEM)
VMEM = pl.BlockSpec(memory_space=pltpu.VMEM)


def wide(row):
    return jnp.broadcast_to(row, (CHUNKS, LANES))


def met_rows(weights, s, at):
    count = weights[0].shape[1] // LANES
    parts = [
        w[s, pl.ds(pl.multiple_of(jnp.clip(at - i * count, 0, count - 1) * LANES, LANES), LANES), :]
        for i, w in enumerate(weights)
    ]
    return parts[0] if len(parts) == 1 else jnp.where(at < count, parts[0], parts[1])


def products(blocks, ids, at, weights):
    total = None
    for b, block in enumerate(blocks):
        rows = [ids[LINES * (at + b) + k] for k in range(LINES)]
        met = jnp.concatenate(
            [jnp.concatenate([met_rows(weights, s, r) for s in range(3)], axis=1) for r in rows], axis=0
        )
        part = jnp.dot(block[...], met, preferred_element_type=jnp.float32)
        total = part if total is None else total + part
    return [total[:, s * LANES : (s + 1) * LANES] for s in range(3)]


def project_kernel(count, kinds, at, ids, *refs):
    weights, refs = refs[:kinds], refs[kinds:]
    blocks, sums, out = refs[:count], refs[count:-1], refs[-1]
    for s, part in enumerate(products(blocks, ids, at, weights)):
        out[s] = sums[0][s] + part if sums else part


def project(sums, blocks, ids, at, in_weights):
    extra = [] if sums is None else [sums]
    rows = blocks[0].shape[0]
    return pl.pallas_call(
        functools.partial(project_kernel, len(blocks), len(in_weights), at),
        in_specs=[SMEM] + [VMEM] * (len(in_weights) + len(blocks) + len(extra)),
        out_specs=VMEM,
        out_shape=jax.ShapeDtypeStruct((3, rows, LANES), jnp.float32),
        input_output_aliases={1 + len(in_weights) + len(blocks): 0} if extra else {},
        compiler_params=pltpu.CompilerParams(vmem_limit_bytes=16 * 2**20),
        cost_estimate=pl.CostEstimate(flops=rows, bytes_accessed=rows, transcendentals=0),
    )(ids, *in_weights, *blocks, *extra)


def local_kernel(count, kinds, at, seat, ids, sums, taps, weights, decays, skip, *refs):
    in_weights, blocks, (pack, sent, proj, ends) = refs[:kinds], refs[kinds : kinds + count], refs[-4:]
    rows = proj.shape[1] - HALO
    length = rows // CHUNKS
    for s, part in enumerate(products(blocks, ids, at, in_weights)):
        proj[s] = sums[s] + part
    poles = [wide(jnp.exp(-decays[m : m + 1, :])) for m in range(MODES)]
    gains = [wide(weights[m : m + 1, :]) for m in range(MODES)]
    skip_row = wide(skip[0:1, :])

    def steps(at, states):
        states = list(states)
        at = at * UNROLL
        taken = [
            [
                proj[s, pl.ds(at + HALO - (TAPS - 1) + k, CHUNKS, stride=length), :]
                for k in range(UNROLL + TAPS - 1)
            ]
            for s in range(3)
        ]
        coef = [[wide(taps[s, j : j + 1, :]) for j in range(TAPS)] for s in range(3)]
        for u in range(UNROLL):
            filtered = [sum(coef[s][j] * taken[s][u + j] for j in range(TAPS)) for s in range(3)]
            gated = filtered[1] * filtered[2]
            total = skip_row * gated
            for m in range(MODES):
                states[m] = poles[m] * states[m] + gated
                total = total + gains[m] * states[m]
            here = pl.multiple_of((at + u) * CHUNKS, CHUNKS)
            pack[pl.ds(here, CHUNKS), :] = filtered[0]
            pack[pl.ds(rows + here, CHUNKS), :] = filtered[0] * total
        return tuple(states)

    zero = jnp.zeros((CHUNKS, LANES), jnp.float32)
    states = lax.fori_loop(0, length // UNROLL, steps, (zero,) * MODES)
    for m in range(MODES):
        ends[m * CHUNKS : (m + 1) * CHUNKS, :] = states[m]
    over = jnp.exp(-decays[...] * float(length))
    carry = jnp.zeros((MODES, LANES), jnp.float32)
    for c in range(CHUNKS):
        pack[2 * rows + c * MODES : 2 * rows + (c + 1) * MODES, :] = carry
        carry = over * carry + ends[pl.ds(c, MODES, stride=CHUNKS), :]
    pack[2 * rows + CHUNKS * MODES : 2 * rows + (CHUNKS + 1) * MODES, :] = carry
    mine, half, owner = seat[0], seat[1], seat[2]
    for j in range(sent.shape[1]):
        ahead = j - mine - 1
        distance = (jnp.maximum(ahead, 0) * 2 * rows + (1 - half) * rows).astype(jnp.float32)
        sent[owner, j] = jnp.where(ahead >= 0, jnp.exp(-decays[...] * distance) * carry, 0.0)


def local_part(sent, sums, blocks, seat, ids, at, in_weights, taps, weights, decays, skip, count):
    rows = sums.shape[1] - HALO
    extra = [] if sent is None else [sent]
    return pl.pallas_call(
        functools.partial(local_kernel, len(blocks), len(in_weights), at),
        in_specs=[SMEM] * 2 + [VMEM] * (5 + len(in_weights) + len(blocks) + len(extra)),
        out_specs=[VMEM] * 2,
        out_shape=[
            jax.ShapeDtypeStruct((2 * rows + (CHUNKS + 1) * MODES, LANES), jnp.float32),
            jax.ShapeDtypeStruct((2, count, MODES, LANES), jnp.float32),
        ],
        input_output_aliases={7 + len(in_weights) + len(blocks): 1} if extra else {},
        scratch_shapes=[
            pltpu.VMEM(sums.shape, jnp.float32),
            pltpu.VMEM((MODES * CHUNKS, LANES), jnp.float32),
        ],
        compiler_params=pltpu.CompilerParams(vmem_limit_bytes=16 * 2**20),
        cost_estimate=pl.CostEstimate(
            flops=rows * LANES * 110, bytes_accessed=rows * LANES * 20, transcendentals=0
        ),
    )(seat, ids, sums, taps, weights, decays, skip, *in_weights, *blocks, *extra)


def final_kernel(rows, seat, arrived, mine, other, weights, decays, out, begins):
    length = rows // CHUNKS
    half = seat[1]
    low = half == 0
    end = slice(2 * rows + CHUNKS * MODES, 2 * rows + (CHUNKS + 1) * MODES)
    poles = [wide(jnp.exp(-decays[m : m + 1, :])) for m in range(MODES)]
    over = jnp.exp(-decays[...] * float(length))
    beyond = jnp.exp(-decays[...] * float(rows))
    early = sum(arrived[k] for k in range(arrived.shape[0]))
    late = beyond * early + jnp.where(low, mine[end, :], other[end, :])
    for pack, begin, offset in (
        (mine, jnp.where(low, early, late), half * rows),
        (other, jnp.where(low, late, early), (1 - half) * rows),
    ):
        reach = jnp.ones_like(over)
        for c in range(CHUNKS):
            start = pack[2 * rows + c * MODES : 2 * rows + (c + 1) * MODES, :]
            begins[pl.ds(c, MODES, stride=CHUNKS), :] = weights[...] * (start + reach * begin)
            reach = reach * over

        def steps(at, terms, pack=pack, offset=offset):
            terms = list(terms)
            at = at * UNROLL
            for u in range(UNROLL):
                terms = [poles[m] * terms[m] for m in range(MODES)]
                sums = terms
                while len(sums) > 1:
                    sums = [sums[i] + sums[i + 1] for i in range(0, len(sums), 2)]
                here = pl.multiple_of((at + u) * CHUNKS, CHUNKS)
                out[pl.ds(offset + at + u, CHUNKS, stride=length), :] = (
                    pack[pl.ds(rows + here, CHUNKS), :] + pack[pl.ds(here, CHUNKS), :] * sums[0]
                )
            return tuple(terms)

        terms = tuple(begins[m * CHUNKS : (m + 1) * CHUNKS, :] for m in range(MODES))
        lax.fori_loop(0, length // UNROLL, steps, terms)


def final_part(seat, arrived, mine, other, weights, decays):
    rows = (mine.shape[0] - (CHUNKS + 1) * MODES) // 2
    return pl.pallas_call(
        functools.partial(final_kernel, rows),
        in_specs=[SMEM] + [VMEM] * 5,
        out_specs=VMEM,
        out_shape=jax.ShapeDtypeStruct((2 * rows, LANES), jnp.float32),
        scratch_shapes=[pltpu.VMEM((MODES * CHUNKS, LANES), jnp.float32)],
        compiler_params=pltpu.CompilerParams(vmem_limit_bytes=16 * 2**20),
        cost_estimate=pl.CostEstimate(
            flops=rows * LANES * 72, bytes_accessed=rows * LANES * 24, transcendentals=0
        ),
    )(seat, arrived, mine, other, weights, decays)


def per_device(tokens, in_weights, short_taps, residues, decays, skip_gain):
    rows = tokens.shape[0]
    part = rows // 2
    blocks = lax.axis_size("ctx")
    ring, lines = RING, LINES
    mine = lax.axis_index("ctx")
    place = mine * lines * ring + lax.axis_index("ch")
    half = lax.axis_index("ch") // ring % 2
    weights = (residues * jnp.sqrt(2.0 * decays / MODES)).T
    rates = decays.T

    def beside(block, step):
        return lax.ppermute(
            block, "ch", [(z * ring + y, (z ^ step) * ring + y) for z in range(lines) for y in range(ring)]
        )

    def onward(block):
        route = []
        for i in range(blocks):
            for z in range(lines):
                for y in range(ring):
                    at = (i * lines + z) * ring
                    route.append((at + y, at + (y + 1 - i % 2 * 2) % ring))
        return lax.ppermute(block, ("ctx", "ch"), route)

    def other_core(block):
        return lax.ppermute(block, "ctx", [(i, i ^ 1) for i in range(blocks)])

    table = np.zeros((2, 2, lines, ring, ring, lines), np.int32)
    for c, z, y, k in np.ndindex(2, lines, ring, lines):
        way = 1 - 2 * c
        places = [y] + [y + way * d for step in range(1, ring // 2) for d in (-step, step)] + [y + ring // 2]
        ids = (z ^ k) * ring + np.array(places) % ring
        count = lines * ring // 2
        table[c, 0, z, y, :, k] = ids
        table[c, 1, z, y, :, k] = ids % count + count * (ids // count != c)
    table = table.transpose(0, 2, 3, 1, 4, 5).reshape(2, lines * ring, -1)[np.arange(blocks) % 2]
    ids = lax.dynamic_index_in_dim(
        jnp.asarray(table.reshape(-1, 2 * lines * ring)), place, 0, keepdims=False
    )

    seat = jnp.stack([mine, half, half]).astype(jnp.int32)
    other_seat = jnp.stack([mine, half, 1 - half]).astype(jnp.int32)

    before = lax.ppermute(tokens[rows - HALO :], "ctx", [(i, i + 1) for i in range(blocks - 1)])
    padded = jnp.concatenate([before, tokens], axis=0)
    kept = lax.dynamic_slice_in_dim(padded, half * part, part + HALO, 0)
    given = lax.dynamic_slice_in_dim(padded, (1 - half) * part, part + HALO, 0)
    nearest = beside(given, 1)
    count = in_weights.shape[1] // 2
    half_weights = lax.dynamic_slice_in_dim(in_weights, mine % 2 * count, count, 1)
    values = jnp.concatenate([short_taps.reshape(3 * TAPS, -1), weights, rates, skip_gain[None, :]], axis=0)
    nearest, half_weights, values = lax.optimization_barrier((nearest, half_weights, values))
    half_weights, values = beside(half_weights, 1), beside(values, 1)
    block = jnp.concatenate([kept, nearest, beside(kept, 2), beside(given, 3)], axis=1)

    straight, turned = onward(block), other_core(block)
    crossed = onward(turned)
    sums, waiting, met = None, [block], 0
    arrived = []
    for step in range(1, ring // 2):
        straight, turned = lax.optimization_barrier((straight, turned))
        crossed, here = lax.optimization_barrier((crossed, straight))
        turned = crossed
        if step == ring // 2 - 1:
            crossed, waiting[1] = lax.optimization_barrier((crossed, waiting[1]))
        straight = onward(straight)
        swapped = other_core(crossed)
        if step < ring // 2 - 1:
            crossed = onward(crossed)
        sums = project(sums, waiting, ids, met, [in_weights])
        arrived += waiting
        met += len(waiting)
        waiting = [here, swapped]
        if step < ring // 2 - 1:
            straight, sums = lax.optimization_barrier((straight, sums))
    half_weights, sums = lax.optimization_barrier((half_weights, sums))
    their_weights = [half_weights, other_core(half_weights)]
    theirs = project(None, arrived[:met], ids, ring, their_weights)
    waiting.append(straight)

    other_pack, sent = local_part(
        None, theirs, waiting, other_seat, ids, ring + met, their_weights,
        values[: 3 * TAPS].reshape(3, TAPS, -1),
        values[3 * TAPS : 3 * TAPS + MODES],
        values[3 * TAPS + MODES : 3 * TAPS + 2 * MODES],
        values[3 * TAPS + 2 * MODES :],
        blocks,
    )
    other = beside(other_pack, 1)
    pack, sent = local_part(
        sent, sums, waiting, seat, ids, met, [in_weights], short_taps, weights, rates, skip_gain[None, :], blocks
    )
    groups = [
        [(i * lines + z + q) * ring + y for q in range(2) for i in range(blocks)]
        for z in range(0, lines, 2)
        for y in range(ring)
    ]
    states = lax.all_to_all(
        sent.reshape(2 * blocks, MODES, LANES), ("ctx", "ch"), 0, 0, axis_index_groups=groups, tiled=True
    )
    return final_part(seat, states, pack, other, weights, rates)


def solution(mesh):
    return jax.shard_map(
        per_device,
        mesh=mesh,
        in_specs=(
            P("ctx", "ch"),
            P(None, None, "ch"),
            P(None, None, "ch"),
            P("ch", None),
            P("ch", None),
            P("ch"),
        ),
        out_specs=P("ctx", "ch"),
        check_vma=False,
    )
```

time: 146 us -> 140 us (0.959)
  Pallas kernels: 25.5 us -> 20.4 us
    pallas_call x11 -> x7, Pallas kernels: 25.5 us -> 20.4 us  [the longest x2 9.47 us: local_part(): pl.pallas_call(functools.partial(local_kernel, len(blocks), len(in_weight...]
    ppermute x6, waiting for transfers between devices: 12.8 us -> 10.9 us  [beside(): lax.ppermute(block, 'ch', [(z * ring + y, (z ^ step) * ring + y) for z in...]
    concatenate x1 -> x0, local copies, waits for them, and re-layouts: 1.7 us -> none  [per_device(): jnp.concatenate([half_weights, other_core(half_weights)], axis=1)]
    ppermute x7, waiting for transfers between devices: 4.96 us -> 6.56 us  [onward(): return lax.ppermute(block, ('ctx', 'ch'), route)]
    unnamed x26 -> x31, local copies, waits for them, and re-layouts: 4.39 us -> 5.91 us
  transfers between devices with their start and end apart: 19 -> 19, of which waited for: 6 -> 6; matrix products, arithmetic and copies ran while one was open for 5% -> 3% of each run, Pallas kernels for 8% -> 9%
where the time goes in v4:
time: 140 us; the launch traced here: 138 us
  starting transfers between devices  65.3 us (47%)
  blocking collectives  22.8 us (16%)
  Pallas kernels  20.4 us (15%)
  waiting for transfers between devices  17.4 us (12%)
  local copies, waits for them, and re-layouts  10.9 us (8%)
    ppermute x7, starting transfers between devices, onward(): return lax.ppermute(block, ('ctx', 'ch'), route)  26.9 us
    all_to_all x1, blocking collectives, per_device(): lax.all_to_all(sent.reshape(2 * blocks, MODES, LANES), ('ctx', 'ch'), 0,...  22.8 us
    ppermute x6, starting transfers between devices, beside(): lax.ppermute(block, 'ch', [(z * ring + y, (z ^ step) * ring + y) for z in...  14.8 us
    ppermute x1, starting transfers between devices, per_device(): lax.ppermute(tokens[rows - HALO:], 'ctx', [(i, i + 1) for i in range(bloc...  12 us
    ppermute x5, starting transfers between devices, other_core(): return lax.ppermute(block, 'ctx', [(i, i ^ 1) for i in range(blocks)])  11.6 us
    ppermute x6, waiting for transfers between devices, beside(): lax.ppermute(block, 'ch', [(z * ring + y, (z ^ step) * ring + y) for z in...  10.9 us
    pallas_call x2, Pallas kernels, local_part(): pl.pallas_call(functools.partial(local_kernel, len(blocks), len(in_weight...  9.47 us
    pallas_call x4, Pallas kernels, project(): pl.pallas_call(functools.partial(project_kernel, len(blocks), len(in_weig...  8.76 us
  transfers between devices with their start and end apart: 19, of which 6 were waited for; matrix products, arithmetic and copies ran while one was open for 3% of the time, Pallas kernels for 9%

profile of v4, /device:TPU:1, one launch (start us, length us, event | category | flops | bytes accessed | tf_op | source)
XLA Modules:
  0.0 138.5 jit_solution(13907286920483178115)
XLA Ops:
  0.7 12.0 %collective-permute-start = (bf16[16,128]{1,0:T(8,128)(2,1)S(1)}, bf16[16,128]{1,0:T(8,128)(2,1)S(1)}, u32[]{:S(2)}, u32[]{:S(2)}) collective-permute-start(bf16[16,128]{1,0:T(8,128)(2,1)S(1)} %slice.15), channel_id=1, source_target_pairs={{0,32},{32,64},{64,96},{96,128},{128,160},{160,192},{192,224},{224... | collective-permute-start | bytes 12296 | tf_op jit(solution)/shard_map/ppermute | solution.py:239
  12.8 2.8 %constant_dynamic-slice_fusion.1 = bf16[3,2048,128]{2,1,0:T(8,128)(2,1)} fusion(bf16[3,4096,128]{2,1,0:T(8,128)(2,1)} %refs_0_.7, s32[]{:T(128)S(6)} %select_n.33), kind=kLoop, calls=%fused_computation.6 | loop fusion | bytes 3145732 | tf_op jit(solution)/shard_map/dynamic_slice | solution.py:245
  16.4 3.1 %collective-permute-start.1 = (bf16[528,128]{1,0:T(8,128)(2,1)}, bf16[528,128]{1,0:T(8,128)(2,1)S(1)}, u32[]{:S(2)}, u32[]{:S(2)}) collective-permute-start(bf16[528,128]{1,0:T(8,128)(2,1)} %get-tuple-element.54), channel_id=1, source_target_pairs={{0,8},{1,9},{2,10},{3,11},{4,12},{5,13},{6,14},{7,15},{8,0},{9,1},... | collective-permute-start | bytes 405512 | tf_op jit(solution)/shard_map/ppermute | solution.py:207
  19.5 4.0 %collective-permute-start.4 = (bf16[528,128]{1,0:T(8,128)(2,1)}, bf16[528,128]{1,0:T(8,128)(2,1)}, u32[]{:S(2)}, u32[]{:S(2)}) collective-permute-start(bf16[528,128]{1,0:T(8,128)(2,1)} %get-tuple-element.54), channel_id=1, source_target_pairs={{0,24},{1,25},{2,26},{3,27},{4,28},{5,29},{6,30},{7,31},{8,16},{9,... | collective-permute-start | bytes 405512 | tf_op jit(solution)/shard_map/ppermute | solution.py:207
  23.5 1.9 %collective-permute-start.3 = (bf16[528,128]{1,0:T(8,128)(2,1)S(1)}, bf16[528,128]{1,0:T(8,128)(2,1)}, u32[]{:S(2)}, u32[]{:S(2)}) collective-permute-start(bf16[528,128]{1,0:T(8,128)(2,1)S(1)} %get-tuple-element.53), channel_id=1, source_target_pairs={{0,16},{1,17},{2,18},{3,19},{4,20},{5,21},{6,22},{7,23},{8,24},{9,... | collective-permute-start | bytes 405512 | tf_op jit(solution)/shard_map/ppermute | solution.py:207
  25.5 7.0 %collective-permute-done.3 = bf16[528,128]{1,0:T(8,128)(2,1)} collective-permute-done((bf16[528,128]{1,0:T(8,128)(2,1)S(1)}, bf16[528,128]{1,0:T(8,128)(2,1)}, u32[]{:S(2)}, u32[]{:S(2)}) %collective-permute-start.3) | collective-permute-done | bytes 135200 | tf_op jit(solution)/shard_map/ppermute | solution.py:207
  35.5 4.4 %collective-permute-start.7 = (bf16[528,512]{1,0:T(8,128)(2,1)S(1)}, bf16[528,512]{1,0:T(8,128)(2,1)}, u32[]{:S(2)}, u32[]{:S(2)}) collective-permute-start(bf16[528,512]{1,0:T(8,128)(2,1)S(1)} %pad_maximum_fusion.refs_1_.refs_2_), channel_id=1, source_target_pairs={{0,1},{1,2},{2,3},{3,4},{4,5},{5,6},{6,7},{7,0},{8,9},{9,10},{10,1... | collective-permute-start | bytes 1622024 | tf_op jit(solution)/shard_map/ppermute | solution.py:218
  40.8 3.0 %collective-permute-start.6 = (bf16[528,512]{1,0:T(8,128)(2,1)S(1)}, bf16[528,512]{1,0:T(8,128)(2,1)}, u32[]{:S(2)}, u32[]{:S(2)}) collective-permute-start(bf16[528,512]{1,0:T(8,128)(2,1)S(1)} %collective-permute-done.5), channel_id=1, source_target_pairs={{0,1},{1,2},{2,3},{3,4},{4,5},{5,6},{6,7},{7,0},{8,9},{9,10},{10,1... | collective-permute-start | bytes 1622024 | tf_op jit(solution)/shard_map/ppermute | solution.py:218
  46.2 5.1 %collective-permute-start.9 = (bf16[528,512]{1,0:T(8,128)(2,1)}, bf16[528,512]{1,0:T(8,128)(2,1)}, u32[]{:S(2)}, u32[]{:S(2)}) collective-permute-start(bf16[528,512]{1,0:T(8,128)(2,1)} %collective-permute-done.7.refs_1_.refs_3_), channel_id=1, source_target_pairs={{0,1},{1,2},{2,3},{3,4},{4,5},{5,6},{6,7},{7,0},{8,9},{9,10},{10,1... | collective-permute-start | bytes 1622024 | tf_op jit(solution)/shard_map/ppermute | solution.py:218
  52.0 5.1 %collective-permute-start.8 = (bf16[528,512]{1,0:T(8,128)(2,1)}, bf16[528,512]{1,0:T(8,128)(2,1)}, u32[]{:S(2)}, u32[]{:S(2)}) collective-permute-start(bf16[528,512]{1,0:T(8,128)(2,1)} %collective-permute-done.6), channel_id=1, source_target_pairs={{0,1},{1,2},{2,3},{3,4},{4,5},{5,6},{6,7},{7,0},{8,9},{9,10},{10,1... | collective-permute-start | bytes 1622024 | tf_op jit(solution)/shard_map/ppermute | solution.py:218
  61.9 4.0 %collective-permute-start.11 = (bf16[528,512]{1,0:T(8,128)(2,1)}, bf16[528,512]{1,0:T(8,128)(2,1)}, u32[]{:S(2)}, u32[]{:S(2)}) collective-permute-start(bf16[528,512]{1,0:T(8,128)(2,1)} %collective-permute-done.9.refs_1_.refs_5_), channel_id=1, source_target_pairs={{0,1},{1,2},{2,3},{3,4},{4,5},{5,6},{6,7},{7,0},{8,9},{9,10},{10,1... | collective-permute-start | bytes 1622024 | tf_op jit(solution)/shard_map/ppermute | solution.py:218
  65.9 2.9 %collective-permute-start.10 = (bf16[528,512]{1,0:T(8,128)(2,1)}, bf16[528,512]{1,0:T(8,128)(2,1)}, u32[]{:S(2)}, u32[]{:S(2)}) collective-permute-start(bf16[528,512]{1,0:T(8,128)(2,1)} %collective-permute-done.8), channel_id=1, source_target_pairs={{0,1},{1,2},{2,3},{3,4},{4,5},{5,6},{6,7},{7,0},{8,9},{9,10},{10,1... | collective-permute-start | bytes 1622024 | tf_op jit(solution)/shard_map/ppermute | solution.py:218
  68.8 2.2 %collective-permute-start.13 = (bf16[528,512]{1,0:T(8,128)(2,1)}, bf16[528,512]{1,0:T(8,128)(2,1)S(1)}, u32[]{:S(2)}, u32[]{:S(2)}) collective-permute-start(bf16[528,512]{1,0:T(8,128)(2,1)} %collective-permute-done.8), channel_id=1, source_target_pairs={{0,32},{32,0},{64,96},{96,64},{128,160},{160,128},{192,224},{224,1... | collective-permute-start | bytes 1622024 | tf_op jit(solution)/shard_map/ppermute | solution.py:221
  71.0 2.0 %shard_map.74.refs_3_ = f32[3,528,128]{2,1,0:T(8,128)S(1)} custom-call(s32[64]{0:T(128)S(1)} %fusion.ids, bf16[3,4096,128]{2,1,0:T(8,128)(2,1)S(1)} %copy-done, bf16[528,512]{1,0:T(8,128)(2,1)} %collective-permute-done.7.refs_1_.refs_3_, bf16[528,512]{1,0:T(8,128)(2,1)S(1)} %collective-permute-done.12.refs_2_.refs_4_, ...), custom_call_target="tpu_custom_call", output_to_operand_aliasing={{}: (4, {})} | custom-call | flops 528 | bytes 528 | tf_op jit(solution)/shard_map/pallas_call | solution.py:58
  73.0 5.3 %collective-permute-done.10 = bf16[528,512]{1,0:T(8,128)(2,1)} collective-permute-done((bf16[528,512]{1,0:T(8,128)(2,1)}, bf16[528,512]{1,0:T(8,128)(2,1)}, u32[]{:S(2)}, u32[]{:S(2)}) %collective-permute-start.10) | collective-permute-done | bytes 540704 | tf_op jit(solution)/shard_map/ppermute | solution.py:218
  78.4 2.0 %shard_map.75.sums = f32[3,528,128]{2,1,0:T(8,128)S(1)} custom-call(s32[64]{0:T(128)S(1)} %fusion.ids, bf16[3,4096,128]{2,1,0:T(8,128)(2,1)S(1)} %copy-done, bf16[528,512]{1,0:T(8,128)(2,1)} %collective-permute-done.9.refs_1_.refs_5_, bf16[528,512]{1,0:T(8,128)(2,1)S(1)} %collective-permute-done.13.refs_2_.refs_6_, ...), custom_call_target="tpu_custom_call", output_to_operand_aliasing={{}: (4, {})} | custom-call | flops 528 | bytes 528 | tf_op jit(solution)/shard_map/pallas_call | solution.py:58
  82.1 3.7 %collective-permute-start.16 = (bf16[3,2048,128]{2,1,0:T(8,128)(2,1)}, bf16[3,2048,128]{2,1,0:T(8,128)(2,1)}, u32[]{:S(2)}, u32[]{:S(2)}) collective-permute-start(bf16[3,2048,128]{2,1,0:T(8,128)(2,1)} %collective-permute-done.2.refs_0_), channel_id=1, source_target_pairs={{0,32},{32,0},{64,96},{96,64},{128,160},{160,128},{192,224},{224,1... | collective-permute-start | bytes 4718600 | tf_op jit(solution)/shard_map/ppermute | solution.py:221
  85.8 2.4 %collective-permute-start.15 = (bf16[528,512]{1,0:T(8,128)(2,1)}, bf16[528,512]{1,0:T(8,128)(2,1)}, u32[]{:S(2)}, u32[]{:S(2)}) collective-permute-start(bf16[528,512]{1,0:T(8,128)(2,1)} %collective-permute-done.11.refs_2_.refs_1_), channel_id=1, source_target_pairs={{0,1},{1,2},{2,3},{3,4},{4,5},{5,6},{6,7},{7,0},{8,9},{9,10},{10,1... | collective-permute-start | bytes 1622024 | tf_op jit(solution)/shard_map/ppermute | solution.py:218
  92.1 3.0 %collective-permute-done.17 = f32[54,128]{1,0:T(8,128)S(1)} collective-permute-done((f32[54,128]{1,0:T(8,128)S(1)}, f32[54,128]{1,0:T(8,128)S(1)}, u32[]{:S(2)}, u32[]{:S(2)}) %collective-permute-start.17) | collective-permute-done | bytes 27680 | tf_op jit(solution)/shard_map/ppermute | solution.py:207
  98.2 3.8 %shard_map.76.sums = f32[3,528,128]{2,1,0:T(8,128)S(1)} custom-call(s32[64]{0:T(128)S(1)} %fusion.ids, bf16[3,2048,128]{2,1,0:T(8,128)(2,1)} %collective-permute-done.2.refs_0_, bf16[3,2048,128]{2,1,0:T(8,128)(2,1)} %collective-permute-done.16.refs_1_, bf16[528,512]{1,0:T(8,128)(2,1)S(1)} %copy-done.5, ...), custom_call_target="tpu_custom_call" | custom-call | flops 528 | bytes 528 | tf_op jit(solution)/shard_map/pallas_call | solution.py:58
  102.1 5.2 %shard_map.77 = (f32[1168,128]{1,0:T(8,128)S(1)}, f32[2,16,16,128]{3,2,1,0:T(8,128)S(1)}) custom-call(s32[3]{0:T(128)S(1)} %pad_add_fusion.2.seat, s32[64]{0:T(128)S(1)} %fusion.ids, f32[3,528,128]{2,1,0:T(8,128)S(1)} %shard_map.76.sums, f32[3,7,128]{2,1,0:T(8,128)S(1)} %reshape.10.taps, f32[16,128]{1,0:T(8,128)S(1)} %get-tuple-element.56.weights, ...), custom_call_target="tpu_custom_call" | custom-call | flops 7208960 | bytes 1310720 | tf_op jit(solution)/shard_map/pallas_call | solution.py:122
  109.3 4.2 %shard_map.78 = (f32[1168,128]{1,0:T(8,128)S(1)}, f32[2,16,16,128]{3,2,1,0:T(8,128)S(1)}) custom-call(s32[3]{0:T(128)S(1)} %pad_add_fusion.seat, s32[64]{0:T(128)S(1)} %fusion.ids, f32[3,528,128]{2,1,0:T(8,128)S(1)} %copy-done.2, f32[3,7,128]{2,1,0:T(8,128)S(1)} %copy-done.11, ...), custom_call_target="tpu_custom_call", output_to_operand_aliasing={{1}: (11, {})} | custom-call | flops 7208960 | bytes 1310720 | tf_op jit(solution)/shard_map/pallas_call | solution.py:122
  113.6 22.8 %all_to_all.5.arrived = f32[32,16,128]{2,1,0:T(8,128)S(1)} all-to-all(f32[32,16,128]{2,1,0:T(8,128)S(1)} %bitcast.10), channel_id=1, replica_groups={{0,32,64,96,128,160,192,224,256,288,320,352,384,416,448,480,8,40,72,104..., dimensions={0} | all-to-all | bytes 524288 | tf_op jit(solution)/shard_map/all_to_all | solution.py:293
  136.3 2.1 %shard_map.79 = f32[1024,128]{1,0:T(8,128)} custom-call(s32[3]{0:T(128)S(1)} %pad_add_fusion.seat, f32[32,16,128]{2,1,0:T(8,128)S(1)} %all_to_all.5.arrived, f32[1168,128]{1,0:T(8,128)S(1)} %get-tuple-element.51.mine, f32[1168,128]{1,0:T(8,128)S(1)} %collective-permute-done.18.other, f32[16,128]{1,0:T(8,128)S(1)} %multiply_bitcast_fusion.weights, ...), custom_call_target="tpu_custom_call" | custom-call | flops 4718592 | bytes 1572864 | tf_op jit(solution)/shard_map/pallas_call | solution.py:182
  (68 shorter events, 23.8 us)
Async XLA Ops:
  0.7 14.9 %collective-permute-start = (bf16[16,128]{1,0:T(8,128)(2,1)S(1)}, bf16[16,128]{1,0:T(8,128)(2,1)S(1)}, u32[]{:S(2)}, u32[]{:S(2)}) collective-permute-start(bf16[16,128]{1,0:T(8,128)(2,1)S(1)} %slice.15), channel_id=1, source_target_pairs={{0,32},{32,64},{64,96},{96,128},{128,160},{160,192},{192,224},{224... | collective-permute-start | bytes 12296 | tf_op jit(solution)/shard_map/ppermute | solution.py:239
  12.7 45.1 %copy-start = (bf16[3,4096,128]{2,1,0:T(8,128)(2,1)S(1)}, bf16[3,4096,128]{2,1,0:T(8,128)(2,1)}, u32[]{:S(2)}) copy-start(bf16[3,4096,128]{2,1,0:T(8,128)(2,1)} %refs_0_.7) | copy-start | bytes 9437188
  15.6 9.9 %copy-start.10 = (f32[128,16]{0,1:T(8,128)S(1)}, f32[128,16]{0,1:T(8,128)}, u32[]{:S(2)}) copy-start(f32[128,16]{0,1:T(8,128)} %param.11) | copy-start | bytes 24580
  15.6 9.9 %copy-start.14 = (f32[128,16]{0,1:T(8,128)S(1)}, f32[128,16]{0,1:T(8,128)}, u32[]{:S(2)}) copy-start(f32[128,16]{0,1:T(8,128)} %param.10) | copy-start | bytes 24580
  15.6 9.9 %copy-start.11 = (f32[3,7,128]{2,1,0:T(8,128)S(1)}, f32[3,7,128]{2,1,0:T(8,128)}, u32[]{:S(2)}) copy-start(f32[3,7,128]{2,1,0:T(8,128)} %taps.1) | copy-start | bytes 32260
  15.6 9.9 %copy-start.12 = (f32[128]{0:T(128)S(1)}, f32[128]{0:T(128)}, u32[]{:S(2)}) copy-start(f32[128]{0:T(128)} %param.12) | copy-start | bytes 1540
  16.4 9.1 %collective-permute-start.1 = (bf16[528,128]{1,0:T(8,128)(2,1)}, bf16[528,128]{1,0:T(8,128)(2,1)S(1)}, u32[]{:S(2)}, u32[]{:S(2)}) collective-permute-start(bf16[528,128]{1,0:T(8,128)(2,1)} %get-tuple-element.54), channel_id=1, source_target_pairs={{0,8},{1,9},{2,10},{3,11},{4,12},{5,13},{6,14},{7,15},{8,0},{9,1},... | collective-permute-start | bytes 405512 | tf_op jit(solution)/shard_map/ppermute | solution.py:207
  19.5 13.1 %collective-permute-start.4 = (bf16[528,128]{1,0:T(8,128)(2,1)}, bf16[528,128]{1,0:T(8,128)(2,1)}, u32[]{:S(2)}, u32[]{:S(2)}) collective-permute-start(bf16[528,128]{1,0:T(8,128)(2,1)} %get-tuple-element.54), channel_id=1, source_target_pairs={{0,24},{1,25},{2,26},{3,27},{4,28},{5,29},{6,30},{7,31},{8,16},{9,... | collective-permute-start | bytes 405512 | tf_op jit(solution)/shard_map/ppermute | solution.py:207
  23.5 9.1 %collective-permute-start.3 = (bf16[528,128]{1,0:T(8,128)(2,1)S(1)}, bf16[528,128]{1,0:T(8,128)(2,1)}, u32[]{:S(2)}, u32[]{:S(2)}) collective-permute-start(bf16[528,128]{1,0:T(8,128)(2,1)S(1)} %get-tuple-element.53), channel_id=1, source_target_pairs={{0,16},{1,17},{2,18},{3,19},{4,20},{5,21},{6,22},{7,23},{8,24},{9,... | collective-permute-start | bytes 405512 | tf_op jit(solution)/shard_map/ppermute | solution.py:207
  33.6 7.2 %collective-permute-start.5 = (bf16[528,512]{1,0:T(8,128)(2,1)S(1)}, bf16[528,512]{1,0:T(8,128)(2,1)S(1)}, u32[]{:S(2)}, u32[]{:S(2)}) collective-permute-start(bf16[528,512]{1,0:T(8,128)(2,1)S(1)} %pad_maximum_fusion.refs_1_.refs_2_), channel_id=1, source_target_pairs={{0,32},{32,0},{64,96},{96,64},{128,160},{160,128},{192,224},{224,1... | collective-permute-start | bytes 1622024 | tf_op jit(solution)/shard_map/ppermute | solution.py:221
  35.5 10.7 %collective-permute-start.7 = (bf16[528,512]{1,0:T(8,128)(2,1)S(1)}, bf16[528,512]{1,0:T(8,128)(2,1)}, u32[]{:S(2)}, u32[]{:S(2)}) collective-permute-start(bf16[528,512]{1,0:T(8,128)(2,1)S(1)} %pad_maximum_fusion.refs_1_.refs_2_), channel_id=1, source_target_pairs={{0,1},{1,2},{2,3},{3,4},{4,5},{5,6},{6,7},{7,0},{8,9},{9,10},{10,1... | collective-permute-start | bytes 1622024 | tf_op jit(solution)/shard_map/ppermute | solution.py:218
  40.8 11.3 %collective-permute-start.6 = (bf16[528,512]{1,0:T(8,128)(2,1)S(1)}, bf16[528,512]{1,0:T(8,128)(2,1)}, u32[]{:S(2)}, u32[]{:S(2)}) collective-permute-start(bf16[528,512]{1,0:T(8,128)(2,1)S(1)} %collective-permute-done.5), channel_id=1, source_target_pairs={{0,1},{1,2},{2,3},{3,4},{4,5},{5,6},{6,7},{7,0},{8,9},{9,10},{10,1... | collective-permute-start | bytes 1622024 | tf_op jit(solution)/shard_map/ppermute | solution.py:218
  43.7 38.3 %collective-permute-start.2 = (bf16[3,2048,128]{2,1,0:T(8,128)(2,1)}, bf16[3,2048,128]{2,1,0:T(8,128)(2,1)}, u32[]{:S(2)}, u32[]{:S(2)}) collective-permute-start(bf16[3,2048,128]{2,1,0:T(8,128)(2,1)} %constant_dynamic-slice_fusion.1), channel_id=1, source_target_pairs={{0,8},{1,9},{2,10},{3,11},{4,12},{5,13},{6,14},{7,15},{8,0},{9,1},... | collective-permute-start | bytes 4718600 | tf_op jit(solution)/shard_map/ppermute | solution.py:207
  46.2 15.6 %collective-permute-start.9 = (bf16[528,512]{1,0:T(8,128)(2,1)}, bf16[528,512]{1,0:T(8,128)(2,1)}, u32[]{:S(2)}, u32[]{:S(2)}) collective-permute-start(bf16[528,512]{1,0:T(8,128)(2,1)} %collective-permute-done.7.refs_1_.refs_3_), channel_id=1, source_target_pairs={{0,1},{1,2},{2,3},{3,4},{4,5},{5,6},{6,7},{7,0},{8,9},{9,10},{10,1... | collective-permute-start | bytes 1622024 | tf_op jit(solution)/shard_map/ppermute | solution.py:218
  52.0 13.8 %collective-permute-start.8 = (bf16[528,512]{1,0:T(8,128)(2,1)}, bf16[528,512]{1,0:T(8,128)(2,1)}, u32[]{:S(2)}, u32[]{:S(2)}) collective-permute-start(bf16[528,512]{1,0:T(8,128)(2,1)} %collective-permute-done.6), channel_id=1, source_target_pairs={{0,1},{1,2},{2,3},{3,4},{4,5},{5,6},{6,7},{7,0},{8,9},{9,10},{10,1... | collective-permute-start | bytes 1622024 | tf_op jit(solution)/shard_map/ppermute | solution.py:218
  59.9 11.1 %collective-permute-start.12 = (bf16[528,512]{1,0:T(8,128)(2,1)}, bf16[528,512]{1,0:T(8,128)(2,1)S(1)}, u32[]{:S(2)}, u32[]{:S(2)}) collective-permute-start(bf16[528,512]{1,0:T(8,128)(2,1)} %collective-permute-done.6), channel_id=1, source_target_pairs={{0,32},{32,0},{64,96},{96,64},{128,160},{160,128},{192,224},{224,1... | collective-permute-start | bytes 1622024 | tf_op jit(solution)/shard_map/ppermute | solution.py:221
  61.9 11.2 %collective-permute-start.11 = (bf16[528,512]{1,0:T(8,128)(2,1)}, bf16[528,512]{1,0:T(8,128)(2,1)}, u32[]{:S(2)}, u32[]{:S(2)}) collective-permute-start(bf16[528,512]{1,0:T(8,128)(2,1)} %collective-permute-done.9.refs_1_.refs_5_), channel_id=1, source_target_pairs={{0,1},{1,2},{2,3},{3,4},{4,5},{5,6},{6,7},{7,0},{8,9},{9,10},{10,1... | collective-permute-start | bytes 1622024 | tf_op jit(solution)/shard_map/ppermute | solution.py:218
  65.9 12.5 %collective-permute-start.10 = (bf16[528,512]{1,0:T(8,128)(2,1)}, bf16[528,512]{1,0:T(8,128)(2,1)}, u32[]{:S(2)}, u32[]{:S(2)}) collective-permute-start(bf16[528,512]{1,0:T(8,128)(2,1)} %collective-permute-done.8), channel_id=1, source_target_pairs={{0,1},{1,2},{2,3},{3,4},{4,5},{5,6},{6,7},{7,0},{8,9},{9,10},{10,1... | collective-permute-start | bytes 1622024 | tf_op jit(solution)/shard_map/ppermute | solution.py:218
  68.8 9.6 %collective-permute-start.13 = (bf16[528,512]{1,0:T(8,128)(2,1)}, bf16[528,512]{1,0:T(8,128)(2,1)S(1)}, u32[]{:S(2)}, u32[]{:S(2)}) collective-permute-start(bf16[528,512]{1,0:T(8,128)(2,1)} %collective-permute-done.8), channel_id=1, source_target_pairs={{0,32},{32,0},{64,96},{96,64},{128,160},{160,128},{192,224},{224,1... | collective-permute-start | bytes 1622024 | tf_op jit(solution)/shard_map/ppermute | solution.py:221
  82.1 13.0 %collective-permute-start.16 = (bf16[3,2048,128]{2,1,0:T(8,128)(2,1)}, bf16[3,2048,128]{2,1,0:T(8,128)(2,1)}, u32[]{:S(2)}, u32[]{:S(2)}) collective-permute-start(bf16[3,2048,128]{2,1,0:T(8,128)(2,1)} %collective-permute-done.2.refs_0_), channel_id=1, source_target_pairs={{0,32},{32,0},{64,96},{96,64},{128,160},{160,128},{192,224},{224,1... | collective-permute-start | bytes 4718600 | tf_op jit(solution)/shard_map/ppermute | solution.py:221
  85.8 16.3 %collective-permute-start.15 = (bf16[528,512]{1,0:T(8,128)(2,1)}, bf16[528,512]{1,0:T(8,128)(2,1)}, u32[]{:S(2)}, u32[]{:S(2)}) collective-permute-start(bf16[528,512]{1,0:T(8,128)(2,1)} %collective-permute-done.11.refs_2_.refs_1_), channel_id=1, source_target_pairs={{0,1},{1,2},{2,3},{3,4},{4,5},{5,6},{6,7},{7,0},{8,9},{9,10},{10,1... | collective-permute-start | bytes 1622024 | tf_op jit(solution)/shard_map/ppermute | solution.py:218
  88.1 13.9 %collective-permute-start.14 = (bf16[528,512]{1,0:T(8,128)(2,1)}, bf16[528,512]{1,0:T(8,128)(2,1)}, u32[]{:S(2)}, u32[]{:S(2)}) collective-permute-start(bf16[528,512]{1,0:T(8,128)(2,1)} %collective-permute-done.10), channel_id=1, source_target_pairs={{0,32},{32,0},{64,96},{96,64},{128,160},{160,128},{192,224},{224,1... | collective-permute-start | bytes 1622024 | tf_op jit(solution)/shard_map/ppermute | solution.py:221
  90.0 5.0 %collective-permute-start.17 = (f32[54,128]{1,0:T(8,128)S(1)}, f32[54,128]{1,0:T(8,128)S(1)}, u32[]{:S(2)}, u32[]{:S(2)}) collective-permute-start(f32[54,128]{1,0:T(8,128)S(1)} %pad_maximum_fusion.1), channel_id=1, source_target_pairs={{0,8},{1,9},{2,10},{3,11},{4,12},{5,13},{6,14},{7,15},{8,0},{9,1},... | collective-permute-start | bytes 82952 | tf_op jit(solution)/shard_map/ppermute | solution.py:207
  107.3 29.0 %collective-permute-start.18 = (f32[1168,128]{1,0:T(8,128)S(1)}, f32[1168,128]{1,0:T(8,128)S(1)}, u32[]{:S(2)}, u32[]{:S(2)}) collective-permute-start(f32[1168,128]{1,0:T(8,128)S(1)} %get-tuple-element.52), channel_id=1, source_target_pairs={{0,8},{1,9},{2,10},{3,11},{4,12},{5,13},{6,14},{7,15},{8,0},{9,1},... | collective-permute-start | bytes 1794056 | tf_op jit(solution)/shard_map/ppermute | solution.py:207
  (10 other events, 20.1 us)

commit v5 on v4

--- a/solution.py
+++ b/solution.py
@@ -18,37 +18,69 @@
 LINES = 4
 SMEM = pl.BlockSpec(memory_space=pltpu.SMEM)
 VMEM = pl.BlockSpec(memory_space=pltpu.VMEM)
+ANY = pl.BlockSpec(memory_space=pl.ANY)
+
+
+def after(value, earlier):
+    return lax.optimization_barrier((value, earlier))[0]
 
 
 def wide(row):
     return jnp.broadcast_to(row, (CHUNKS, LANES))
 
 
-def met_rows(weights, s, at):
-    count = weights[0].shape[1] // LANES
-    parts = [
-        w[s, pl.ds(pl.multiple_of(jnp.clip(at - i * count, 0, count - 1) * LANES, LANES), LANES), :]
-        for i, w in enumerate(weights)
-    ]
-    return parts[0] if len(parts) == 1 else jnp.where(at < count, parts[0], parts[1])
-
-
-def products(blocks, ids, at, weights):
+def fetch(count, at, ids, weights, blocks, block_buf, weight_buf, sems):
+    pending = []
+    for b in range(count):
+        here = [pltpu.make_async_copy(blocks[b], block_buf.at[b], sems.at[b, 0])]
+        here[0].start()
+        for k in range(LINES):
+            row = ids[LINES * (at + b) + k]
+            for s in range(3):
+                target = weight_buf.at[b, k * LANES : (k + 1) * LANES, s * LANES : (s + 1) * LANES]
+                sem = sems.at[b, 1 + 3 * k + s]
+                most = weights[0].shape[1] // LANES
+                copies = [
+                    pltpu.make_async_copy(
+                        w.at[s, pl.ds(pl.multiple_of(jnp.clip(row - i * most, 0, most - 1) * LANES, LANES), LANES), :],
+                        target, sem,
+                    )
+                    for i, w in enumerate(weights)
+                ]
+                if len(copies) == 1:
+                    copies[0].start()
+                else:
+                    pl.when(row < most)(copies[0].start)
+                    pl.when(row >= most)(copies[1].start)
+                here.append(copies[0])
+        pending.append(here)
+    return pending
+
+
+def products(pending, block_buf, weight_buf):
     total = None
-    for b, block in enumerate(blocks):
-        rows = [ids[LINES * (at + b) + k] for k in range(LINES)]
-        met = jnp.concatenate(
-            [jnp.concatenate([met_rows(weights, s, r) for s in range(3)], axis=1) for r in rows], axis=0
-        )
-        part = jnp.dot(block[...], met, preferred_element_type=jnp.float32)
+    for b, copies in enumerate(pending):
+        for copy in copies:
+            copy.wait()
+        part = jnp.dot(block_buf[b], weight_buf[b], preferred_element_type=jnp.float32)
         total = part if total is None else total + part
     return [total[:, s * LANES : (s + 1) * LANES] for s in range(3)]
 
 
+def buffers(blocks):
+    count, (rows, depth) = len(blocks), blocks[0].shape
+    return [
+        pltpu.VMEM((count, rows, depth), jnp.bfloat16),
+        pltpu.VMEM((count, depth, 3 * LANES), jnp.bfloat16),
+        pltpu.SemaphoreType.DMA((count, 1 + 3 * LINES)),
+    ]
+
+
 def project_kernel(count, kinds, at, ids, *refs):
-    weights, refs = refs[:kinds], refs[kinds:]
-    blocks, sums, out = refs[:count], refs[count:-1], refs[-1]
-    for s, part in enumerate(products(blocks, ids, at, weights)):
+    weights, blocks, refs = refs[:kinds], refs[kinds : kinds + count], refs[kinds + count :]
+    sums, out, (block_buf, weight_buf, sems) = refs[:-4], refs[-4], refs[-3:]
+    pending = fetch(count, at, ids, weights, blocks, block_buf, weight_buf, sems)
+    for s, part in enumerate(products(pending, block_buf, weight_buf)):
         out[s] = sums[0][s] + part if sums else part
 
 
@@ -57,8 +89,9 @@
     rows = blocks[0].shape[0]
     return pl.pallas_call(
         functools.partial(project_kernel, len(blocks), len(in_weights), at),
-        in_specs=[SMEM] + [VMEM] * (len(in_weights) + len(blocks) + len(extra)),
+        in_specs=[SMEM] + [ANY] * (len(in_weights) + len(blocks)) + [VMEM] * len(extra),
         out_specs=VMEM,
+        scratch_shapes=buffers(blocks),
         out_shape=jax.ShapeDtypeStruct((3, rows, LANES), jnp.float32),
         input_output_aliases={1 + len(in_weights) + len(blocks): 0} if extra else {},
         compiler_params=pltpu.CompilerParams(vmem_limit_bytes=16 * 2**20),
@@ -67,11 +100,19 @@
 
 
 def local_kernel(count, kinds, at, seat, ids, sums, taps, weights, decays, skip, *refs):
-    in_weights, blocks, (pack, sent, proj, ends) = refs[:kinds], refs[kinds : kinds + count], refs[-4:]
-    rows = proj.shape[1] - HALO
+    in_weights, blocks = refs[:kinds], refs[kinds : kinds + count]
+    pack, sent, proj, ends, block_buf, weight_buf, sems = refs[-7:]
+    pending = fetch(count, at, ids, in_weights, blocks, block_buf, weight_buf, sems)
+    rows = sums.shape[1] - HALO
     length = rows // CHUNKS
-    for s, part in enumerate(products(blocks, ids, at, in_weights)):
-        proj[s] = sums[s] + part
+    early = TAPS - 1
+    top = lax.broadcasted_iota(jnp.int32, (CHUNKS, LANES), 0) == 0
+    for s, part in enumerate(products(pending, block_buf, weight_buf)):
+        proj[s, early * CHUNKS :, :] = sums[s, HALO:, :] + part[HALO:]
+        halo = sums[s, :HALO, :] + part[:HALO]
+        for p in range(early):
+            end = pltpu.roll(proj[s, (length + p) * CHUNKS : (length + p + 1) * CHUNKS, :], 1, 0)
+            proj[s, p * CHUNKS : (p + 1) * CHUNKS, :] = jnp.where(top, wide(halo[HALO - early + p : HALO - early + p + 1]), end)
     poles = [wide(jnp.exp(-decays[m : m + 1, :])) for m in range(MODES)]
     gains = [wide(weights[m : m + 1, :]) for m in range(MODES)]
     skip_row = wide(skip[0:1, :])
@@ -81,7 +122,7 @@
         at = at * UNROLL
         taken = [
             [
-                proj[s, pl.ds(at + HALO - (TAPS - 1) + k, CHUNKS, stride=length), :]
+                proj[s, pl.ds(pl.multiple_of((at + k) * CHUNKS, CHUNKS), CHUNKS), :]
                 for k in range(UNROLL + TAPS - 1)
             ]
             for s in range(3)
@@ -121,7 +162,7 @@
     extra = [] if sent is None else [sent]
     return pl.pallas_call(
         functools.partial(local_kernel, len(blocks), len(in_weights), at),
-        in_specs=[SMEM] * 2 + [VMEM] * (5 + len(in_weights) + len(blocks) + len(extra)),
+        in_specs=[SMEM] * 2 + [VMEM] * 5 + [ANY] * (len(in_weights) + len(blocks)) + [VMEM] * len(extra),
         out_specs=[VMEM] * 2,
         out_shape=[
             jax.ShapeDtypeStruct((2 * rows + (CHUNKS + 1) * MODES, LANES), jnp.float32),
@@ -129,9 +170,10 @@
         ],
         input_output_aliases={7 + len(in_weights) + len(blocks): 1} if extra else {},
         scratch_shapes=[
-            pltpu.VMEM(sums.shape, jnp.float32),
+            pltpu.VMEM((3, rows + (TAPS - 1) * CHUNKS, LANES), jnp.float32),
             pltpu.VMEM((MODES * CHUNKS, LANES), jnp.float32),
-        ],
+        ]
+        + buffers(blocks),
         compiler_params=pltpu.CompilerParams(vmem_limit_bytes=16 * 2**20),
         cost_estimate=pl.CostEstimate(
             flops=rows * LANES * 110, bytes_accessed=rows * LANES * 20, transcendentals=0
@@ -236,16 +278,19 @@
     seat = jnp.stack([mine, half, half]).astype(jnp.int32)
     other_seat = jnp.stack([mine, half, 1 - half]).astype(jnp.int32)
 
+    values = jnp.concatenate([short_taps.reshape(3 * TAPS, -1), weights, rates, skip_gain[None, :]], axis=0)
+    values = beside(values, 1)
     before = lax.ppermute(tokens[rows - HALO :], "ctx", [(i, i + 1) for i in range(blocks - 1)])
-    padded = jnp.concatenate([before, tokens], axis=0)
-    kept = lax.dynamic_slice_in_dim(padded, half * part, part + HALO, 0)
-    given = lax.dynamic_slice_in_dim(padded, (1 - half) * part, part + HALO, 0)
+    ordered = tokens.reshape(2, CHUNKS, part // CHUNKS, -1).swapaxes(1, 2).reshape(2, part, -1)
+    before = after(before, values)
+    between = tokens[part - HALO : part]
+    low = half == 0
+    kept = jnp.concatenate([jnp.where(low, before, between), jnp.where(low, ordered[0], ordered[1])], axis=0)
+    given = jnp.concatenate([jnp.where(low, between, before), jnp.where(low, ordered[1], ordered[0])], axis=0)
     nearest = beside(given, 1)
     count = in_weights.shape[1] // 2
     half_weights = lax.dynamic_slice_in_dim(in_weights, mine % 2 * count, count, 1)
-    values = jnp.concatenate([short_taps.reshape(3 * TAPS, -1), weights, rates, skip_gain[None, :]], axis=0)
-    nearest, half_weights, values = lax.optimization_barrier((nearest, half_weights, values))
-    half_weights, values = beside(half_weights, 1), beside(values, 1)
+    half_weights = beside(after(half_weights, nearest), 1)
     block = jnp.concatenate([kept, nearest, beside(kept, 2), beside(given, 3)], axis=1)
 
     straight, turned = onward(block), other_core(block)
@@ -268,7 +313,7 @@
         waiting = [here, swapped]
         if step < ring // 2 - 1:
             straight, sums = lax.optimization_barrier((straight, sums))
-    half_weights, sums = lax.optimization_barrier((half_weights, sums))
+    half_weights = after(half_weights, sums)
     their_weights = [half_weights, other_core(half_weights)]
     theirs = project(None, arrived[:met], ids, ring, their_weights)
     waiting.append(straight)

time: 140 us -> 142 us (1.014)
  waiting for transfers between devices: 17.4 us -> 12 us
  blocking collectives: 22.8 us -> 26 us
  Pallas kernels: 20.4 us -> 23.1 us
  other arithmetic: 1.21 us -> 3.22 us
  local copies, waits for them, and re-layouts: 10.9 us -> 8.91 us
    ppermute x6, waiting for transfers between devices: 10.9 us -> 6.24 us  [beside(): lax.ppermute(block, 'ch', [(z * ring + y, (z ^ step) * ring + y) for z in...]
    ppermute x6, starting transfers between devices: 14.8 us -> 19.4 us  [beside(): lax.ppermute(block, 'ch', [(z * ring + y, (z ^ step) * ring + y) for z in...]
    all_to_all x1, blocking collectives: 22.8 us -> 26 us  [per_device(): lax.all_to_all(sent.reshape(2 * blocks, MODES, LANES), ('ctx', 'ch'), 0,...]
    pallas_call x4, Pallas kernels: 8.76 us -> 11.8 us  [project(): pl.pallas_call(functools.partial(project_kernel, len(blocks), len(in_weig...]
    unnamed x31 -> x20, local copies, waits for them, and re-layouts: 5.91 us -> 3.01 us
    ppermute x1, starting transfers between devices: 12 us -> 10.6 us  [per_device(): lax.ppermute(tokens[rows - HALO:], 'ctx', [(i, i + 1) for i in range(bloc...]
  transfers between devices with their start and end apart: 19 -> 19, of which waited for: 6 -> 6; matrix products, arithmetic and copies ran while one was open for 3% -> 4% of each run, Pallas kernels for 9% -> 12%
where the time goes in v5:
time: 142 us; the launch traced here: 140 us
  starting transfers between devices  66.7 us (47%)
  blocking collectives  26 us (18%)
  Pallas kernels  23.1 us (16%)
  waiting for transfers between devices  12 us (8%)
  local copies, waits for them, and re-layouts  8.91 us (6%)
  other arithmetic  3.22 us (2%)
    ppermute x7, starting transfers between devices, onward(): return lax.ppermute(block, ('ctx', 'ch'), route)  26.2 us
    all_to_all x1, blocking collectives, per_device(): lax.all_to_all(sent.reshape(2 * blocks, MODES, LANES), ('ctx', 'ch'), 0,...  26 us
    ppermute x6, starting transfers between devices, beside(): lax.ppermute(block, 'ch', [(z * ring + y, (z ^ step) * ring + y) for z in...  19.4 us
    pallas_call x4, Pallas kernels, project(): pl.pallas_call(functools.partial(project_kernel, len(blocks), len(in_weig...  11.8 us
    ppermute x5, starting transfers between devices, other_core(): return lax.ppermute(block, 'ctx', [(i, i ^ 1) for i in range(blocks)])  10.6 us
    ppermute x1, starting transfers between devices, per_device(): lax.ppermute(tokens[rows - HALO:], 'ctx', [(i, i + 1) for i in range(bloc...  10.6 us
    pallas_call x2, Pallas kernels, local_part(): pl.pallas_call(functools.partial(local_kernel, len(blocks), len(in_weight...  9.19 us
    ppermute x6, waiting for transfers between devices, beside(): lax.ppermute(block, 'ch', [(z * ring + y, (z ^ step) * ring + y) for z in...  6.24 us
  transfers between devices with their start and end apart: 19, of which 6 were waited for; matrix products, arithmetic and copies ran while one was open for 4% of the time, Pallas kernels for 12%

profile of v5, /device:TPU:1, one launch (start us, length us, event | category | flops | bytes accessed | tf_op | source)
XLA Modules:
  0.0 140.4 jit_solution(15383861677271395825)
XLA Ops:
  2.2 4.8 %collective-permute-start.1 = (f32[54,128]{1,0:T(8,128)S(1)}, f32[54,128]{1,0:T(8,128)S(1)}, u32[]{:S(2)}, u32[]{:S(2)}) collective-permute-start(f32[54,128]{1,0:T(8,128)S(1)} %pad_maximum_fusion.3), channel_id=1, source_target_pairs={{0,8},{1,9},{2,10},{3,11},{4,12},{5,13},{6,14},{7,15},{8,0},{9,1},... | collective-permute-start | bytes 82952 | tf_op jit(solution)/shard_map/ppermute | solution.py:249
  7.7 10.6 %collective-permute-start = (bf16[16,128]{1,0:T(8,128)(2,1)S(1)}, bf16[16,128]{1,0:T(8,128)(2,1)S(1)}, u32[]{:S(2)}, u32[]{:S(2)}) collective-permute-start(bf16[16,128]{1,0:T(8,128)(2,1)S(1)} %slice.28), channel_id=1, source_target_pairs={{0,32},{32,64},{64,96},{96,128},{128,160},{160,192},{192,224},{224... | collective-permute-start | bytes 12296 | tf_op jit(solution)/shard_map/ppermute | solution.py:283
  20.2 4.0 %collective-permute-start.3 = (bf16[528,128]{1,0:T(8,128)(2,1)S(1)}, bf16[528,128]{1,0:T(8,128)(2,1)S(1)}, u32[]{:S(2)}, u32[]{:S(2)}) collective-permute-start(bf16[528,128]{1,0:T(8,128)(2,1)S(1)} %pad_maximum_fusion.1), channel_id=1, source_target_pairs={{0,16},{1,17},{2,18},{3,19},{4,20},{5,21},{6,22},{7,23},{8,24},{9,... | collective-permute-start | bytes 405512 | tf_op jit(solution)/shard_map/ppermute | solution.py:249
  24.2 2.2 %collective-permute-start.2 = (bf16[528,128]{1,0:T(8,128)(2,1)S(1)}, bf16[528,128]{1,0:T(8,128)(2,1)S(1)}, u32[]{:S(2)}, u32[]{:S(2)}) collective-permute-start(bf16[528,128]{1,0:T(8,128)(2,1)S(1)} %pad_maximum_fusion.2), channel_id=1, source_target_pairs={{0,8},{1,9},{2,10},{3,11},{4,12},{5,13},{6,14},{7,15},{8,0},{9,1},... | collective-permute-start | bytes 405512 | tf_op jit(solution)/shard_map/ppermute | solution.py:249
  26.4 3.1 %collective-permute-start.4 = (bf16[528,128]{1,0:T(8,128)(2,1)S(1)}, bf16[528,128]{1,0:T(8,128)(2,1)S(1)}, u32[]{:S(2)}, u32[]{:S(2)}) collective-permute-start(bf16[528,128]{1,0:T(8,128)(2,1)S(1)} %pad_maximum_fusion.2), channel_id=1, source_target_pairs={{0,24},{1,25},{2,26},{3,27},{4,28},{5,29},{6,30},{7,31},{8,16},{9,... | collective-permute-start | bytes 405512 | tf_op jit(solution)/shard_map/ppermute | solution.py:249
  31.2 2.8 %collective-permute-done.4 = bf16[528,128]{1,0:T(8,128)(2,1)S(1)} collective-permute-done((bf16[528,128]{1,0:T(8,128)(2,1)S(1)}, bf16[528,128]{1,0:T(8,128)(2,1)S(1)}, u32[]{:S(2)}, u32[]{:S(2)}) %collective-permute-start.4) | collective-permute-done | bytes 135200 | tf_op jit(solution)/shard_map/ppermute | solution.py:249
  36.9 5.4 %collective-permute-start.7 = (bf16[528,512]{1,0:T(8,128)(2,1)}, bf16[528,512]{1,0:T(8,128)(2,1)}, u32[]{:S(2)}, u32[]{:S(2)}) collective-permute-start(bf16[528,512]{1,0:T(8,128)(2,1)} %pad_maximum_fusion.refs_1_.refs_2_), channel_id=1, source_target_pairs={{0,1},{1,2},{2,3},{3,4},{4,5},{5,6},{6,7},{7,0},{8,9},{9,10},{10,1... | collective-permute-start | bytes 1622024 | tf_op jit(solution)/shard_map/ppermute | solution.py:260
  42.3 3.0 %collective-permute-start.6 = (bf16[528,512]{1,0:T(8,128)(2,1)}, bf16[528,512]{1,0:T(8,128)(2,1)}, u32[]{:S(2)}, u32[]{:S(2)}) collective-permute-start(bf16[528,512]{1,0:T(8,128)(2,1)} %collective-permute-done.5), channel_id=1, source_target_pairs={{0,1},{1,2},{2,3},{3,4},{4,5},{5,6},{6,7},{7,0},{8,9},{9,10},{10,1... | collective-permute-start | bytes 1622024 | tf_op jit(solution)/shard_map/ppermute | solution.py:260
  45.2 2.7 %constant_dynamic-slice_fusion = bf16[3,2048,128]{2,1,0:T(8,128)(2,1)} fusion(bf16[3,4096,128]{2,1,0:T(8,128)(2,1)} %refs_0_.7, s32[]{:T(128)S(6)} %select_n.64), kind=kLoop, calls=%fused_computation.14 | loop fusion | bytes 3145732 | tf_op jit(solution)/shard_map/dynamic_slice | solution.py:292
  47.9 2.6 %collective-permute-start.16 = (bf16[3,2048,128]{2,1,0:T(8,128)(2,1)}, bf16[3,2048,128]{2,1,0:T(8,128)(2,1)}, u32[]{:S(2)}, u32[]{:S(2)}) collective-permute-start(bf16[3,2048,128]{2,1,0:T(8,128)(2,1)} %constant_dynamic-slice_fusion), channel_id=1, source_target_pairs={{0,8},{1,9},{2,10},{3,11},{4,12},{5,13},{6,14},{7,15},{8,0},{9,1},... | collective-permute-start | bytes 4718600 | tf_op jit(solution)/shard_map/ppermute | solution.py:249
  50.6 3.3 %collective-permute-start.9 = (bf16[528,512]{1,0:T(8,128)(2,1)}, bf16[528,512]{1,0:T(8,128)(2,1)}, u32[]{:S(2)}, u32[]{:S(2)}) collective-permute-start(bf16[528,512]{1,0:T(8,128)(2,1)} %collective-permute-done.7.refs_1_.refs_3_), channel_id=1, source_target_pairs={{0,1},{1,2},{2,3},{3,4},{4,5},{5,6},{6,7},{7,0},{8,9},{9,10},{10,1... | collective-permute-start | bytes 1622024 | tf_op jit(solution)/shard_map/ppermute | solution.py:260
  54.6 5.0 %collective-permute-start.8 = (bf16[528,512]{1,0:T(8,128)(2,1)}, bf16[528,512]{1,0:T(8,128)(2,1)}, u32[]{:S(2)}, u32[]{:S(2)}) collective-permute-start(bf16[528,512]{1,0:T(8,128)(2,1)} %collective-permute-done.6), channel_id=1, source_target_pairs={{0,1},{1,2},{2,3},{3,4},{4,5},{5,6},{6,7},{7,0},{8,9},{9,10},{10,1... | collective-permute-start | bytes 1622024 | tf_op jit(solution)/shard_map/ppermute | solution.py:260
  64.5 3.6 %collective-permute-start.11 = (bf16[528,512]{1,0:T(8,128)(2,1)}, bf16[528,512]{1,0:T(8,128)(2,1)}, u32[]{:S(2)}, u32[]{:S(2)}) collective-permute-start(bf16[528,512]{1,0:T(8,128)(2,1)} %collective-permute-done.9.refs_1_.refs_5_), channel_id=1, source_target_pairs={{0,1},{1,2},{2,3},{3,4},{4,5},{5,6},{6,7},{7,0},{8,9},{9,10},{10,1... | collective-permute-start | bytes 1622024 | tf_op jit(solution)/shard_map/ppermute | solution.py:260
  68.1 3.2 %collective-permute-start.10 = (bf16[528,512]{1,0:T(8,128)(2,1)}, bf16[528,512]{1,0:T(8,128)(2,1)}, u32[]{:S(2)}, u32[]{:S(2)}) collective-permute-start(bf16[528,512]{1,0:T(8,128)(2,1)} %collective-permute-done.8), channel_id=1, source_target_pairs={{0,1},{1,2},{2,3},{3,4},{4,5},{5,6},{6,7},{7,0},{8,9},{9,10},{10,1... | collective-permute-start | bytes 1622024 | tf_op jit(solution)/shard_map/ppermute | solution.py:260
  73.3 2.7 %shard_map.74.refs_3_ = f32[3,528,128]{2,1,0:T(8,128)S(1)} custom-call(s32[64]{0:T(128)S(1)} %dynamic-slice_bitcast_fusion.ids, bf16[3,4096,128]{2,1,0:T(8,128)(2,1)S(1)} %copy-done, bf16[528,512]{1,0:T(8,128)(2,1)} %collective-permute-done.7.refs_1_.refs_3_, ...), custom_call_target="tpu_custom_call", output_to_operand_aliasing={{}: (4, {})} | custom-call | flops 528 | bytes 528 | tf_op jit(solution)/shard_map/pallas_call | solution.py:90
  76.0 5.0 %collective-permute-done.10 = bf16[528,512]{1,0:T(8,128)(2,1)} collective-permute-done((bf16[528,512]{1,0:T(8,128)(2,1)}, bf16[528,512]{1,0:T(8,128)(2,1)}, u32[]{:S(2)}, u32[]{:S(2)}) %collective-permute-start.10) | collective-permute-done | bytes 540704 | tf_op jit(solution)/shard_map/ppermute | solution.py:260
  81.0 2.7 %shard_map.75.sums = f32[3,528,128]{2,1,0:T(8,128)S(1)} custom-call(s32[64]{0:T(128)S(1)} %dynamic-slice_bitcast_fusion.ids, bf16[3,4096,128]{2,1,0:T(8,128)(2,1)S(1)} %copy-done, bf16[528,512]{1,0:T(8,128)(2,1)} %collective-permute-done.9.refs_1_.refs_5_, ...), custom_call_target="tpu_custom_call", output_to_operand_aliasing={{}: (4, {})} | custom-call | flops 528 | bytes 528 | tf_op jit(solution)/shard_map/pallas_call | solution.py:90
  86.2 2.8 %collective-permute-start.17 = (bf16[3,2048,128]{2,1,0:T(8,128)(2,1)}, bf16[3,2048,128]{2,1,0:T(8,128)(2,1)}, u32[]{:S(2)}, u32[]{:S(2)}) collective-permute-start(bf16[3,2048,128]{2,1,0:T(8,128)(2,1)} %collective-permute-done.16.refs_0_), channel_id=1, source_target_pairs={{0,32},{32,0},{64,96},{96,64},{128,160},{160,128},{192,224},{224,1... | collective-permute-start | bytes 4718600 | tf_op jit(solution)/shard_map/ppermute | solution.py:263
  89.0 2.8 %collective-permute-start.15 = (bf16[528,512]{1,0:T(8,128)(2,1)}, bf16[528,512]{1,0:T(8,128)(2,1)}, u32[]{:S(2)}, u32[]{:S(2)}) collective-permute-start(bf16[528,512]{1,0:T(8,128)(2,1)} %collective-permute-done.11.refs_2_.refs_1_), channel_id=1, source_target_pairs={{0,1},{1,2},{2,3},{3,4},{4,5},{5,6},{6,7},{7,0},{8,9},{9,10},{10,1... | collective-permute-start | bytes 1622024 | tf_op jit(solution)/shard_map/ppermute | solution.py:260
  95.9 4.3 %shard_map.76.sums = f32[3,528,128]{2,1,0:T(8,128)S(1)} custom-call(s32[64]{0:T(128)S(1)} %dynamic-slice_bitcast_fusion.ids, bf16[3,2048,128]{2,1,0:T(8,128)(2,1)} %collective-permute-done.16.refs_0_, bf16[3,2048,128]{2,1,0:T(8,128)(2,1)} %collective-permute-done.17.refs_1_, bf16[528,512]{1,0:T(8,128)(2,1)} %pad_maximum_fusion.refs_1_.refs_2_, ...), custom_call_target="tpu_custom_call" | custom-call | flops 528 | bytes 528 | tf_op jit(solution)/shard_map/pallas_call | solution.py:90
  100.3 4.7 %shard_map.77 = (f32[1168,128]{1,0:T(8,128)S(1)}, f32[2,16,16,128]{3,2,1,0:T(8,128)S(1)}) custom-call(s32[3]{0:T(128)S(1)} %pad_add_fusion.2.seat, s32[64]{0:T(128)S(1)} %dynamic-slice_bitcast_fusion.ids, f32[3,528,128]{2,1,0:T(8,128)S(1)} %shard_map.76.sums, f32[3,7,128]{2,1,0:T(8,128)S(1)} %reshape.23.taps, f32[16,128]{1,0:T(8,128)S(1)} %get-tuple-element.54.weights, ...), custom_call_target="tpu_custom_call" | custom-call | flops 7208960 | bytes 1310720 | tf_op jit(solution)/shard_map/pallas_call | solution.py:163
  105.0 2.7 %collective-permute-start.18 = (f32[1168,128]{1,0:T(8,128)S(1)}, f32[1168,128]{1,0:T(8,128)S(1)}, u32[]{:S(2)}, u32[]{:S(2)}) collective-permute-start(f32[1168,128]{1,0:T(8,128)S(1)} %get-tuple-element.48), channel_id=1, source_target_pairs={{0,8},{1,9},{2,10},{3,11},{4,12},{5,13},{6,14},{7,15},{8,0},{9,1},... | collective-permute-start | bytes 1794056 | tf_op jit(solution)/shard_map/ppermute | solution.py:249
  107.8 4.5 %shard_map.78 = (f32[1168,128]{1,0:T(8,128)S(1)}, f32[2,16,16,128]{3,2,1,0:T(8,128)S(1)}) custom-call(s32[3]{0:T(128)S(1)} %pad_add_fusion.seat, s32[64]{0:T(128)S(1)} %dynamic-slice_bitcast_fusion.ids, f32[3,528,128]{2,1,0:T(8,128)S(1)} %copy-done.2, f32[3,7,128]{2,1,0:T(8,128)S(1)} %copy-done.8, ...), custom_call_target="tpu_custom_call", output_to_operand_aliasing={{1}: (11, {})} | custom-call | flops 7208960 | bytes 1310720 | tf_op jit(solution)/shard_map/pallas_call | solution.py:163
  112.3 26.0 %all_to_all.5.arrived = f32[32,16,128]{2,1,0:T(8,128)S(1)} all-to-all(f32[32,16,128]{2,1,0:T(8,128)S(1)} %bitcast.18), channel_id=1, replica_groups={{0,32,64,96,128,160,192,224,256,288,320,352,384,416,448,480,8,40,72,104..., dimensions={0} | all-to-all | bytes 524288 | tf_op jit(solution)/shard_map/all_to_all | solution.py:338
  (60 shorter events, 25.7 us)
Async XLA Ops:
  2.2 17.3 %collective-permute-start.1 = (f32[54,128]{1,0:T(8,128)S(1)}, f32[54,128]{1,0:T(8,128)S(1)}, u32[]{:S(2)}, u32[]{:S(2)}) collective-permute-start(f32[54,128]{1,0:T(8,128)S(1)} %pad_maximum_fusion.3), channel_id=1, source_target_pairs={{0,8},{1,9},{2,10},{3,11},{4,12},{5,13},{6,14},{7,15},{8,0},{9,1},... | collective-permute-start | bytes 82952 | tf_op jit(solution)/shard_map/ppermute | solution.py:249
  7.7 11.8 %collective-permute-start = (bf16[16,128]{1,0:T(8,128)(2,1)S(1)}, bf16[16,128]{1,0:T(8,128)(2,1)S(1)}, u32[]{:S(2)}, u32[]{:S(2)}) collective-permute-start(bf16[16,128]{1,0:T(8,128)(2,1)S(1)} %slice.28), channel_id=1, source_target_pairs={{0,32},{32,64},{64,96},{96,128},{128,160},{160,192},{192,224},{224... | collective-permute-start | bytes 12296 | tf_op jit(solution)/shard_map/ppermute | solution.py:283
  20.2 10.5 %collective-permute-start.3 = (bf16[528,128]{1,0:T(8,128)(2,1)S(1)}, bf16[528,128]{1,0:T(8,128)(2,1)S(1)}, u32[]{:S(2)}, u32[]{:S(2)}) collective-permute-start(bf16[528,128]{1,0:T(8,128)(2,1)S(1)} %pad_maximum_fusion.1), channel_id=1, source_target_pairs={{0,16},{1,17},{2,18},{3,19},{4,20},{5,21},{6,22},{7,23},{8,24},{9,... | collective-permute-start | bytes 405512 | tf_op jit(solution)/shard_map/ppermute | solution.py:249
  24.2 7.0 %collective-permute-start.2 = (bf16[528,128]{1,0:T(8,128)(2,1)S(1)}, bf16[528,128]{1,0:T(8,128)(2,1)S(1)}, u32[]{:S(2)}, u32[]{:S(2)}) collective-permute-start(bf16[528,128]{1,0:T(8,128)(2,1)S(1)} %pad_maximum_fusion.2), channel_id=1, source_target_pairs={{0,8},{1,9},{2,10},{3,11},{4,12},{5,13},{6,14},{7,15},{8,0},{9,1},... | collective-permute-start | bytes 405512 | tf_op jit(solution)/shard_map/ppermute | solution.py:249
  26.4 7.7 %collective-permute-start.4 = (bf16[528,128]{1,0:T(8,128)(2,1)S(1)}, bf16[528,128]{1,0:T(8,128)(2,1)S(1)}, u32[]{:S(2)}, u32[]{:S(2)}) collective-permute-start(bf16[528,128]{1,0:T(8,128)(2,1)S(1)} %pad_maximum_fusion.2), channel_id=1, source_target_pairs={{0,24},{1,25},{2,26},{3,27},{4,28},{5,29},{6,30},{7,31},{8,16},{9,... | collective-permute-start | bytes 405512 | tf_op jit(solution)/shard_map/ppermute | solution.py:249
  34.9 7.3 %collective-permute-start.5 = (bf16[528,512]{1,0:T(8,128)(2,1)}, bf16[528,512]{1,0:T(8,128)(2,1)}, u32[]{:S(2)}, u32[]{:S(2)}) collective-permute-start(bf16[528,512]{1,0:T(8,128)(2,1)} %pad_maximum_fusion.refs_1_.refs_2_), channel_id=1, source_target_pairs={{0,32},{32,0},{64,96},{96,64},{128,160},{160,128},{192,224},{224,1... | collective-permute-start | bytes 1622024 | tf_op jit(solution)/shard_map/ppermute | solution.py:263
  36.9 23.5 %copy-start = (bf16[3,4096,128]{2,1,0:T(8,128)(2,1)S(1)}, bf16[3,4096,128]{2,1,0:T(8,128)(2,1)}, u32[]{:S(2)}) copy-start(bf16[3,4096,128]{2,1,0:T(8,128)(2,1)} %refs_0_.7) | copy-start | bytes 9437188
  36.9 13.7 %collective-permute-start.7 = (bf16[528,512]{1,0:T(8,128)(2,1)}, bf16[528,512]{1,0:T(8,128)(2,1)}, u32[]{:S(2)}, u32[]{:S(2)}) collective-permute-start(bf16[528,512]{1,0:T(8,128)(2,1)} %pad_maximum_fusion.refs_1_.refs_2_), channel_id=1, source_target_pairs={{0,1},{1,2},{2,3},{3,4},{4,5},{5,6},{6,7},{7,0},{8,9},{9,10},{10,1... | collective-permute-start | bytes 1622024 | tf_op jit(solution)/shard_map/ppermute | solution.py:260
  42.3 12.4 %collective-permute-start.6 = (bf16[528,512]{1,0:T(8,128)(2,1)}, bf16[528,512]{1,0:T(8,128)(2,1)}, u32[]{:S(2)}, u32[]{:S(2)}) collective-permute-start(bf16[528,512]{1,0:T(8,128)(2,1)} %collective-permute-done.5), channel_id=1, source_target_pairs={{0,1},{1,2},{2,3},{3,4},{4,5},{5,6},{6,7},{7,0},{8,9},{9,10},{10,1... | collective-permute-start | bytes 1622024 | tf_op jit(solution)/shard_map/ppermute | solution.py:260
  47.9 38.3 %collective-permute-start.16 = (bf16[3,2048,128]{2,1,0:T(8,128)(2,1)}, bf16[3,2048,128]{2,1,0:T(8,128)(2,1)}, u32[]{:S(2)}, u32[]{:S(2)}) collective-permute-start(bf16[3,2048,128]{2,1,0:T(8,128)(2,1)} %constant_dynamic-slice_fusion), channel_id=1, source_target_pairs={{0,8},{1,9},{2,10},{3,11},{4,12},{5,13},{6,14},{7,15},{8,0},{9,1},... | collective-permute-start | bytes 4718600 | tf_op jit(solution)/shard_map/ppermute | solution.py:249
  50.6 13.9 %collective-permute-start.9 = (bf16[528,512]{1,0:T(8,128)(2,1)}, bf16[528,512]{1,0:T(8,128)(2,1)}, u32[]{:S(2)}, u32[]{:S(2)}) collective-permute-start(bf16[528,512]{1,0:T(8,128)(2,1)} %collective-permute-done.7.refs_1_.refs_3_), channel_id=1, source_target_pairs={{0,1},{1,2},{2,3},{3,4},{4,5},{5,6},{6,7},{7,0},{8,9},{9,10},{10,1... | collective-permute-start | bytes 1622024 | tf_op jit(solution)/shard_map/ppermute | solution.py:260
  54.6 13.4 %collective-permute-start.8 = (bf16[528,512]{1,0:T(8,128)(2,1)}, bf16[528,512]{1,0:T(8,128)(2,1)}, u32[]{:S(2)}, u32[]{:S(2)}) collective-permute-start(bf16[528,512]{1,0:T(8,128)(2,1)} %collective-permute-done.6), channel_id=1, source_target_pairs={{0,1},{1,2},{2,3},{3,4},{4,5},{5,6},{6,7},{7,0},{8,9},{9,10},{10,1... | collective-permute-start | bytes 1622024 | tf_op jit(solution)/shard_map/ppermute | solution.py:260
  62.5 10.8 %collective-permute-start.12 = (bf16[528,512]{1,0:T(8,128)(2,1)}, bf16[528,512]{1,0:T(8,128)(2,1)S(1)}, u32[]{:S(2)}, u32[]{:S(2)}) collective-permute-start(bf16[528,512]{1,0:T(8,128)(2,1)} %collective-permute-done.6), channel_id=1, source_target_pairs={{0,32},{32,0},{64,96},{96,64},{128,160},{160,128},{192,224},{224,1... | collective-permute-start | bytes 1622024 | tf_op jit(solution)/shard_map/ppermute | solution.py:263
  64.5 11.5 %collective-permute-start.11 = (bf16[528,512]{1,0:T(8,128)(2,1)}, bf16[528,512]{1,0:T(8,128)(2,1)}, u32[]{:S(2)}, u32[]{:S(2)}) collective-permute-start(bf16[528,512]{1,0:T(8,128)(2,1)} %collective-permute-done.9.refs_1_.refs_5_), channel_id=1, source_target_pairs={{0,1},{1,2},{2,3},{3,4},{4,5},{5,6},{6,7},{7,0},{8,9},{9,10},{10,1... | collective-permute-start | bytes 1622024 | tf_op jit(solution)/shard_map/ppermute | solution.py:260
  68.1 12.9 %collective-permute-start.10 = (bf16[528,512]{1,0:T(8,128)(2,1)}, bf16[528,512]{1,0:T(8,128)(2,1)}, u32[]{:S(2)}, u32[]{:S(2)}) collective-permute-start(bf16[528,512]{1,0:T(8,128)(2,1)} %collective-permute-done.8), channel_id=1, source_target_pairs={{0,1},{1,2},{2,3},{3,4},{4,5},{5,6},{6,7},{7,0},{8,9},{9,10},{10,1... | collective-permute-start | bytes 1622024 | tf_op jit(solution)/shard_map/ppermute | solution.py:260
  71.3 9.7 %collective-permute-start.13 = (bf16[528,512]{1,0:T(8,128)(2,1)}, bf16[528,512]{1,0:T(8,128)(2,1)S(1)}, u32[]{:S(2)}, u32[]{:S(2)}) collective-permute-start(bf16[528,512]{1,0:T(8,128)(2,1)} %collective-permute-done.8), channel_id=1, source_target_pairs={{0,32},{32,0},{64,96},{96,64},{128,160},{160,128},{192,224},{224,1... | collective-permute-start | bytes 1622024 | tf_op jit(solution)/shard_map/ppermute | solution.py:263
  86.2 7.6 %collective-permute-start.17 = (bf16[3,2048,128]{2,1,0:T(8,128)(2,1)}, bf16[3,2048,128]{2,1,0:T(8,128)(2,1)}, u32[]{:S(2)}, u32[]{:S(2)}) collective-permute-start(bf16[3,2048,128]{2,1,0:T(8,128)(2,1)} %collective-permute-done.16.refs_0_), channel_id=1, source_target_pairs={{0,32},{32,0},{64,96},{96,64},{128,160},{160,128},{192,224},{224,1... | collective-permute-start | bytes 4718600 | tf_op jit(solution)/shard_map/ppermute | solution.py:263
  89.0 11.2 %collective-permute-start.15 = (bf16[528,512]{1,0:T(8,128)(2,1)}, bf16[528,512]{1,0:T(8,128)(2,1)}, u32[]{:S(2)}, u32[]{:S(2)}) collective-permute-start(bf16[528,512]{1,0:T(8,128)(2,1)} %collective-permute-done.11.refs_2_.refs_1_), channel_id=1, source_target_pairs={{0,1},{1,2},{2,3},{3,4},{4,5},{5,6},{6,7},{7,0},{8,9},{9,10},{10,1... | collective-permute-start | bytes 1622024 | tf_op jit(solution)/shard_map/ppermute | solution.py:260
  91.8 8.5 %collective-permute-start.14 = (bf16[528,512]{1,0:T(8,128)(2,1)}, bf16[528,512]{1,0:T(8,128)(2,1)}, u32[]{:S(2)}, u32[]{:S(2)}) collective-permute-start(bf16[528,512]{1,0:T(8,128)(2,1)} %collective-permute-done.10), channel_id=1, source_target_pairs={{0,32},{32,0},{64,96},{96,64},{128,160},{160,128},{192,224},{224,1... | collective-permute-start | bytes 1622024 | tf_op jit(solution)/shard_map/ppermute | solution.py:263
  100.3 7.5 %copy-start.2 = (f32[3,528,128]{2,1,0:T(8,128)S(1)}, f32[3,528,128]{2,1,0:T(8,128)}, u32[]{:S(2)}) copy-start(f32[3,528,128]{2,1,0:T(8,128)} %copy-done.1) | copy-start | bytes 2433028
  100.3 7.5 %copy-start.7 = (f32[128,16]{0,1:T(8,128)S(1)}, f32[128,16]{0,1:T(8,128)}, u32[]{:S(2)}) copy-start(f32[128,16]{0,1:T(8,128)} %param.11) | copy-start | bytes 24580
  100.3 7.5 %copy-start.8 = (f32[3,7,128]{2,1,0:T(8,128)S(1)}, f32[3,7,128]{2,1,0:T(8,128)}, u32[]{:S(2)}) copy-start(f32[3,7,128]{2,1,0:T(8,128)} %taps.1) | copy-start | bytes 32260
  100.3 7.5 %copy-start.9 = (f32[128]{0:T(128)S(1)}, f32[128]{0:T(128)}, u32[]{:S(2)}) copy-start(f32[128]{0:T(128)} %param.12) | copy-start | bytes 1540
  105.0 33.3 %collective-permute-start.18 = (f32[1168,128]{1,0:T(8,128)S(1)}, f32[1168,128]{1,0:T(8,128)S(1)}, u32[]{:S(2)}, u32[]{:S(2)}) collective-permute-start(f32[1168,128]{1,0:T(8,128)S(1)} %get-tuple-element.48), channel_id=1, source_target_pairs={{0,8},{1,9},{2,10},{3,11},{4,12},{5,13},{6,14},{7,15},{8,0},{9,1},... | collective-permute-start | bytes 1794056 | tf_op jit(solution)/shard_map/ppermute | solution.py:249
  (5 other events, 8.3 us)

commit v6 on v4

--- a/solution.py
+++ b/solution.py
@@ -18,6 +18,10 @@
 LINES = 4
 SMEM = pl.BlockSpec(memory_space=pltpu.SMEM)
 VMEM = pl.BlockSpec(memory_space=pltpu.VMEM)
+
+
+def after(value, earlier):
+    return lax.optimization_barrier((value, earlier))[0]
 
 
 def wide(row):
@@ -66,12 +70,21 @@
     )(ids, *in_weights, *blocks, *extra)
 
 
-def local_kernel(count, kinds, at, seat, ids, sums, taps, weights, decays, skip, *refs):
+def local_kernel(count, kinds, summed, at, seat, ids, taps, weights, decays, skip, *refs):
+    sums, refs = refs[:summed], refs[summed:]
     in_weights, blocks, (pack, sent, proj, ends) = refs[:kinds], refs[kinds : kinds + count], refs[-4:]
-    rows = proj.shape[1] - HALO
+    rows = blocks[0].shape[0] - HALO
     length = rows // CHUNKS
+    early = TAPS - 1
+    top = lax.broadcasted_iota(jnp.int32, (CHUNKS, LANES), 0) == 0
     for s, part in enumerate(products(blocks, ids, at, in_weights)):
-        proj[s] = sums[s] + part
+        total = sums[0][s] + part if sums else part
+        proj[s, early * CHUNKS :, :] = total[HALO:]
+        for p in range(early):
+            end = pltpu.roll(proj[s, (length + p) * CHUNKS : (length + p + 1) * CHUNKS, :], 1, 0)
+            proj[s, p * CHUNKS : (p + 1) * CHUNKS, :] = jnp.where(
+                top, wide(total[HALO - early + p : HALO - early + p + 1]), end
+            )
     poles = [wide(jnp.exp(-decays[m : m + 1, :])) for m in range(MODES)]
     gains = [wide(weights[m : m + 1, :]) for m in range(MODES)]
     skip_row = wide(skip[0:1, :])
@@ -81,7 +94,7 @@
         at = at * UNROLL
         taken = [
             [
-                proj[s, pl.ds(at + HALO - (TAPS - 1) + k, CHUNKS, stride=length), :]
+                proj[s, pl.ds(pl.multiple_of((at + k) * CHUNKS, CHUNKS), CHUNKS), :]
                 for k in range(UNROLL + TAPS - 1)
             ]
             for s in range(3)
@@ -117,26 +130,27 @@
 
 
 def local_part(sent, sums, blocks, seat, ids, at, in_weights, taps, weights, decays, skip, count):
-    rows = sums.shape[1] - HALO
+    rows = blocks[0].shape[0] - HALO
     extra = [] if sent is None else [sent]
+    summed = [] if sums is None else [sums]
     return pl.pallas_call(
-        functools.partial(local_kernel, len(blocks), len(in_weights), at),
-        in_specs=[SMEM] * 2 + [VMEM] * (5 + len(in_weights) + len(blocks) + len(extra)),
+        functools.partial(local_kernel, len(blocks), len(in_weights), len(summed), at),
+        in_specs=[SMEM] * 2 + [VMEM] * (4 + len(summed) + len(in_weights) + len(blocks) + len(extra)),
         out_specs=[VMEM] * 2,
         out_shape=[
             jax.ShapeDtypeStruct((2 * rows + (CHUNKS + 1) * MODES, LANES), jnp.float32),
             jax.ShapeDtypeStruct((2, count, MODES, LANES), jnp.float32),
         ],
-        input_output_aliases={7 + len(in_weights) + len(blocks): 1} if extra else {},
+        input_output_aliases={6 + len(summed) + len(in_weights) + len(blocks): 1} if extra else {},
         scratch_shapes=[
-            pltpu.VMEM(sums.shape, jnp.float32),
+            pltpu.VMEM((3, rows + (TAPS - 1) * CHUNKS, LANES), jnp.float32),
             pltpu.VMEM((MODES * CHUNKS, LANES), jnp.float32),
         ],
         compiler_params=pltpu.CompilerParams(vmem_limit_bytes=16 * 2**20),
         cost_estimate=pl.CostEstimate(
             flops=rows * LANES * 110, bytes_accessed=rows * LANES * 20, transcendentals=0
         ),
-    )(seat, ids, sums, taps, weights, decays, skip, *in_weights, *blocks, *extra)
+    )(seat, ids, taps, weights, decays, skip, *summed, *in_weights, *blocks, *extra)
 
 
 def final_kernel(rows, seat, arrived, mine, other, weights, decays, out, begins):
@@ -237,17 +251,19 @@
     other_seat = jnp.stack([mine, half, 1 - half]).astype(jnp.int32)
 
     before = lax.ppermute(tokens[rows - HALO :], "ctx", [(i, i + 1) for i in range(blocks - 1)])
-    padded = jnp.concatenate([before, tokens], axis=0)
-    kept = lax.dynamic_slice_in_dim(padded, half * part, part + HALO, 0)
-    given = lax.dynamic_slice_in_dim(padded, (1 - half) * part, part + HALO, 0)
+    ordered = tokens.reshape(2, CHUNKS, part // CHUNKS, -1).swapaxes(1, 2).reshape(2, part, -1)
+    between = tokens[part - HALO : part]
+    low = half == 0
+    kept = jnp.concatenate([jnp.where(low, before, between), jnp.where(low, ordered[0], ordered[1])], axis=0)
+    given = jnp.concatenate([jnp.where(low, between, before), jnp.where(low, ordered[1], ordered[0])], axis=0)
     nearest = beside(given, 1)
     count = in_weights.shape[1] // 2
     half_weights = lax.dynamic_slice_in_dim(in_weights, mine % 2 * count, count, 1)
     values = jnp.concatenate([short_taps.reshape(3 * TAPS, -1), weights, rates, skip_gain[None, :]], axis=0)
-    nearest, half_weights, values = lax.optimization_barrier((nearest, half_weights, values))
-    half_weights, values = beside(half_weights, 1), beside(values, 1)
+    half_weights, values = beside(after(half_weights, nearest), 1), beside(values, 1)
     block = jnp.concatenate([kept, nearest, beside(kept, 2), beside(given, 3)], axis=1)
 
+    block = after(block, values)
     straight, turned = onward(block), other_core(block)
     crossed = onward(turned)
     sums, waiting, met = None, [block], 0
@@ -257,7 +273,7 @@
         crossed, here = lax.optimization_barrier((crossed, straight))
         turned = crossed
         if step == ring // 2 - 1:
-            crossed, waiting[1] = lax.optimization_barrier((crossed, waiting[1]))
+            crossed = after(after(crossed, waiting[1]), half_weights)
         straight = onward(straight)
         swapped = other_core(crossed)
         if step < ring // 2 - 1:
@@ -268,13 +284,14 @@
         waiting = [here, swapped]
         if step < ring // 2 - 1:
             straight, sums = lax.optimization_barrier((straight, sums))
-    half_weights, sums = lax.optimization_barrier((half_weights, sums))
+    half_weights = after(after(half_weights, straight), swapped)
     their_weights = [half_weights, other_core(half_weights)]
-    theirs = project(None, arrived[:met], ids, ring, their_weights)
     waiting.append(straight)
-
+    pack, sent = local_part(
+        None, sums, waiting, seat, ids, met, [in_weights], short_taps, weights, rates, skip_gain[None, :], blocks
+    )
     other_pack, sent = local_part(
-        None, theirs, waiting, other_seat, ids, ring + met, their_weights,
+        sent, None, arrived + waiting, other_seat, ids, ring, their_weights,
         values[: 3 * TAPS].reshape(3, TAPS, -1),
         values[3 * TAPS : 3 * TAPS + MODES],
         values[3 * TAPS + MODES : 3 * TAPS + 2 * MODES],
@@ -282,9 +299,6 @@
         blocks,
     )
     other = beside(other_pack, 1)
-    pack, sent = local_part(
-        sent, sums, waiting, seat, ids, met, [in_weights], short_taps, weights, rates, skip_gain[None, :], blocks
-    )
     groups = [
         [(i * lines + z + q) * ring + y for q in range(2) for i in range(blocks)]
         for z in range(0, lines, 2)

time: 140 us -> 135 us (0.964)
  waiting for transfers between devices: 17.4 us -> 8.07 us
  blocking collectives: 22.8 us -> 27.6 us
  Pallas kernels: 20.4 us -> 16.2 us
  starting transfers between devices: 65.3 us -> 67.8 us
    ppermute x7, waiting for transfers between devices: 6.56 us -> 0.79 us  [onward(): return lax.ppermute(block, ('ctx', 'ch'), route)]
    all_to_all x1, blocking collectives: 22.8 us -> 27.6 us  [per_device(): lax.all_to_all(sent.reshape(2 * blocks, MODES, LANES), ('ctx', 'ch'), 0,...]
    ppermute x6, waiting for transfers between devices: 10.9 us -> 6.57 us  [beside(): lax.ppermute(block, 'ch', [(z * ring + y, (z ^ step) * ring + y) for z in...]
    pallas_call x4 -> x3, Pallas kernels: 8.76 us -> 5.43 us  [project(): pl.pallas_call(functools.partial(project_kernel, len(blocks), len(in_weig...]
    ppermute x7, starting transfers between devices: 26.9 us -> 29.4 us  [onward(): return lax.ppermute(block, ('ctx', 'ch'), route)]
    unnamed x31 -> x36, local copies, waits for them, and re-layouts: 5.91 us -> 6.37 us
  transfers between devices with their start and end apart: 19 -> 19, of which waited for: 6 -> 4; matrix products, arithmetic and copies ran while one was open for 3% -> 4% of each run, Pallas kernels for 9% -> 6%
where the time goes in v6:
time: 135 us; the launch traced here: 134 us
  starting transfers between devices  67.8 us (50%)
  blocking collectives  27.6 us (20%)
  Pallas kernels  16.2 us (12%)
  local copies, waits for them, and re-layouts  11.6 us (9%)
  waiting for transfers between devices  8.07 us (6%)
  other arithmetic  1.8 us (1%)
    ppermute x7, starting transfers between devices, onward(): return lax.ppermute(block, ('ctx', 'ch'), route)  29.4 us
    all_to_all x1, blocking collectives, per_device(): lax.all_to_all(sent.reshape(2 * blocks, MODES, LANES), ('ctx', 'ch'), 0,...  27.6 us
    ppermute x6, starting transfers between devices, beside(): lax.ppermute(block, 'ch', [(z * ring + y, (z ^ step) * ring + y) for z in...  16.1 us
    ppermute x1, starting transfers between devices, per_device(): lax.ppermute(tokens[rows - HALO:], 'ctx', [(i, i + 1) for i in range(bloc...  12 us
    ppermute x5, starting transfers between devices, other_core(): return lax.ppermute(block, 'ctx', [(i, i ^ 1) for i in range(blocks)])  10.2 us
    pallas_call x2, Pallas kernels, local_part(): pl.pallas_call(functools.partial(local_kernel, len(blocks), len(in_weight...  8.69 us
    ppermute x6, waiting for transfers between devices, beside(): lax.ppermute(block, 'ch', [(z * ring + y, (z ^ step) * ring + y) for z in...  6.57 us
    unnamed x36, local copies, waits for them, and re-layouts  6.37 us
  transfers between devices with their start and end apart: 19, of which 4 were waited for; matrix products, arithmetic and copies ran while one was open for 4% of the time, Pallas kernels for 6%

profile of v6, /device:TPU:1, one launch (start us, length us, event | category | flops | bytes accessed | tf_op | source)
XLA Modules:
  0.0 133.6 jit_solution(3762318390973995909)
XLA Ops:
  0.8 12.0 %collective-permute-start.1 = (bf16[16,128]{1,0:T(8,128)(2,1)S(1)}, bf16[16,128]{1,0:T(8,128)(2,1)S(1)}, u32[]{:S(2)}, u32[]{:S(2)}) collective-permute-start(bf16[16,128]{1,0:T(8,128)(2,1)S(1)} %slice.33), channel_id=1, source_target_pairs={{0,32},{32,64},{64,96},{96,128},{128,160},{160,192},{192,224},{224... | collective-permute-start | bytes 12296 | tf_op jit(solution)/shard_map/ppermute | solution.py:253
  14.7 4.9 %collective-permute-start.5 = (bf16[528,128]{1,0:T(8,128)(2,1)S(1)}, bf16[528,128]{1,0:T(8,128)(2,1)S(1)}, u32[]{:S(2)}, u32[]{:S(2)}) collective-permute-start(bf16[528,128]{1,0:T(8,128)(2,1)S(1)} %pad_maximum_fusion.1), channel_id=1, source_target_pairs={{0,24},{1,25},{2,26},{3,27},{4,28},{5,29},{6,30},{7,31},{8,16},{9,... | collective-permute-start | bytes 405512 | tf_op jit(solution)/shard_map/ppermute | solution.py:221
  19.6 1.9 %collective-permute-start.2 = (bf16[528,128]{1,0:T(8,128)(2,1)S(1)}, bf16[528,128]{1,0:T(8,128)(2,1)S(1)}, u32[]{:S(2)}, u32[]{:S(2)}) collective-permute-start(bf16[528,128]{1,0:T(8,128)(2,1)S(1)} %pad_maximum_fusion.1), channel_id=1, source_target_pairs={{0,8},{1,9},{2,10},{3,11},{4,12},{5,13},{6,14},{7,15},{8,0},{9,1},... | collective-permute-start | bytes 405512 | tf_op jit(solution)/shard_map/ppermute | solution.py:221
  21.6 2.4 %collective-permute-start.4 = (bf16[528,128]{1,0:T(8,128)(2,1)S(1)}, bf16[528,128]{1,0:T(8,128)(2,1)S(1)}, u32[]{:S(2)}, u32[]{:S(2)}) collective-permute-start(bf16[528,128]{1,0:T(8,128)(2,1)S(1)} %pad_maximum_fusion.2), channel_id=1, source_target_pairs={{0,16},{1,17},{2,18},{3,19},{4,20},{5,21},{6,22},{7,23},{8,24},{9,... | collective-permute-start | bytes 405512 | tf_op jit(solution)/shard_map/ppermute | solution.py:221
  24.1 2.9 %collective-permute-start = (f32[54,128]{1,0:T(8,128)S(1)}, f32[54,128]{1,0:T(8,128)S(1)}, u32[]{:S(2)}, u32[]{:S(2)}) collective-permute-start(f32[54,128]{1,0:T(8,128)S(1)} %pad_maximum_fusion.3), channel_id=1, source_target_pairs={{0,8},{1,9},{2,10},{3,11},{4,12},{5,13},{6,14},{7,15},{8,0},{9,1},... | collective-permute-start | bytes 82952 | tf_op jit(solution)/shard_map/ppermute | solution.py:221
  26.9 2.7 %collective-permute-done.4 = bf16[528,128]{1,0:T(8,128)(2,1)S(1)} collective-permute-done((bf16[528,128]{1,0:T(8,128)(2,1)S(1)}, bf16[528,128]{1,0:T(8,128)(2,1)S(1)}, u32[]{:S(2)}, u32[]{:S(2)}) %collective-permute-start.4) | collective-permute-done | bytes 135200 | tf_op jit(solution)/shard_map/ppermute | solution.py:221
  32.5 5.4 %collective-permute-start.6 = (bf16[528,512]{1,0:T(8,128)(2,1)}, bf16[528,512]{1,0:T(8,128)(2,1)}, u32[]{:S(2)}, u32[]{:S(2)}) collective-permute-start(bf16[528,512]{1,0:T(8,128)(2,1)} %pad_maximum_fusion.refs_1_.refs_2_), channel_id=1, source_target_pairs={{0,1},{1,2},{2,3},{3,4},{4,5},{5,6},{6,7},{7,0},{8,9},{9,10},{10,1... | collective-permute-start | bytes 1622024 | tf_op jit(solution)/shard_map/ppermute | solution.py:232
  37.9 3.0 %collective-permute-start.9 = (bf16[528,512]{1,0:T(8,128)(2,1)}, bf16[528,512]{1,0:T(8,128)(2,1)}, u32[]{:S(2)}, u32[]{:S(2)}) collective-permute-start(bf16[528,512]{1,0:T(8,128)(2,1)} %collective-permute-done.7), channel_id=1, source_target_pairs={{0,1},{1,2},{2,3},{3,4},{4,5},{5,6},{6,7},{7,0},{8,9},{9,10},{10,1... | collective-permute-start | bytes 1622024 | tf_op jit(solution)/shard_map/ppermute | solution.py:232
  40.9 2.7 %constant_dynamic-slice_fusion = bf16[3,2048,128]{2,1,0:T(8,128)(2,1)} fusion(bf16[3,4096,128]{2,1,0:T(8,128)(2,1)} %refs_1_.1, s32[]{:T(128)S(6)} %select_n.56), kind=kLoop, calls=%fused_computation.14 | loop fusion | bytes 3145732 | tf_op jit(solution)/shard_map/dynamic_slice | solution.py:261
  43.5 2.0 %collective-permute-start.3 = (bf16[3,2048,128]{2,1,0:T(8,128)(2,1)}, bf16[3,2048,128]{2,1,0:T(8,128)(2,1)}, u32[]{:S(2)}, u32[]{:S(2)}) collective-permute-start(bf16[3,2048,128]{2,1,0:T(8,128)(2,1)} %constant_dynamic-slice_fusion), channel_id=1, source_target_pairs={{0,8},{1,9},{2,10},{3,11},{4,12},{5,13},{6,14},{7,15},{8,0},{9,1},... | collective-permute-start | bytes 4718600 | tf_op jit(solution)/shard_map/ppermute | solution.py:221
  45.6 3.9 %collective-permute-start.8 = (bf16[528,512]{1,0:T(8,128)(2,1)}, bf16[528,512]{1,0:T(8,128)(2,1)}, u32[]{:S(2)}, u32[]{:S(2)}) collective-permute-start(bf16[528,512]{1,0:T(8,128)(2,1)} %collective-permute-done.6.refs_1_.refs_3_), channel_id=1, source_target_pairs={{0,1},{1,2},{2,3},{3,4},{4,5},{5,6},{6,7},{7,0},{8,9},{9,10},{10,1... | collective-permute-start | bytes 1622024 | tf_op jit(solution)/shard_map/ppermute | solution.py:232
  50.3 5.0 %collective-permute-start.12 = (bf16[528,512]{1,0:T(8,128)(2,1)}, bf16[528,512]{1,0:T(8,128)(2,1)}, u32[]{:S(2)}, u32[]{:S(2)}) collective-permute-start(bf16[528,512]{1,0:T(8,128)(2,1)} %collective-permute-done.9), channel_id=1, source_target_pairs={{0,1},{1,2},{2,3},{3,4},{4,5},{5,6},{6,7},{7,0},{8,9},{9,10},{10,1... | collective-permute-start | bytes 1622024 | tf_op jit(solution)/shard_map/ppermute | solution.py:232
  59.4 3.6 %collective-permute-start.10 = (bf16[528,512]{1,0:T(8,128)(2,1)}, bf16[528,512]{1,0:T(8,128)(2,1)S(1)}, u32[]{:S(2)}, u32[]{:S(2)}) collective-permute-start(bf16[528,512]{1,0:T(8,128)(2,1)} %collective-permute-done.8.refs_1_.refs_5_), channel_id=1, source_target_pairs={{0,1},{1,2},{2,3},{3,4},{4,5},{5,6},{6,7},{7,0},{8,9},{9,10},{10,1... | collective-permute-start | bytes 1622024 | tf_op jit(solution)/shard_map/ppermute | solution.py:232
  63.0 3.9 %collective-permute-start.14 = (bf16[528,512]{1,0:T(8,128)(2,1)}, bf16[528,512]{1,0:T(8,128)(2,1)S(1)}, u32[]{:S(2)}, u32[]{:S(2)}) collective-permute-start(bf16[528,512]{1,0:T(8,128)(2,1)} %collective-permute-done.12), channel_id=1, source_target_pairs={{0,1},{1,2},{2,3},{3,4},{4,5},{5,6},{6,7},{7,0},{8,9},{9,10},{10,1... | collective-permute-start | bytes 1622024 | tf_op jit(solution)/shard_map/ppermute | solution.py:232
  68.9 2.0 %shard_map.74.refs_3_ = f32[3,528,128]{2,1,0:T(8,128)S(1)} custom-call(s32[64]{0:T(128)S(1)} %dynamic-slice_bitcast_fusion.ids, bf16[3,4096,128]{2,1,0:T(8,128)(2,1)S(1)} %copy-done, bf16[528,512]{1,0:T(8,128)(2,1)} %collective-permute-done.6.refs_1_.refs_3_, ...), custom_call_target="tpu_custom_call", output_to_operand_aliasing={{}: (4, {})} | custom-call | flops 528 | bytes 528 | tf_op jit(solution)/shard_map/pallas_call | solution.py:62
  71.8 4.7 %collective-permute-start.13 = (bf16[528,512]{1,0:T(8,128)(2,1)S(1)}, bf16[528,512]{1,0:T(8,128)(2,1)S(1)}, u32[]{:S(2)}, u32[]{:S(2)}) collective-permute-start(bf16[528,512]{1,0:T(8,128)(2,1)S(1)} %collective-permute-done.10.refs_2_.refs_7_), channel_id=1, source_target_pairs={{0,1},{1,2},{2,3},{3,4},{4,5},{5,6},{6,7},{7,0},{8,9},{9,10},{10,1... | collective-permute-start | bytes 1622024 | tf_op jit(solution)/shard_map/ppermute | solution.py:232
  78.1 3.8 %collective-permute-done.3.refs_0_ = bf16[3,2048,128]{2,1,0:T(8,128)(2,1)} collective-permute-done((bf16[3,2048,128]{2,1,0:T(8,128)(2,1)}, bf16[3,2048,128]{2,1,0:T(8,128)(2,1)}, u32[]{:S(2)}, u32[]{:S(2)}) %collective-permute-start.3) | collective-permute-done | bytes 1572896 | tf_op jit(solution)/shard_map/ppermute | solution.py:221
  81.9 2.2 %collective-permute-start.16 = (bf16[528,512]{1,0:T(8,128)(2,1)S(1)}, bf16[528,512]{1,0:T(8,128)(2,1)S(1)}, u32[]{:S(2)}, u32[]{:S(2)}) collective-permute-start(bf16[528,512]{1,0:T(8,128)(2,1)S(1)} %collective-permute-done.14), channel_id=1, source_target_pairs={{0,32},{32,0},{64,96},{96,64},{128,160},{160,128},{192,224},{224,1... | collective-permute-start | bytes 1622024 | tf_op jit(solution)/shard_map/ppermute | solution.py:235
  86.6 2.2 %collective-permute-start.17 = (bf16[3,2048,128]{2,1,0:T(8,128)(2,1)}, bf16[3,2048,128]{2,1,0:T(8,128)(2,1)}, u32[]{:S(2)}, u32[]{:S(2)}) collective-permute-start(bf16[3,2048,128]{2,1,0:T(8,128)(2,1)} %collective-permute-done.3.refs_0_), channel_id=1, source_target_pairs={{0,32},{32,0},{64,96},{96,64},{128,160},{160,128},{192,224},{224,1... | collective-permute-start | bytes 4718600 | tf_op jit(solution)/shard_map/ppermute | solution.py:235
  93.2 2.8 %shard_map.76 = (f32[1168,128]{1,0:T(8,128)S(1)}, f32[2,16,16,128]{3,2,1,0:T(8,128)S(1)}) custom-call(s32[3]{0:T(128)S(1)} %pad_add_fusion.seat, s32[64]{0:T(128)S(1)} %dynamic-slice_bitcast_fusion.ids, f32[3,7,128]{2,1,0:T(8,128)S(1)} %copy-done.15, f32[16,128]{1,0:T(8,128)S(1)} %multiply_bitcast_fusion.weights, f32[16,128]{1,0:T(8,128)S(1)} %bitcast.20, ...), custom_call_target="tpu_custom_call" | custom-call | flops 7208960 | bytes 1310720 | tf_op jit(solution)/shard_map/pallas_call | solution.py:136
  96.0 5.9 %shard_map.77 = (f32[1168,128]{1,0:T(8,128)S(1)}, f32[2,16,16,128]{3,2,1,0:T(8,128)S(1)}) custom-call(s32[3]{0:T(128)S(1)} %pad_add_fusion.2.seat, s32[64]{0:T(128)S(1)} %dynamic-slice_bitcast_fusion.ids, f32[3,7,128]{2,1,0:T(8,128)S(1)} %reshape.22.taps, f32[16,128]{1,0:T(8,128)S(1)} %get-tuple-element.56.weights, ...), custom_call_target="tpu_custom_call", output_to_operand_aliasing={{1}: (16, {})} | custom-call | flops 7208960 | bytes 1310720 | tf_op jit(solution)/shard_map/pallas_call | solution.py:136
  101.9 2.0 %collective-permute-start.18 = (f32[1168,128]{1,0:T(8,128)S(1)}, f32[1168,128]{1,0:T(8,128)S(1)}, u32[]{:S(2)}, u32[]{:S(2)}) collective-permute-start(f32[1168,128]{1,0:T(8,128)S(1)} %get-tuple-element.50), channel_id=1, source_target_pairs={{0,8},{1,9},{2,10},{3,11},{4,12},{5,13},{6,14},{7,15},{8,0},{9,1},... | collective-permute-start | bytes 1794056 | tf_op jit(solution)/shard_map/ppermute | solution.py:221
  103.9 27.6 %all_to_all.5.arrived = f32[32,16,128]{2,1,0:T(8,128)S(1)} all-to-all(f32[32,16,128]{2,1,0:T(8,128)S(1)} %bitcast.18), channel_id=1, replica_groups={{0,32,64,96,128,160,192,224,256,288,320,352,384,416,448,480,8,40,72,104..., dimensions={0} | all-to-all | bytes 524288 | tf_op jit(solution)/shard_map/all_to_all | solution.py:307
  131.5 2.1 %shard_map.78 = f32[1024,128]{1,0:T(8,128)} custom-call(s32[3]{0:T(128)S(1)} %pad_add_fusion.seat, f32[32,16,128]{2,1,0:T(8,128)S(1)} %all_to_all.5.arrived, f32[1168,128]{1,0:T(8,128)S(1)} %get-tuple-element.49.mine, f32[1168,128]{1,0:T(8,128)S(1)} %collective-permute-done.18.other, f32[16,128]{1,0:T(8,128)S(1)} %multiply_bitcast_fusion.weights, ...), custom_call_target="tpu_custom_call" | custom-call | flops 4718592 | bytes 1572864 | tf_op jit(solution)/shard_map/pallas_call | solution.py:196
  (75 shorter events, 21.4 us)
Async XLA Ops:
  0.0 24.0 %copy-start.14 = (f32[128,16]{0,1:T(8,128)S(1)}, f32[128,16]{0,1:T(8,128)}, u32[]{:S(2)}) copy-start(f32[128,16]{0,1:T(8,128)} %param.11) | copy-start | bytes 24580
  0.0 24.0 %copy-start.17 = (f32[128,16]{0,1:T(8,128)S(1)}, f32[128,16]{0,1:T(8,128)}, u32[]{:S(2)}) copy-start(f32[128,16]{0,1:T(8,128)} %param.10) | copy-start | bytes 24580
  0.0 24.0 %copy-start.15 = (f32[3,7,128]{2,1,0:T(8,128)S(1)}, f32[3,7,128]{2,1,0:T(8,128)}, u32[]{:S(2)}) copy-start(f32[3,7,128]{2,1,0:T(8,128)} %taps.1) | copy-start | bytes 32260
  0.0 24.1 %copy-start.16 = (f32[128]{0:T(128)S(1)}, f32[128]{0:T(128)}, u32[]{:S(2)}) copy-start(f32[128]{0:T(128)} %param.12) | copy-start | bytes 1540
  0.8 13.2 %collective-permute-start.1 = (bf16[16,128]{1,0:T(8,128)(2,1)S(1)}, bf16[16,128]{1,0:T(8,128)(2,1)S(1)}, u32[]{:S(2)}, u32[]{:S(2)}) collective-permute-start(bf16[16,128]{1,0:T(8,128)(2,1)S(1)} %slice.33), channel_id=1, source_target_pairs={{0,32},{32,64},{64,96},{96,128},{128,160},{160,192},{192,224},{224... | collective-permute-start | bytes 12296 | tf_op jit(solution)/shard_map/ppermute | solution.py:253
  14.7 15.0 %collective-permute-start.5 = (bf16[528,128]{1,0:T(8,128)(2,1)S(1)}, bf16[528,128]{1,0:T(8,128)(2,1)S(1)}, u32[]{:S(2)}, u32[]{:S(2)}) collective-permute-start(bf16[528,128]{1,0:T(8,128)(2,1)S(1)} %pad_maximum_fusion.1), channel_id=1, source_target_pairs={{0,24},{1,25},{2,26},{3,27},{4,28},{5,29},{6,30},{7,31},{8,16},{9,... | collective-permute-start | bytes 405512 | tf_op jit(solution)/shard_map/ppermute | solution.py:221
  19.6 10.1 %collective-permute-start.2 = (bf16[528,128]{1,0:T(8,128)(2,1)S(1)}, bf16[528,128]{1,0:T(8,128)(2,1)S(1)}, u32[]{:S(2)}, u32[]{:S(2)}) collective-permute-start(bf16[528,128]{1,0:T(8,128)(2,1)S(1)} %pad_maximum_fusion.1), channel_id=1, source_target_pairs={{0,8},{1,9},{2,10},{3,11},{4,12},{5,13},{6,14},{7,15},{8,0},{9,1},... | collective-permute-start | bytes 405512 | tf_op jit(solution)/shard_map/ppermute | solution.py:221
  21.6 8.1 %collective-permute-start.4 = (bf16[528,128]{1,0:T(8,128)(2,1)S(1)}, bf16[528,128]{1,0:T(8,128)(2,1)S(1)}, u32[]{:S(2)}, u32[]{:S(2)}) collective-permute-start(bf16[528,128]{1,0:T(8,128)(2,1)S(1)} %pad_maximum_fusion.2), channel_id=1, source_target_pairs={{0,16},{1,17},{2,18},{3,19},{4,20},{5,21},{6,22},{7,23},{8,24},{9,... | collective-permute-start | bytes 405512 | tf_op jit(solution)/shard_map/ppermute | solution.py:221
  24.1 6.5 %collective-permute-start = (f32[54,128]{1,0:T(8,128)S(1)}, f32[54,128]{1,0:T(8,128)S(1)}, u32[]{:S(2)}, u32[]{:S(2)}) collective-permute-start(f32[54,128]{1,0:T(8,128)S(1)} %pad_maximum_fusion.3), channel_id=1, source_target_pairs={{0,8},{1,9},{2,10},{3,11},{4,12},{5,13},{6,14},{7,15},{8,0},{9,1},... | collective-permute-start | bytes 82952 | tf_op jit(solution)/shard_map/ppermute | solution.py:221
  30.6 7.3 %collective-permute-start.7 = (bf16[528,512]{1,0:T(8,128)(2,1)}, bf16[528,512]{1,0:T(8,128)(2,1)}, u32[]{:S(2)}, u32[]{:S(2)}) collective-permute-start(bf16[528,512]{1,0:T(8,128)(2,1)} %pad_maximum_fusion.refs_1_.refs_2_), channel_id=1, source_target_pairs={{0,32},{32,0},{64,96},{96,64},{128,160},{160,128},{192,224},{224,1... | collective-permute-start | bytes 1622024 | tf_op jit(solution)/shard_map/ppermute | solution.py:235
  32.5 23.5 %copy-start = (bf16[3,4096,128]{2,1,0:T(8,128)(2,1)S(1)}, bf16[3,4096,128]{2,1,0:T(8,128)(2,1)}, u32[]{:S(2)}) copy-start(bf16[3,4096,128]{2,1,0:T(8,128)(2,1)} %refs_1_.1) | copy-start | bytes 9437188
  32.5 13.1 %collective-permute-start.6 = (bf16[528,512]{1,0:T(8,128)(2,1)}, bf16[528,512]{1,0:T(8,128)(2,1)}, u32[]{:S(2)}, u32[]{:S(2)}) collective-permute-start(bf16[528,512]{1,0:T(8,128)(2,1)} %pad_maximum_fusion.refs_1_.refs_2_), channel_id=1, source_target_pairs={{0,1},{1,2},{2,3},{3,4},{4,5},{5,6},{6,7},{7,0},{8,9},{9,10},{10,1... | collective-permute-start | bytes 1622024 | tf_op jit(solution)/shard_map/ppermute | solution.py:232
  37.9 12.4 %collective-permute-start.9 = (bf16[528,512]{1,0:T(8,128)(2,1)}, bf16[528,512]{1,0:T(8,128)(2,1)}, u32[]{:S(2)}, u32[]{:S(2)}) collective-permute-start(bf16[528,512]{1,0:T(8,128)(2,1)} %collective-permute-done.7), channel_id=1, source_target_pairs={{0,1},{1,2},{2,3},{3,4},{4,5},{5,6},{6,7},{7,0},{8,9},{9,10},{10,1... | collective-permute-start | bytes 1622024 | tf_op jit(solution)/shard_map/ppermute | solution.py:232
  43.5 38.4 %collective-permute-start.3 = (bf16[3,2048,128]{2,1,0:T(8,128)(2,1)}, bf16[3,2048,128]{2,1,0:T(8,128)(2,1)}, u32[]{:S(2)}, u32[]{:S(2)}) collective-permute-start(bf16[3,2048,128]{2,1,0:T(8,128)(2,1)} %constant_dynamic-slice_fusion), channel_id=1, source_target_pairs={{0,8},{1,9},{2,10},{3,11},{4,12},{5,13},{6,14},{7,15},{8,0},{9,1},... | collective-permute-start | bytes 4718600 | tf_op jit(solution)/shard_map/ppermute | solution.py:221
  45.6 13.9 %collective-permute-start.8 = (bf16[528,512]{1,0:T(8,128)(2,1)}, bf16[528,512]{1,0:T(8,128)(2,1)}, u32[]{:S(2)}, u32[]{:S(2)}) collective-permute-start(bf16[528,512]{1,0:T(8,128)(2,1)} %collective-permute-done.6.refs_1_.refs_3_), channel_id=1, source_target_pairs={{0,1},{1,2},{2,3},{3,4},{4,5},{5,6},{6,7},{7,0},{8,9},{9,10},{10,1... | collective-permute-start | bytes 1622024 | tf_op jit(solution)/shard_map/ppermute | solution.py:232
  50.3 12.7 %collective-permute-start.12 = (bf16[528,512]{1,0:T(8,128)(2,1)}, bf16[528,512]{1,0:T(8,128)(2,1)}, u32[]{:S(2)}, u32[]{:S(2)}) collective-permute-start(bf16[528,512]{1,0:T(8,128)(2,1)} %collective-permute-done.9), channel_id=1, source_target_pairs={{0,1},{1,2},{2,3},{3,4},{4,5},{5,6},{6,7},{7,0},{8,9},{9,10},{10,1... | collective-permute-start | bytes 1622024 | tf_op jit(solution)/shard_map/ppermute | solution.py:232
  57.5 11.3 %collective-permute-start.11 = (bf16[528,512]{1,0:T(8,128)(2,1)}, bf16[528,512]{1,0:T(8,128)(2,1)S(1)}, u32[]{:S(2)}, u32[]{:S(2)}) collective-permute-start(bf16[528,512]{1,0:T(8,128)(2,1)} %collective-permute-done.9), channel_id=1, source_target_pairs={{0,32},{32,0},{64,96},{96,64},{128,160},{160,128},{192,224},{224,1... | collective-permute-start | bytes 1622024 | tf_op jit(solution)/shard_map/ppermute | solution.py:235
  59.4 12.3 %collective-permute-start.10 = (bf16[528,512]{1,0:T(8,128)(2,1)}, bf16[528,512]{1,0:T(8,128)(2,1)S(1)}, u32[]{:S(2)}, u32[]{:S(2)}) collective-permute-start(bf16[528,512]{1,0:T(8,128)(2,1)} %collective-permute-done.8.refs_1_.refs_5_), channel_id=1, source_target_pairs={{0,1},{1,2},{2,3},{3,4},{4,5},{5,6},{6,7},{7,0},{8,9},{9,10},{10,1... | collective-permute-start | bytes 1622024 | tf_op jit(solution)/shard_map/ppermute | solution.py:232
  63.0 14.2 %collective-permute-start.14 = (bf16[528,512]{1,0:T(8,128)(2,1)}, bf16[528,512]{1,0:T(8,128)(2,1)S(1)}, u32[]{:S(2)}, u32[]{:S(2)}) collective-permute-start(bf16[528,512]{1,0:T(8,128)(2,1)} %collective-permute-done.12), channel_id=1, source_target_pairs={{0,1},{1,2},{2,3},{3,4},{4,5},{5,6},{6,7},{7,0},{8,9},{9,10},{10,1... | collective-permute-start | bytes 1622024 | tf_op jit(solution)/shard_map/ppermute | solution.py:232
  66.9 10.3 %collective-permute-start.15 = (bf16[528,512]{1,0:T(8,128)(2,1)}, bf16[528,512]{1,0:T(8,128)(2,1)S(1)}, u32[]{:S(2)}, u32[]{:S(2)}) collective-permute-start(bf16[528,512]{1,0:T(8,128)(2,1)} %collective-permute-done.12), channel_id=1, source_target_pairs={{0,32},{32,0},{64,96},{96,64},{128,160},{160,128},{192,224},{224,1... | collective-permute-start | bytes 1622024 | tf_op jit(solution)/shard_map/ppermute | solution.py:235
  71.8 12.4 %collective-permute-start.13 = (bf16[528,512]{1,0:T(8,128)(2,1)S(1)}, bf16[528,512]{1,0:T(8,128)(2,1)S(1)}, u32[]{:S(2)}, u32[]{:S(2)}) collective-permute-start(bf16[528,512]{1,0:T(8,128)(2,1)S(1)} %collective-permute-done.10.refs_2_.refs_7_), channel_id=1, source_target_pairs={{0,1},{1,2},{2,3},{3,4},{4,5},{5,6},{6,7},{7,0},{8,9},{9,10},{10,1... | collective-permute-start | bytes 1622024 | tf_op jit(solution)/shard_map/ppermute | solution.py:232
  81.9 3.8 %collective-permute-start.16 = (bf16[528,512]{1,0:T(8,128)(2,1)S(1)}, bf16[528,512]{1,0:T(8,128)(2,1)S(1)}, u32[]{:S(2)}, u32[]{:S(2)}) collective-permute-start(bf16[528,512]{1,0:T(8,128)(2,1)S(1)} %collective-permute-done.14), channel_id=1, source_target_pairs={{0,32},{32,0},{64,96},{96,64},{128,160},{160,128},{192,224},{224,1... | collective-permute-start | bytes 1622024 | tf_op jit(solution)/shard_map/ppermute | solution.py:235
  86.6 9.4 %collective-permute-start.17 = (bf16[3,2048,128]{2,1,0:T(8,128)(2,1)}, bf16[3,2048,128]{2,1,0:T(8,128)(2,1)}, u32[]{:S(2)}, u32[]{:S(2)}) collective-permute-start(bf16[3,2048,128]{2,1,0:T(8,128)(2,1)} %collective-permute-done.3.refs_0_), channel_id=1, source_target_pairs={{0,32},{32,0},{64,96},{96,64},{128,160},{160,128},{192,224},{224,1... | collective-permute-start | bytes 4718600 | tf_op jit(solution)/shard_map/ppermute | solution.py:235
  101.9 29.6 %collective-permute-start.18 = (f32[1168,128]{1,0:T(8,128)S(1)}, f32[1168,128]{1,0:T(8,128)S(1)}, u32[]{:S(2)}, u32[]{:S(2)}) collective-permute-start(f32[1168,128]{1,0:T(8,128)S(1)} %get-tuple-element.50), channel_id=1, source_target_pairs={{0,8},{1,9},{2,10},{3,11},{4,12},{5,13},{6,14},{7,15},{8,0},{9,1},... | collective-permute-start | bytes 1794056 | tf_op jit(solution)/shard_map/ppermute | solution.py:221
  (13 other events, 19.8 us)

commit v7 on v6

--- a/solution.py
+++ b/solution.py
@@ -258,12 +258,12 @@
     given = jnp.concatenate([jnp.where(low, between, before), jnp.where(low, ordered[1], ordered[0])], axis=0)
     nearest = beside(given, 1)
     count = in_weights.shape[1] // 2
-    half_weights = lax.dynamic_slice_in_dim(in_weights, mine % 2 * count, count, 1)
+    sliced = lax.dynamic_slice_in_dim(in_weights, mine % 2 * count, count, 1)
     values = jnp.concatenate([short_taps.reshape(3 * TAPS, -1), weights, rates, skip_gain[None, :]], axis=0)
-    half_weights, values = beside(after(half_weights, nearest), 1), beside(values, 1)
+    half_weights, values = beside(after(sliced, nearest), 1), beside(values, 1)
     block = jnp.concatenate([kept, nearest, beside(kept, 2), beside(given, 3)], axis=1)
 
-    block = after(block, values)
+    block = after(after(block, values), sliced)
     straight, turned = onward(block), other_core(block)
     crossed = onward(turned)
     sums, waiting, met = None, [block], 0

time: 135 us -> 134 us (level)
  blocking collectives: 27.6 us -> 23.3 us
  local copies, waits for them, and re-layouts: 11.6 us -> 14.3 us
  starting transfers between devices: 67.8 us -> 70.3 us
  waiting for transfers between devices: 8.07 us -> 6.41 us
    all_to_all x1, blocking collectives: 27.6 us -> 23.3 us  [per_device(): lax.all_to_all(sent.reshape(2 * blocks, MODES, LANES), ('ctx', 'ch'), 0,...]
    ppermute x6, waiting for transfers between devices: 6.57 us -> 4.38 us  [beside(): lax.ppermute(block, 'ch', [(z * ring + y, (z ^ step) * ring + y) for z in...]
    ppermute x5, starting transfers between devices: 10.2 us -> 12.2 us  [other_core(): return lax.ppermute(block, 'ctx', [(i, i ^ 1) for i in range(blocks)])]
    unnamed x36 -> x40, local copies, waits for them, and re-layouts: 6.37 us -> 8.23 us
  transfers between devices with their start and end apart: 19 -> 19, of which waited for: 4 -> 5; matrix products, arithmetic and copies ran while one was open for 4% -> 6% of each run, Pallas kernels for 6% -> 6%
where the time goes in v7:
time: 134 us; the launch traced here: 133 us
  starting transfers between devices  70.3 us (52%)
  blocking collectives  23.3 us (17%)
  Pallas kernels  15.6 us (12%)
  local copies, waits for them, and re-layouts  14.3 us (11%)
  waiting for transfers between devices  6.41 us (5%)
  other arithmetic  2.41 us (2%)
    ppermute x7, starting transfers between devices, onward(): return lax.ppermute(block, ('ctx', 'ch'), route)  29.9 us
    all_to_all x1, blocking collectives, per_device(): lax.all_to_all(sent.reshape(2 * blocks, MODES, LANES), ('ctx', 'ch'), 0,...  23.3 us
    ppermute x6, starting transfers between devices, beside(): lax.ppermute(block, 'ch', [(z * ring + y, (z ^ step) * ring + y) for z in...  16.2 us
    ppermute x5, starting transfers between devices, other_core(): return lax.ppermute(block, 'ctx', [(i, i ^ 1) for i in range(blocks)])  12.2 us
    ppermute x1, starting transfers between devices, per_device(): lax.ppermute(tokens[rows - HALO:], 'ctx', [(i, i + 1) for i in range(bloc...  12 us
    pallas_call x2, Pallas kernels, local_part(): pl.pallas_call(functools.partial(local_kernel, len(blocks), len(in_weight...  8.58 us
    unnamed x40, local copies, waits for them, and re-layouts  8.23 us
    pallas_call x3, Pallas kernels, project(): pl.pallas_call(functools.partial(project_kernel, len(blocks), len(in_weig...  4.91 us
  transfers between devices with their start and end apart: 19, of which 5 were waited for; matrix products, arithmetic and copies ran while one was open for 6% of the time, Pallas kernels for 6%

profile of v7, /device:TPU:1, one launch (start us, length us, event | category | flops | bytes accessed | tf_op | source)
XLA Modules:
  0.0 132.8 jit_solution(14285919727210495669)
XLA Ops:
  0.7 12.0 %collective-permute-start.1 = (bf16[16,128]{1,0:T(8,128)(2,1)S(1)}, bf16[16,128]{1,0:T(8,128)(2,1)S(1)}, u32[]{:S(2)}, u32[]{:S(2)}) collective-permute-start(bf16[16,128]{1,0:T(8,128)(2,1)S(1)} %slice.33), channel_id=1, source_target_pairs={{0,32},{32,64},{64,96},{96,128},{128,160},{160,192},{192,224},{224... | collective-permute-start | bytes 12296 | tf_op jit(solution)/shard_map/ppermute | solution.py:253
  14.9 3.1 %collective-permute-start = (f32[54,128]{1,0:T(8,128)S(1)}, f32[54,128]{1,0:T(8,128)S(1)}, u32[]{:S(2)}, u32[]{:S(2)}) collective-permute-start(f32[54,128]{1,0:T(8,128)S(1)} %pad_maximum_fusion.3), channel_id=1, source_target_pairs={{0,8},{1,9},{2,10},{3,11},{4,12},{5,13},{6,14},{7,15},{8,0},{9,1},... | collective-permute-start | bytes 82952 | tf_op jit(solution)/shard_map/ppermute | solution.py:221
  19.9 4.0 %collective-permute-start.5 = (bf16[528,128]{1,0:T(8,128)(2,1)S(1)}, bf16[528,128]{1,0:T(8,128)(2,1)S(1)}, u32[]{:S(2)}, u32[]{:S(2)}) collective-permute-start(bf16[528,128]{1,0:T(8,128)(2,1)S(1)} %pad_maximum_fusion.1), channel_id=1, source_target_pairs={{0,24},{1,25},{2,26},{3,27},{4,28},{5,29},{6,30},{7,31},{8,16},{9,... | collective-permute-start | bytes 405512 | tf_op jit(solution)/shard_map/ppermute | solution.py:221
  23.9 2.2 %collective-permute-start.2 = (bf16[528,128]{1,0:T(8,128)(2,1)S(1)}, bf16[528,128]{1,0:T(8,128)(2,1)S(1)}, u32[]{:S(2)}, u32[]{:S(2)}) collective-permute-start(bf16[528,128]{1,0:T(8,128)(2,1)S(1)} %pad_maximum_fusion.1), channel_id=1, source_target_pairs={{0,8},{1,9},{2,10},{3,11},{4,12},{5,13},{6,14},{7,15},{8,0},{9,1},... | collective-permute-start | bytes 405512 | tf_op jit(solution)/shard_map/ppermute | solution.py:221
  26.1 3.1 %collective-permute-start.4 = (bf16[528,128]{1,0:T(8,128)(2,1)S(1)}, bf16[528,128]{1,0:T(8,128)(2,1)S(1)}, u32[]{:S(2)}, u32[]{:S(2)}) collective-permute-start(bf16[528,128]{1,0:T(8,128)(2,1)S(1)} %pad_maximum_fusion.2), channel_id=1, source_target_pairs={{0,16},{1,17},{2,18},{3,19},{4,20},{5,21},{6,22},{7,23},{8,24},{9,... | collective-permute-start | bytes 405512 | tf_op jit(solution)/shard_map/ppermute | solution.py:221
  29.2 2.8 %constant_dynamic-slice_fusion = bf16[3,2048,128]{2,1,0:T(8,128)(2,1)} fusion(bf16[3,4096,128]{2,1,0:T(8,128)(2,1)} %refs_1_.1, s32[]{:T(128)S(6)} %select_n.56), kind=kLoop, calls=%fused_computation.14 | loop fusion | bytes 3145732 | tf_op jit(solution)/shard_map/dynamic_slice | solution.py:261
  32.1 2.2 %collective-permute-done.4 = bf16[528,128]{1,0:T(8,128)(2,1)S(1)} collective-permute-done((bf16[528,128]{1,0:T(8,128)(2,1)S(1)}, bf16[528,128]{1,0:T(8,128)(2,1)S(1)}, u32[]{:S(2)}, u32[]{:S(2)}) %collective-permute-start.4) | collective-permute-done | bytes 135200 | tf_op jit(solution)/shard_map/ppermute | solution.py:221
  34.3 1.9 %collective-permute-start.7 = (bf16[528,512]{1,0:T(8,128)(2,1)S(1)}, bf16[528,512]{1,0:T(8,128)(2,1)S(1)}, u32[]{:S(2)}, u32[]{:S(2)}) collective-permute-start(bf16[528,512]{1,0:T(8,128)(2,1)S(1)} %pad_maximum_fusion.refs_1_.refs_2_), channel_id=1, source_target_pairs={{0,32},{32,0},{64,96},{96,64},{128,160},{160,128},{192,224},{224,1... | collective-permute-start | bytes 1622024 | tf_op jit(solution)/shard_map/ppermute | solution.py:235
  36.3 5.1 %collective-permute-start.6 = (bf16[528,512]{1,0:T(8,128)(2,1)S(1)}, bf16[528,512]{1,0:T(8,128)(2,1)}, u32[]{:S(2)}, u32[]{:S(2)}) collective-permute-start(bf16[528,512]{1,0:T(8,128)(2,1)S(1)} %pad_maximum_fusion.refs_1_.refs_2_), channel_id=1, source_target_pairs={{0,1},{1,2},{2,3},{3,4},{4,5},{5,6},{6,7},{7,0},{8,9},{9,10},{10,1... | collective-permute-start | bytes 1622024 | tf_op jit(solution)/shard_map/ppermute | solution.py:232
  42.2 3.0 %collective-permute-start.9 = (bf16[528,512]{1,0:T(8,128)(2,1)S(1)}, bf16[528,512]{1,0:T(8,128)(2,1)}, u32[]{:S(2)}, u32[]{:S(2)}) collective-permute-start(bf16[528,512]{1,0:T(8,128)(2,1)S(1)} %collective-permute-done.7), channel_id=1, source_target_pairs={{0,1},{1,2},{2,3},{3,4},{4,5},{5,6},{6,7},{7,0},{8,9},{9,10},{10,1... | collective-permute-start | bytes 1622024 | tf_op jit(solution)/shard_map/ppermute | solution.py:232
  45.2 1.9 %collective-permute-start.3 = (bf16[3,2048,128]{2,1,0:T(8,128)(2,1)}, bf16[3,2048,128]{2,1,0:T(8,128)(2,1)}, u32[]{:S(2)}, u32[]{:S(2)}) collective-permute-start(bf16[3,2048,128]{2,1,0:T(8,128)(2,1)} %constant_dynamic-slice_fusion), channel_id=1, source_target_pairs={{0,8},{1,9},{2,10},{3,11},{4,12},{5,13},{6,14},{7,15},{8,0},{9,1},... | collective-permute-start | bytes 4718600 | tf_op jit(solution)/shard_map/ppermute | solution.py:221
  47.6 5.1 %collective-permute-start.8 = (bf16[528,512]{1,0:T(8,128)(2,1)}, bf16[528,512]{1,0:T(8,128)(2,1)}, u32[]{:S(2)}, u32[]{:S(2)}) collective-permute-start(bf16[528,512]{1,0:T(8,128)(2,1)} %collective-permute-done.6.refs_1_.refs_3_), channel_id=1, source_target_pairs={{0,1},{1,2},{2,3},{3,4},{4,5},{5,6},{6,7},{7,0},{8,9},{9,10},{10,1... | collective-permute-start | bytes 1622024 | tf_op jit(solution)/shard_map/ppermute | solution.py:232
  53.4 5.1 %collective-permute-start.12 = (bf16[528,512]{1,0:T(8,128)(2,1)}, bf16[528,512]{1,0:T(8,128)(2,1)}, u32[]{:S(2)}, u32[]{:S(2)}) collective-permute-start(bf16[528,512]{1,0:T(8,128)(2,1)} %collective-permute-done.9), channel_id=1, source_target_pairs={{0,1},{1,2},{2,3},{3,4},{4,5},{5,6},{6,7},{7,0},{8,9},{9,10},{10,1... | collective-permute-start | bytes 1622024 | tf_op jit(solution)/shard_map/ppermute | solution.py:232
  63.3 3.6 %collective-permute-start.10 = (bf16[528,512]{1,0:T(8,128)(2,1)}, bf16[528,512]{1,0:T(8,128)(2,1)S(1)}, u32[]{:S(2)}, u32[]{:S(2)}) collective-permute-start(bf16[528,512]{1,0:T(8,128)(2,1)} %collective-permute-done.8.refs_1_.refs_5_), channel_id=1, source_target_pairs={{0,1},{1,2},{2,3},{3,4},{4,5},{5,6},{6,7},{7,0},{8,9},{9,10},{10,1... | collective-permute-start | bytes 1622024 | tf_op jit(solution)/shard_map/ppermute | solution.py:232
  66.8 3.3 %collective-permute-start.14 = (bf16[528,512]{1,0:T(8,128)(2,1)}, bf16[528,512]{1,0:T(8,128)(2,1)S(1)}, u32[]{:S(2)}, u32[]{:S(2)}) collective-permute-start(bf16[528,512]{1,0:T(8,128)(2,1)} %collective-permute-done.12), channel_id=1, source_target_pairs={{0,1},{1,2},{2,3},{3,4},{4,5},{5,6},{6,7},{7,0},{8,9},{9,10},{10,1... | collective-permute-start | bytes 1622024 | tf_op jit(solution)/shard_map/ppermute | solution.py:232
  72.1 2.0 %shard_map.74.refs_3_ = f32[3,528,128]{2,1,0:T(8,128)S(1)} custom-call(s32[64]{0:T(128)S(1)} %dynamic-slice_bitcast_fusion.ids, bf16[3,4096,128]{2,1,0:T(8,128)(2,1)S(1)} %copy-done, bf16[528,512]{1,0:T(8,128)(2,1)} %collective-permute-done.6.refs_1_.refs_3_, ...), custom_call_target="tpu_custom_call", output_to_operand_aliasing={{}: (4, {})} | custom-call | flops 528 | bytes 528 | tf_op jit(solution)/shard_map/pallas_call | solution.py:62
  75.0 4.7 %collective-permute-start.13 = (bf16[528,512]{1,0:T(8,128)(2,1)S(1)}, bf16[528,512]{1,0:T(8,128)(2,1)S(1)}, u32[]{:S(2)}, u32[]{:S(2)}) collective-permute-start(bf16[528,512]{1,0:T(8,128)(2,1)S(1)} %collective-permute-done.10.refs_2_.refs_7_), channel_id=1, source_target_pairs={{0,1},{1,2},{2,3},{3,4},{4,5},{5,6},{6,7},{7,0},{8,9},{9,10},{10,1... | collective-permute-start | bytes 1622024 | tf_op jit(solution)/shard_map/ppermute | solution.py:232
  81.3 2.2 %collective-permute-done.3.refs_0_ = bf16[3,2048,128]{2,1,0:T(8,128)(2,1)} collective-permute-done((bf16[3,2048,128]{2,1,0:T(8,128)(2,1)}, bf16[3,2048,128]{2,1,0:T(8,128)(2,1)}, u32[]{:S(2)}, u32[]{:S(2)}) %collective-permute-start.3) | collective-permute-done | bytes 1572896 | tf_op jit(solution)/shard_map/ppermute | solution.py:221
  83.5 2.2 %collective-permute-start.16 = (bf16[528,512]{1,0:T(8,128)(2,1)S(1)}, bf16[528,512]{1,0:T(8,128)(2,1)S(1)}, u32[]{:S(2)}, u32[]{:S(2)}) collective-permute-start(bf16[528,512]{1,0:T(8,128)(2,1)S(1)} %collective-permute-done.14), channel_id=1, source_target_pairs={{0,32},{32,0},{64,96},{96,64},{128,160},{160,128},{192,224},{224,1... | collective-permute-start | bytes 1622024 | tf_op jit(solution)/shard_map/ppermute | solution.py:235
  88.3 4.2 %collective-permute-start.17 = (bf16[3,2048,128]{2,1,0:T(8,128)(2,1)}, bf16[3,2048,128]{2,1,0:T(8,128)(2,1)}, u32[]{:S(2)}, u32[]{:S(2)}) collective-permute-start(bf16[3,2048,128]{2,1,0:T(8,128)(2,1)} %collective-permute-done.3.refs_0_), channel_id=1, source_target_pairs={{0,32},{32,0},{64,96},{96,64},{128,160},{160,128},{192,224},{224,1... | collective-permute-start | bytes 4718600 | tf_op jit(solution)/shard_map/ppermute | solution.py:235
  96.9 2.8 %shard_map.76 = (f32[1168,128]{1,0:T(8,128)S(1)}, f32[2,16,16,128]{3,2,1,0:T(8,128)S(1)}) custom-call(s32[3]{0:T(128)S(1)} %pad_add_fusion.seat, s32[64]{0:T(128)S(1)} %dynamic-slice_bitcast_fusion.ids, f32[3,7,128]{2,1,0:T(8,128)S(1)} %copy-done.18, f32[16,128]{1,0:T(8,128)S(1)} %multiply_bitcast_fusion.weights, f32[16,128]{1,0:T(8,128)S(1)} %bitcast.20, ...), custom_call_target="tpu_custom_call" | custom-call | flops 7208960 | bytes 1310720 | tf_op jit(solution)/shard_map/pallas_call | solution.py:136
  99.7 5.8 %shard_map.77 = (f32[1168,128]{1,0:T(8,128)S(1)}, f32[2,16,16,128]{3,2,1,0:T(8,128)S(1)}) custom-call(s32[3]{0:T(128)S(1)} %pad_add_fusion.2.seat, s32[64]{0:T(128)S(1)} %dynamic-slice_bitcast_fusion.ids, f32[3,7,128]{2,1,0:T(8,128)S(1)} %reshape.22.taps, f32[16,128]{1,0:T(8,128)S(1)} %get-tuple-element.58.weights, ...), custom_call_target="tpu_custom_call", output_to_operand_aliasing={{1}: (16, {})} | custom-call | flops 7208960 | bytes 1310720 | tf_op jit(solution)/shard_map/pallas_call | solution.py:136
  107.5 23.3 %all_to_all.5.arrived = f32[32,16,128]{2,1,0:T(8,128)S(1)} all-to-all(f32[32,16,128]{2,1,0:T(8,128)S(1)} %bitcast.18), channel_id=1, replica_groups={{0,32,64,96,128,160,192,224,256,288,320,352,384,416,448,480,8,40,72,104..., dimensions={0} | all-to-all | bytes 524288 | tf_op jit(solution)/shard_map/all_to_all | solution.py:307
  130.7 2.1 %shard_map.78 = f32[1024,128]{1,0:T(8,128)} custom-call(s32[3]{0:T(128)S(1)} %pad_add_fusion.seat, f32[32,16,128]{2,1,0:T(8,128)S(1)} %all_to_all.5.arrived, f32[1168,128]{1,0:T(8,128)S(1)} %get-tuple-element.51.mine, f32[1168,128]{1,0:T(8,128)S(1)} %collective-permute-done.18.other, f32[16,128]{1,0:T(8,128)S(1)} %multiply_bitcast_fusion.weights, ...), custom_call_target="tpu_custom_call" | custom-call | flops 4718592 | bytes 1572864 | tf_op jit(solution)/shard_map/pallas_call | solution.py:196
  (79 shorter events, 24.6 us)
Async XLA Ops:
  0.7 18.5 %collective-permute-start.1 = (bf16[16,128]{1,0:T(8,128)(2,1)S(1)}, bf16[16,128]{1,0:T(8,128)(2,1)S(1)}, u32[]{:S(2)}, u32[]{:S(2)}) collective-permute-start(bf16[16,128]{1,0:T(8,128)(2,1)S(1)} %slice.33), channel_id=1, source_target_pairs={{0,32},{32,64},{64,96},{96,128},{128,160},{160,192},{192,224},{224... | collective-permute-start | bytes 12296 | tf_op jit(solution)/shard_map/ppermute | solution.py:253
  14.9 19.4 %collective-permute-start = (f32[54,128]{1,0:T(8,128)S(1)}, f32[54,128]{1,0:T(8,128)S(1)}, u32[]{:S(2)}, u32[]{:S(2)}) collective-permute-start(f32[54,128]{1,0:T(8,128)S(1)} %pad_maximum_fusion.3), channel_id=1, source_target_pairs={{0,8},{1,9},{2,10},{3,11},{4,12},{5,13},{6,14},{7,15},{8,0},{9,1},... | collective-permute-start | bytes 82952 | tf_op jit(solution)/shard_map/ppermute | solution.py:221
  19.9 14.3 %collective-permute-start.5 = (bf16[528,128]{1,0:T(8,128)(2,1)S(1)}, bf16[528,128]{1,0:T(8,128)(2,1)S(1)}, u32[]{:S(2)}, u32[]{:S(2)}) collective-permute-start(bf16[528,128]{1,0:T(8,128)(2,1)S(1)} %pad_maximum_fusion.1), channel_id=1, source_target_pairs={{0,24},{1,25},{2,26},{3,27},{4,28},{5,29},{6,30},{7,31},{8,16},{9,... | collective-permute-start | bytes 405512 | tf_op jit(solution)/shard_map/ppermute | solution.py:221
  23.9 10.3 %collective-permute-start.2 = (bf16[528,128]{1,0:T(8,128)(2,1)S(1)}, bf16[528,128]{1,0:T(8,128)(2,1)S(1)}, u32[]{:S(2)}, u32[]{:S(2)}) collective-permute-start(bf16[528,128]{1,0:T(8,128)(2,1)S(1)} %pad_maximum_fusion.1), channel_id=1, source_target_pairs={{0,8},{1,9},{2,10},{3,11},{4,12},{5,13},{6,14},{7,15},{8,0},{9,1},... | collective-permute-start | bytes 405512 | tf_op jit(solution)/shard_map/ppermute | solution.py:221
  26.1 8.1 %collective-permute-start.4 = (bf16[528,128]{1,0:T(8,128)(2,1)S(1)}, bf16[528,128]{1,0:T(8,128)(2,1)S(1)}, u32[]{:S(2)}, u32[]{:S(2)}) collective-permute-start(bf16[528,128]{1,0:T(8,128)(2,1)S(1)} %pad_maximum_fusion.2), channel_id=1, source_target_pairs={{0,16},{1,17},{2,18},{3,19},{4,20},{5,21},{6,22},{7,23},{8,24},{9,... | collective-permute-start | bytes 405512 | tf_op jit(solution)/shard_map/ppermute | solution.py:221
  29.2 30.1 %copy-start = (bf16[3,4096,128]{2,1,0:T(8,128)(2,1)S(1)}, bf16[3,4096,128]{2,1,0:T(8,128)(2,1)}, u32[]{:S(2)}) copy-start(bf16[3,4096,128]{2,1,0:T(8,128)(2,1)} %refs_1_.1) | copy-start | bytes 9437188
  34.3 7.8 %collective-permute-start.7 = (bf16[528,512]{1,0:T(8,128)(2,1)S(1)}, bf16[528,512]{1,0:T(8,128)(2,1)S(1)}, u32[]{:S(2)}, u32[]{:S(2)}) collective-permute-start(bf16[528,512]{1,0:T(8,128)(2,1)S(1)} %pad_maximum_fusion.refs_1_.refs_2_), channel_id=1, source_target_pairs={{0,32},{32,0},{64,96},{96,64},{128,160},{160,128},{192,224},{224,1... | collective-permute-start | bytes 1622024 | tf_op jit(solution)/shard_map/ppermute | solution.py:235
  36.3 11.4 %collective-permute-start.6 = (bf16[528,512]{1,0:T(8,128)(2,1)S(1)}, bf16[528,512]{1,0:T(8,128)(2,1)}, u32[]{:S(2)}, u32[]{:S(2)}) collective-permute-start(bf16[528,512]{1,0:T(8,128)(2,1)S(1)} %pad_maximum_fusion.refs_1_.refs_2_), channel_id=1, source_target_pairs={{0,1},{1,2},{2,3},{3,4},{4,5},{5,6},{6,7},{7,0},{8,9},{9,10},{10,1... | collective-permute-start | bytes 1622024 | tf_op jit(solution)/shard_map/ppermute | solution.py:232
  42.2 11.3 %collective-permute-start.9 = (bf16[528,512]{1,0:T(8,128)(2,1)S(1)}, bf16[528,512]{1,0:T(8,128)(2,1)}, u32[]{:S(2)}, u32[]{:S(2)}) collective-permute-start(bf16[528,512]{1,0:T(8,128)(2,1)S(1)} %collective-permute-done.7), channel_id=1, source_target_pairs={{0,1},{1,2},{2,3},{3,4},{4,5},{5,6},{6,7},{7,0},{8,9},{9,10},{10,1... | collective-permute-start | bytes 1622024 | tf_op jit(solution)/shard_map/ppermute | solution.py:232
  45.2 38.4 %collective-permute-start.3 = (bf16[3,2048,128]{2,1,0:T(8,128)(2,1)}, bf16[3,2048,128]{2,1,0:T(8,128)(2,1)}, u32[]{:S(2)}, u32[]{:S(2)}) collective-permute-start(bf16[3,2048,128]{2,1,0:T(8,128)(2,1)} %constant_dynamic-slice_fusion), channel_id=1, source_target_pairs={{0,8},{1,9},{2,10},{3,11},{4,12},{5,13},{6,14},{7,15},{8,0},{9,1},... | collective-permute-start | bytes 4718600 | tf_op jit(solution)/shard_map/ppermute | solution.py:221
  47.6 15.6 %collective-permute-start.8 = (bf16[528,512]{1,0:T(8,128)(2,1)}, bf16[528,512]{1,0:T(8,128)(2,1)}, u32[]{:S(2)}, u32[]{:S(2)}) collective-permute-start(bf16[528,512]{1,0:T(8,128)(2,1)} %collective-permute-done.6.refs_1_.refs_3_), channel_id=1, source_target_pairs={{0,1},{1,2},{2,3},{3,4},{4,5},{5,6},{6,7},{7,0},{8,9},{9,10},{10,1... | collective-permute-start | bytes 1622024 | tf_op jit(solution)/shard_map/ppermute | solution.py:232
  53.4 13.4 %collective-permute-start.12 = (bf16[528,512]{1,0:T(8,128)(2,1)}, bf16[528,512]{1,0:T(8,128)(2,1)}, u32[]{:S(2)}, u32[]{:S(2)}) collective-permute-start(bf16[528,512]{1,0:T(8,128)(2,1)} %collective-permute-done.9), channel_id=1, source_target_pairs={{0,1},{1,2},{2,3},{3,4},{4,5},{5,6},{6,7},{7,0},{8,9},{9,10},{10,1... | collective-permute-start | bytes 1622024 | tf_op jit(solution)/shard_map/ppermute | solution.py:232
  61.3 10.8 %collective-permute-start.11 = (bf16[528,512]{1,0:T(8,128)(2,1)}, bf16[528,512]{1,0:T(8,128)(2,1)S(1)}, u32[]{:S(2)}, u32[]{:S(2)}) collective-permute-start(bf16[528,512]{1,0:T(8,128)(2,1)} %collective-permute-done.9), channel_id=1, source_target_pairs={{0,32},{32,0},{64,96},{96,64},{128,160},{160,128},{192,224},{224,1... | collective-permute-start | bytes 1622024 | tf_op jit(solution)/shard_map/ppermute | solution.py:235
  63.3 11.8 %collective-permute-start.10 = (bf16[528,512]{1,0:T(8,128)(2,1)}, bf16[528,512]{1,0:T(8,128)(2,1)S(1)}, u32[]{:S(2)}, u32[]{:S(2)}) collective-permute-start(bf16[528,512]{1,0:T(8,128)(2,1)} %collective-permute-done.8.refs_1_.refs_5_), channel_id=1, source_target_pairs={{0,1},{1,2},{2,3},{3,4},{4,5},{5,6},{6,7},{7,0},{8,9},{9,10},{10,1... | collective-permute-start | bytes 1622024 | tf_op jit(solution)/shard_map/ppermute | solution.py:232
  66.8 13.7 %collective-permute-start.14 = (bf16[528,512]{1,0:T(8,128)(2,1)}, bf16[528,512]{1,0:T(8,128)(2,1)S(1)}, u32[]{:S(2)}, u32[]{:S(2)}) collective-permute-start(bf16[528,512]{1,0:T(8,128)(2,1)} %collective-permute-done.12), channel_id=1, source_target_pairs={{0,1},{1,2},{2,3},{3,4},{4,5},{5,6},{6,7},{7,0},{8,9},{9,10},{10,1... | collective-permute-start | bytes 1622024 | tf_op jit(solution)/shard_map/ppermute | solution.py:232
  70.2 10.3 %collective-permute-start.15 = (bf16[528,512]{1,0:T(8,128)(2,1)}, bf16[528,512]{1,0:T(8,128)(2,1)S(1)}, u32[]{:S(2)}, u32[]{:S(2)}) collective-permute-start(bf16[528,512]{1,0:T(8,128)(2,1)} %collective-permute-done.12), channel_id=1, source_target_pairs={{0,32},{32,0},{64,96},{96,64},{128,160},{160,128},{192,224},{224,1... | collective-permute-start | bytes 1622024 | tf_op jit(solution)/shard_map/ppermute | solution.py:235
  72.1 2.0 %copy-start.6 = (bf16[528,512]{1,0:T(8,128)(2,1)}, bf16[528,512]{1,0:T(8,128)(2,1)S(1)}, u32[]{:S(2)}) copy-start(bf16[528,512]{1,0:T(8,128)(2,1)S(1)} %collective-permute-done.11.refs_2_.refs_4_) | copy-start | bytes 1622020
  75.0 11.5 %collective-permute-start.13 = (bf16[528,512]{1,0:T(8,128)(2,1)S(1)}, bf16[528,512]{1,0:T(8,128)(2,1)S(1)}, u32[]{:S(2)}, u32[]{:S(2)}) collective-permute-start(bf16[528,512]{1,0:T(8,128)(2,1)S(1)} %collective-permute-done.10.refs_2_.refs_7_), channel_id=1, source_target_pairs={{0,1},{1,2},{2,3},{3,4},{4,5},{5,6},{6,7},{7,0},{8,9},{9,10},{10,1... | collective-permute-start | bytes 1622024 | tf_op jit(solution)/shard_map/ppermute | solution.py:232
  83.5 3.9 %collective-permute-start.16 = (bf16[528,512]{1,0:T(8,128)(2,1)S(1)}, bf16[528,512]{1,0:T(8,128)(2,1)S(1)}, u32[]{:S(2)}, u32[]{:S(2)}) collective-permute-start(bf16[528,512]{1,0:T(8,128)(2,1)S(1)} %collective-permute-done.14), channel_id=1, source_target_pairs={{0,32},{32,0},{64,96},{96,64},{128,160},{160,128},{192,224},{224,1... | collective-permute-start | bytes 1622024 | tf_op jit(solution)/shard_map/ppermute | solution.py:235
  88.3 11.4 %collective-permute-start.17 = (bf16[3,2048,128]{2,1,0:T(8,128)(2,1)}, bf16[3,2048,128]{2,1,0:T(8,128)(2,1)}, u32[]{:S(2)}, u32[]{:S(2)}) collective-permute-start(bf16[3,2048,128]{2,1,0:T(8,128)(2,1)} %collective-permute-done.3.refs_0_), channel_id=1, source_target_pairs={{0,32},{32,0},{64,96},{96,64},{128,160},{160,128},{192,224},{224,1... | collective-permute-start | bytes 4718600 | tf_op jit(solution)/shard_map/ppermute | solution.py:235
  96.9 2.8 %copy-start.5 = (bf16[528,512]{1,0:T(8,128)(2,1)S(1)}, bf16[528,512]{1,0:T(8,128)(2,1)}, u32[]{:S(2)}) copy-start(bf16[528,512]{1,0:T(8,128)(2,1)} %copy-done.3) | copy-start | bytes 1622020
  96.9 2.8 %copy-start.7 = (bf16[528,512]{1,0:T(8,128)(2,1)S(1)}, bf16[528,512]{1,0:T(8,128)(2,1)}, u32[]{:S(2)}) copy-start(bf16[528,512]{1,0:T(8,128)(2,1)} %copy-done.6) | copy-start | bytes 1622020
  96.9 2.8 %copy-start.10 = (bf16[528,512]{1,0:T(8,128)(2,1)S(1)}, bf16[528,512]{1,0:T(8,128)(2,1)}, u32[]{:S(2)}) copy-start(bf16[528,512]{1,0:T(8,128)(2,1)} %copy-done.8) | copy-start | bytes 1622020
  105.5 25.2 %collective-permute-start.18 = (f32[1168,128]{1,0:T(8,128)S(1)}, f32[1168,128]{1,0:T(8,128)S(1)}, u32[]{:S(2)}, u32[]{:S(2)}) collective-permute-start(f32[1168,128]{1,0:T(8,128)S(1)} %get-tuple-element.52), channel_id=1, source_target_pairs={{0,8},{1,9},{2,10},{3,11},{4,12},{5,13},{6,14},{7,15},{8,0},{9,1},... | collective-permute-start | bytes 1794056 | tf_op jit(solution)/shard_map/ppermute | solution.py:221
  (15 other events, 20.1 us)

commit v8 on v7

--- a/solution.py
+++ b/solution.py
@@ -260,6 +260,7 @@
     count = in_weights.shape[1] // 2
     sliced = lax.dynamic_slice_in_dim(in_weights, mine % 2 * count, count, 1)
     values = jnp.concatenate([short_taps.reshape(3 * TAPS, -1), weights, rates, skip_gain[None, :]], axis=0)
+    values = after(values, before)
     half_weights, values = beside(after(sliced, nearest), 1), beside(values, 1)
     block = jnp.concatenate([kept, nearest, beside(kept, 2), beside(given, 3)], axis=1)
 

time: 134 us -> 137 us (1.022)
  other arithmetic: 2.41 us -> 4.26 us
    unnamed x40 -> x42, local copies, waits for them, and re-layouts: 8.23 us -> 8.24 us
where the time goes in v8:
time: 137 us; the launch traced here: 136 us
  starting transfers between devices  70.3 us (51%)
  blocking collectives  23.6 us (17%)
  Pallas kernels  15.6 us (11%)
  local copies, waits for them, and re-layouts  14.3 us (10%)
  waiting for transfers between devices  7.16 us (5%)
  other arithmetic  4.26 us (3%)
    ppermute x7, starting transfers between devices, onward(): return lax.ppermute(block, ('ctx', 'ch'), route)  29.9 us
    all_to_all x1, blocking collectives, per_device(): lax.all_to_all(sent.reshape(2 * blocks, MODES, LANES), ('ctx', 'ch'), 0,...  23.6 us
    ppermute x6, starting transfers between devices, beside(): lax.ppermute(block, 'ch', [(z * ring + y, (z ^ step) * ring + y) for z in...  16.1 us
    ppermute x5, starting transfers between devices, other_core(): return lax.ppermute(block, 'ctx', [(i, i ^ 1) for i in range(blocks)])  12.2 us
    ppermute x1, starting transfers between devices, per_device(): lax.ppermute(tokens[rows - HALO:], 'ctx', [(i, i + 1) for i in range(bloc...  12 us
    pallas_call x2, Pallas kernels, local_part(): pl.pallas_call(functools.partial(local_kernel, len(blocks), len(in_weight...  8.61 us
    unnamed x42, local copies, waits for them, and re-layouts  8.24 us
    ppermute x6, waiting for transfers between devices, beside(): lax.ppermute(block, 'ch', [(z * ring + y, (z ^ step) * ring + y) for z in...  5.21 us
  transfers between devices with their start and end apart: 19, of which 5 were waited for; matrix products, arithmetic and copies ran while one was open for 6% of the time, Pallas kernels for 6%

profile of v8, /device:TPU:1, one launch (start us, length us, event | category | flops | bytes accessed | tf_op | source)
XLA Modules:
  0.0 135.7 jit_solution(13785418253890828523)
XLA Ops:
  0.7 12.0 %collective-permute-start = (bf16[16,128]{1,0:T(8,128)(2,1)S(1)}, bf16[16,128]{1,0:T(8,128)(2,1)S(1)}, u32[]{:S(2)}, u32[]{:S(2)}) collective-permute-start(bf16[16,128]{1,0:T(8,128)(2,1)S(1)} %slice.28), channel_id=1, source_target_pairs={{0,32},{32,64},{64,96},{96,128},{128,160},{160,192},{192,224},{224... | collective-permute-start | bytes 12296 | tf_op jit(solution)/shard_map/ppermute | solution.py:253
  14.6 2.8 %constant_dynamic-slice_fusion = bf16[3,2048,128]{2,1,0:T(8,128)(2,1)} fusion(bf16[3,4096,128]{2,1,0:T(8,128)(2,1)} %refs_1_.1, s32[]{:T(128)S(6)} %select_n.56), kind=kLoop, calls=%fused_computation.14 | loop fusion | bytes 3145732 | tf_op jit(solution)/shard_map/dynamic_slice | solution.py:261
  19.8 4.9 %collective-permute-start.5 = (bf16[528,128]{1,0:T(8,128)(2,1)}, bf16[528,128]{1,0:T(8,128)(2,1)S(1)}, u32[]{:S(2)}, u32[]{:S(2)}) collective-permute-start(bf16[528,128]{1,0:T(8,128)(2,1)} %pad_maximum_fusion.1), channel_id=1, source_target_pairs={{0,24},{1,25},{2,26},{3,27},{4,28},{5,29},{6,30},{7,31},{8,16},{9,... | collective-permute-start | bytes 405512 | tf_op jit(solution)/shard_map/ppermute | solution.py:221
  24.7 1.9 %collective-permute-start.2 = (bf16[528,128]{1,0:T(8,128)(2,1)}, bf16[528,128]{1,0:T(8,128)(2,1)}, u32[]{:S(2)}, u32[]{:S(2)}) collective-permute-start(bf16[528,128]{1,0:T(8,128)(2,1)} %pad_maximum_fusion.1), channel_id=1, source_target_pairs={{0,8},{1,9},{2,10},{3,11},{4,12},{5,13},{6,14},{7,15},{8,0},{9,1},... | collective-permute-start | bytes 405512 | tf_op jit(solution)/shard_map/ppermute | solution.py:221
  27.3 2.4 %collective-permute-start.4 = (bf16[528,128]{1,0:T(8,128)(2,1)}, bf16[528,128]{1,0:T(8,128)(2,1)}, u32[]{:S(2)}, u32[]{:S(2)}) collective-permute-start(bf16[528,128]{1,0:T(8,128)(2,1)} %pad_maximum_fusion.2), channel_id=1, source_target_pairs={{0,16},{1,17},{2,18},{3,19},{4,20},{5,21},{6,22},{7,23},{8,24},{9,... | collective-permute-start | bytes 405512 | tf_op jit(solution)/shard_map/ppermute | solution.py:221
  29.9 2.9 %collective-permute-start.1 = (f32[54,128]{1,0:T(8,128)S(1)}, f32[54,128]{1,0:T(8,128)S(1)}, u32[]{:S(2)}, u32[]{:S(2)}) collective-permute-start(f32[54,128]{1,0:T(8,128)S(1)} %pad_maximum_fusion.3), channel_id=1, source_target_pairs={{0,8},{1,9},{2,10},{3,11},{4,12},{5,13},{6,14},{7,15},{8,0},{9,1},... | collective-permute-start | bytes 82952 | tf_op jit(solution)/shard_map/ppermute | solution.py:221
  32.7 3.0 %collective-permute-done.4 = bf16[528,128]{1,0:T(8,128)(2,1)} collective-permute-done((bf16[528,128]{1,0:T(8,128)(2,1)}, bf16[528,128]{1,0:T(8,128)(2,1)}, u32[]{:S(2)}, u32[]{:S(2)}) %collective-permute-start.4) | collective-permute-done | bytes 135200 | tf_op jit(solution)/shard_map/ppermute | solution.py:221
  38.7 5.1 %collective-permute-start.6 = (bf16[528,512]{1,0:T(8,128)(2,1)S(1)}, bf16[528,512]{1,0:T(8,128)(2,1)}, u32[]{:S(2)}, u32[]{:S(2)}) collective-permute-start(bf16[528,512]{1,0:T(8,128)(2,1)S(1)} %pad_maximum_fusion.refs_1_.refs_2_), channel_id=1, source_target_pairs={{0,1},{1,2},{2,3},{3,4},{4,5},{5,6},{6,7},{7,0},{8,9},{9,10},{10,1... | collective-permute-start | bytes 1622024 | tf_op jit(solution)/shard_map/ppermute | solution.py:232
  44.6 3.0 %collective-permute-start.9 = (bf16[528,512]{1,0:T(8,128)(2,1)S(1)}, bf16[528,512]{1,0:T(8,128)(2,1)}, u32[]{:S(2)}, u32[]{:S(2)}) collective-permute-start(bf16[528,512]{1,0:T(8,128)(2,1)S(1)} %collective-permute-done.7), channel_id=1, source_target_pairs={{0,1},{1,2},{2,3},{3,4},{4,5},{5,6},{6,7},{7,0},{8,9},{9,10},{10,1... | collective-permute-start | bytes 1622024 | tf_op jit(solution)/shard_map/ppermute | solution.py:232
  47.6 2.0 %collective-permute-start.3 = (bf16[3,2048,128]{2,1,0:T(8,128)(2,1)}, bf16[3,2048,128]{2,1,0:T(8,128)(2,1)}, u32[]{:S(2)}, u32[]{:S(2)}) collective-permute-start(bf16[3,2048,128]{2,1,0:T(8,128)(2,1)} %constant_dynamic-slice_fusion), channel_id=1, source_target_pairs={{0,8},{1,9},{2,10},{3,11},{4,12},{5,13},{6,14},{7,15},{8,0},{9,1},... | collective-permute-start | bytes 4718600 | tf_op jit(solution)/shard_map/ppermute | solution.py:221
  50.1 5.1 %collective-permute-start.8 = (bf16[528,512]{1,0:T(8,128)(2,1)}, bf16[528,512]{1,0:T(8,128)(2,1)}, u32[]{:S(2)}, u32[]{:S(2)}) collective-permute-start(bf16[528,512]{1,0:T(8,128)(2,1)} %collective-permute-done.6.refs_1_.refs_3_), channel_id=1, source_target_pairs={{0,1},{1,2},{2,3},{3,4},{4,5},{5,6},{6,7},{7,0},{8,9},{9,10},{10,1... | collective-permute-start | bytes 1622024 | tf_op jit(solution)/shard_map/ppermute | solution.py:232
  55.9 5.1 %collective-permute-start.12 = (bf16[528,512]{1,0:T(8,128)(2,1)}, bf16[528,512]{1,0:T(8,128)(2,1)}, u32[]{:S(2)}, u32[]{:S(2)}) collective-permute-start(bf16[528,512]{1,0:T(8,128)(2,1)} %collective-permute-done.9), channel_id=1, source_target_pairs={{0,1},{1,2},{2,3},{3,4},{4,5},{5,6},{6,7},{7,0},{8,9},{9,10},{10,1... | collective-permute-start | bytes 1622024 | tf_op jit(solution)/shard_map/ppermute | solution.py:232
  65.7 3.6 %collective-permute-start.10 = (bf16[528,512]{1,0:T(8,128)(2,1)}, bf16[528,512]{1,0:T(8,128)(2,1)S(1)}, u32[]{:S(2)}, u32[]{:S(2)}) collective-permute-start(bf16[528,512]{1,0:T(8,128)(2,1)} %collective-permute-done.8.refs_1_.refs_5_), channel_id=1, source_target_pairs={{0,1},{1,2},{2,3},{3,4},{4,5},{5,6},{6,7},{7,0},{8,9},{9,10},{10,1... | collective-permute-start | bytes 1622024 | tf_op jit(solution)/shard_map/ppermute | solution.py:232
  69.3 3.3 %collective-permute-start.14 = (bf16[528,512]{1,0:T(8,128)(2,1)}, bf16[528,512]{1,0:T(8,128)(2,1)S(1)}, u32[]{:S(2)}, u32[]{:S(2)}) collective-permute-start(bf16[528,512]{1,0:T(8,128)(2,1)} %collective-permute-done.12), channel_id=1, source_target_pairs={{0,1},{1,2},{2,3},{3,4},{4,5},{5,6},{6,7},{7,0},{8,9},{9,10},{10,1... | collective-permute-start | bytes 1622024 | tf_op jit(solution)/shard_map/ppermute | solution.py:232
  74.6 2.0 %shard_map.74.refs_3_ = f32[3,528,128]{2,1,0:T(8,128)S(1)} custom-call(s32[64]{0:T(128)S(1)} %dynamic-slice_bitcast_fusion.ids, bf16[3,4096,128]{2,1,0:T(8,128)(2,1)S(1)} %copy-done, bf16[528,512]{1,0:T(8,128)(2,1)} %collective-permute-done.6.refs_1_.refs_3_, ...), custom_call_target="tpu_custom_call", output_to_operand_aliasing={{}: (4, {})} | custom-call | flops 528 | bytes 528 | tf_op jit(solution)/shard_map/pallas_call | solution.py:62
  77.5 4.7 %collective-permute-start.13 = (bf16[528,512]{1,0:T(8,128)(2,1)S(1)}, bf16[528,512]{1,0:T(8,128)(2,1)S(1)}, u32[]{:S(2)}, u32[]{:S(2)}) collective-permute-start(bf16[528,512]{1,0:T(8,128)(2,1)S(1)} %collective-permute-done.10.refs_2_.refs_7_), channel_id=1, source_target_pairs={{0,1},{1,2},{2,3},{3,4},{4,5},{5,6},{6,7},{7,0},{8,9},{9,10},{10,1... | collective-permute-start | bytes 1622024 | tf_op jit(solution)/shard_map/ppermute | solution.py:232
  83.8 2.2 %collective-permute-done.3.refs_0_ = bf16[3,2048,128]{2,1,0:T(8,128)(2,1)} collective-permute-done((bf16[3,2048,128]{2,1,0:T(8,128)(2,1)}, bf16[3,2048,128]{2,1,0:T(8,128)(2,1)}, u32[]{:S(2)}, u32[]{:S(2)}) %collective-permute-start.3) | collective-permute-done | bytes 1572896 | tf_op jit(solution)/shard_map/ppermute | solution.py:221
  86.0 2.2 %collective-permute-start.16 = (bf16[528,512]{1,0:T(8,128)(2,1)S(1)}, bf16[528,512]{1,0:T(8,128)(2,1)S(1)}, u32[]{:S(2)}, u32[]{:S(2)}) collective-permute-start(bf16[528,512]{1,0:T(8,128)(2,1)S(1)} %collective-permute-done.14), channel_id=1, source_target_pairs={{0,32},{32,0},{64,96},{96,64},{128,160},{160,128},{192,224},{224,1... | collective-permute-start | bytes 1622024 | tf_op jit(solution)/shard_map/ppermute | solution.py:235
  90.7 4.2 %collective-permute-start.17 = (bf16[3,2048,128]{2,1,0:T(8,128)(2,1)}, bf16[3,2048,128]{2,1,0:T(8,128)(2,1)}, u32[]{:S(2)}, u32[]{:S(2)}) collective-permute-start(bf16[3,2048,128]{2,1,0:T(8,128)(2,1)} %collective-permute-done.3.refs_0_), channel_id=1, source_target_pairs={{0,32},{32,0},{64,96},{96,64},{128,160},{160,128},{192,224},{224,1... | collective-permute-start | bytes 4718600 | tf_op jit(solution)/shard_map/ppermute | solution.py:235
  99.3 2.8 %shard_map.76 = (f32[1168,128]{1,0:T(8,128)S(1)}, f32[2,16,16,128]{3,2,1,0:T(8,128)S(1)}) custom-call(s32[3]{0:T(128)S(1)} %pad_add_fusion.seat, s32[64]{0:T(128)S(1)} %dynamic-slice_bitcast_fusion.ids, f32[3,7,128]{2,1,0:T(8,128)S(1)} %copy-done.18, f32[16,128]{1,0:T(8,128)S(1)} %multiply_bitcast_fusion.weights, f32[16,128]{1,0:T(8,128)S(1)} %bitcast.20, ...), custom_call_target="tpu_custom_call" | custom-call | flops 7208960 | bytes 1310720 | tf_op jit(solution)/shard_map/pallas_call | solution.py:136
  102.1 5.9 %shard_map.77 = (f32[1168,128]{1,0:T(8,128)S(1)}, f32[2,16,16,128]{3,2,1,0:T(8,128)S(1)}) custom-call(s32[3]{0:T(128)S(1)} %pad_add_fusion.2.seat, s32[64]{0:T(128)S(1)} %dynamic-slice_bitcast_fusion.ids, f32[3,7,128]{2,1,0:T(8,128)S(1)} %reshape.22.taps, f32[16,128]{1,0:T(8,128)S(1)} %get-tuple-element.60.weights, ...), custom_call_target="tpu_custom_call", output_to_operand_aliasing={{1}: (16, {})} | custom-call | flops 7208960 | bytes 1310720 | tf_op jit(solution)/shard_map/pallas_call | solution.py:136
  108.0 2.0 %collective-permute-start.18 = (f32[1168,128]{1,0:T(8,128)S(1)}, f32[1168,128]{1,0:T(8,128)S(1)}, u32[]{:S(2)}, u32[]{:S(2)}) collective-permute-start(f32[1168,128]{1,0:T(8,128)S(1)} %get-tuple-element.54), channel_id=1, source_target_pairs={{0,8},{1,9},{2,10},{3,11},{4,12},{5,13},{6,14},{7,15},{8,0},{9,1},... | collective-permute-start | bytes 1794056 | tf_op jit(solution)/shard_map/ppermute | solution.py:221
  110.0 23.6 %all_to_all.5.arrived = f32[32,16,128]{2,1,0:T(8,128)S(1)} all-to-all(f32[32,16,128]{2,1,0:T(8,128)S(1)} %bitcast.18), channel_id=1, replica_groups={{0,32,64,96,128,160,192,224,256,288,320,352,384,416,448,480,8,40,72,104..., dimensions={0} | all-to-all | bytes 524288 | tf_op jit(solution)/shard_map/all_to_all | solution.py:308
  133.6 2.1 %shard_map.78 = f32[1024,128]{1,0:T(8,128)} custom-call(s32[3]{0:T(128)S(1)} %pad_add_fusion.seat, f32[32,16,128]{2,1,0:T(8,128)S(1)} %all_to_all.5.arrived, f32[1168,128]{1,0:T(8,128)S(1)} %get-tuple-element.53.mine, f32[1168,128]{1,0:T(8,128)S(1)} %collective-permute-done.18.other, f32[16,128]{1,0:T(8,128)S(1)} %multiply_bitcast_fusion.weights, ...), custom_call_target="tpu_custom_call" | custom-call | flops 4718592 | bytes 1572864 | tf_op jit(solution)/shard_map/pallas_call | solution.py:196
  (81 shorter events, 26.4 us)
Async XLA Ops:
  0.7 17.8 %collective-permute-start = (bf16[16,128]{1,0:T(8,128)(2,1)S(1)}, bf16[16,128]{1,0:T(8,128)(2,1)S(1)}, u32[]{:S(2)}, u32[]{:S(2)}) collective-permute-start(bf16[16,128]{1,0:T(8,128)(2,1)S(1)} %slice.28), channel_id=1, source_target_pairs={{0,32},{32,64},{64,96},{96,128},{128,160},{160,192},{192,224},{224... | collective-permute-start | bytes 12296 | tf_op jit(solution)/shard_map/ppermute | solution.py:253
  14.6 47.2 %copy-start = (bf16[3,4096,128]{2,1,0:T(8,128)(2,1)S(1)}, bf16[3,4096,128]{2,1,0:T(8,128)(2,1)}, u32[]{:S(2)}) copy-start(bf16[3,4096,128]{2,1,0:T(8,128)(2,1)} %refs_1_.1) | copy-start | bytes 9437188
  17.4 12.4 %copy-start.17 = (f32[128,16]{0,1:T(8,128)S(1)}, f32[128,16]{0,1:T(8,128)}, u32[]{:S(2)}) copy-start(f32[128,16]{0,1:T(8,128)} %param.11) | copy-start | bytes 24580
  17.4 12.4 %copy-start.20 = (f32[128,16]{0,1:T(8,128)S(1)}, f32[128,16]{0,1:T(8,128)}, u32[]{:S(2)}) copy-start(f32[128,16]{0,1:T(8,128)} %param.10) | copy-start | bytes 24580
  17.4 12.4 %copy-start.18 = (f32[3,7,128]{2,1,0:T(8,128)S(1)}, f32[3,7,128]{2,1,0:T(8,128)}, u32[]{:S(2)}) copy-start(f32[3,7,128]{2,1,0:T(8,128)} %taps.1) | copy-start | bytes 32260
  17.4 12.4 %copy-start.19 = (f32[128]{0:T(128)S(1)}, f32[128]{0:T(128)}, u32[]{:S(2)}) copy-start(f32[128]{0:T(128)} %param.12) | copy-start | bytes 1540
  19.8 15.9 %collective-permute-start.5 = (bf16[528,128]{1,0:T(8,128)(2,1)}, bf16[528,128]{1,0:T(8,128)(2,1)S(1)}, u32[]{:S(2)}, u32[]{:S(2)}) collective-permute-start(bf16[528,128]{1,0:T(8,128)(2,1)} %pad_maximum_fusion.1), channel_id=1, source_target_pairs={{0,24},{1,25},{2,26},{3,27},{4,28},{5,29},{6,30},{7,31},{8,16},{9,... | collective-permute-start | bytes 405512 | tf_op jit(solution)/shard_map/ppermute | solution.py:221
  24.7 11.0 %collective-permute-start.2 = (bf16[528,128]{1,0:T(8,128)(2,1)}, bf16[528,128]{1,0:T(8,128)(2,1)}, u32[]{:S(2)}, u32[]{:S(2)}) collective-permute-start(bf16[528,128]{1,0:T(8,128)(2,1)} %pad_maximum_fusion.1), channel_id=1, source_target_pairs={{0,8},{1,9},{2,10},{3,11},{4,12},{5,13},{6,14},{7,15},{8,0},{9,1},... | collective-permute-start | bytes 405512 | tf_op jit(solution)/shard_map/ppermute | solution.py:221
  27.3 8.4 %collective-permute-start.4 = (bf16[528,128]{1,0:T(8,128)(2,1)}, bf16[528,128]{1,0:T(8,128)(2,1)}, u32[]{:S(2)}, u32[]{:S(2)}) collective-permute-start(bf16[528,128]{1,0:T(8,128)(2,1)} %pad_maximum_fusion.2), channel_id=1, source_target_pairs={{0,16},{1,17},{2,18},{3,19},{4,20},{5,21},{6,22},{7,23},{8,24},{9,... | collective-permute-start | bytes 405512 | tf_op jit(solution)/shard_map/ppermute | solution.py:221
  29.9 6.9 %collective-permute-start.1 = (f32[54,128]{1,0:T(8,128)S(1)}, f32[54,128]{1,0:T(8,128)S(1)}, u32[]{:S(2)}, u32[]{:S(2)}) collective-permute-start(f32[54,128]{1,0:T(8,128)S(1)} %pad_maximum_fusion.3), channel_id=1, source_target_pairs={{0,8},{1,9},{2,10},{3,11},{4,12},{5,13},{6,14},{7,15},{8,0},{9,1},... | collective-permute-start | bytes 82952 | tf_op jit(solution)/shard_map/ppermute | solution.py:221
  36.8 7.8 %collective-permute-start.7 = (bf16[528,512]{1,0:T(8,128)(2,1)S(1)}, bf16[528,512]{1,0:T(8,128)(2,1)S(1)}, u32[]{:S(2)}, u32[]{:S(2)}) collective-permute-start(bf16[528,512]{1,0:T(8,128)(2,1)S(1)} %pad_maximum_fusion.refs_1_.refs_2_), channel_id=1, source_target_pairs={{0,32},{32,0},{64,96},{96,64},{128,160},{160,128},{192,224},{224,1... | collective-permute-start | bytes 1622024 | tf_op jit(solution)/shard_map/ppermute | solution.py:235
  38.7 11.4 %collective-permute-start.6 = (bf16[528,512]{1,0:T(8,128)(2,1)S(1)}, bf16[528,512]{1,0:T(8,128)(2,1)}, u32[]{:S(2)}, u32[]{:S(2)}) collective-permute-start(bf16[528,512]{1,0:T(8,128)(2,1)S(1)} %pad_maximum_fusion.refs_1_.refs_2_), channel_id=1, source_target_pairs={{0,1},{1,2},{2,3},{3,4},{4,5},{5,6},{6,7},{7,0},{8,9},{9,10},{10,1... | collective-permute-start | bytes 1622024 | tf_op jit(solution)/shard_map/ppermute | solution.py:232
  44.6 11.3 %collective-permute-start.9 = (bf16[528,512]{1,0:T(8,128)(2,1)S(1)}, bf16[528,512]{1,0:T(8,128)(2,1)}, u32[]{:S(2)}, u32[]{:S(2)}) collective-permute-start(bf16[528,512]{1,0:T(8,128)(2,1)S(1)} %collective-permute-done.7), channel_id=1, source_target_pairs={{0,1},{1,2},{2,3},{3,4},{4,5},{5,6},{6,7},{7,0},{8,9},{9,10},{10,1... | collective-permute-start | bytes 1622024 | tf_op jit(solution)/shard_map/ppermute | solution.py:232
  47.6 38.4 %collective-permute-start.3 = (bf16[3,2048,128]{2,1,0:T(8,128)(2,1)}, bf16[3,2048,128]{2,1,0:T(8,128)(2,1)}, u32[]{:S(2)}, u32[]{:S(2)}) collective-permute-start(bf16[3,2048,128]{2,1,0:T(8,128)(2,1)} %constant_dynamic-slice_fusion), channel_id=1, source_target_pairs={{0,8},{1,9},{2,10},{3,11},{4,12},{5,13},{6,14},{7,15},{8,0},{9,1},... | collective-permute-start | bytes 4718600 | tf_op jit(solution)/shard_map/ppermute | solution.py:221
  50.1 15.6 %collective-permute-start.8 = (bf16[528,512]{1,0:T(8,128)(2,1)}, bf16[528,512]{1,0:T(8,128)(2,1)}, u32[]{:S(2)}, u32[]{:S(2)}) collective-permute-start(bf16[528,512]{1,0:T(8,128)(2,1)} %collective-permute-done.6.refs_1_.refs_3_), channel_id=1, source_target_pairs={{0,1},{1,2},{2,3},{3,4},{4,5},{5,6},{6,7},{7,0},{8,9},{9,10},{10,1... | collective-permute-start | bytes 1622024 | tf_op jit(solution)/shard_map/ppermute | solution.py:232
  55.9 13.4 %collective-permute-start.12 = (bf16[528,512]{1,0:T(8,128)(2,1)}, bf16[528,512]{1,0:T(8,128)(2,1)}, u32[]{:S(2)}, u32[]{:S(2)}) collective-permute-start(bf16[528,512]{1,0:T(8,128)(2,1)} %collective-permute-done.9), channel_id=1, source_target_pairs={{0,1},{1,2},{2,3},{3,4},{4,5},{5,6},{6,7},{7,0},{8,9},{9,10},{10,1... | collective-permute-start | bytes 1622024 | tf_op jit(solution)/shard_map/ppermute | solution.py:232
  63.8 10.8 %collective-permute-start.11 = (bf16[528,512]{1,0:T(8,128)(2,1)}, bf16[528,512]{1,0:T(8,128)(2,1)S(1)}, u32[]{:S(2)}, u32[]{:S(2)}) collective-permute-start(bf16[528,512]{1,0:T(8,128)(2,1)} %collective-permute-done.9), channel_id=1, source_target_pairs={{0,32},{32,0},{64,96},{96,64},{128,160},{160,128},{192,224},{224,1... | collective-permute-start | bytes 1622024 | tf_op jit(solution)/shard_map/ppermute | solution.py:235
  65.7 11.8 %collective-permute-start.10 = (bf16[528,512]{1,0:T(8,128)(2,1)}, bf16[528,512]{1,0:T(8,128)(2,1)S(1)}, u32[]{:S(2)}, u32[]{:S(2)}) collective-permute-start(bf16[528,512]{1,0:T(8,128)(2,1)} %collective-permute-done.8.refs_1_.refs_5_), channel_id=1, source_target_pairs={{0,1},{1,2},{2,3},{3,4},{4,5},{5,6},{6,7},{7,0},{8,9},{9,10},{10,1... | collective-permute-start | bytes 1622024 | tf_op jit(solution)/shard_map/ppermute | solution.py:232
  69.3 13.7 %collective-permute-start.14 = (bf16[528,512]{1,0:T(8,128)(2,1)}, bf16[528,512]{1,0:T(8,128)(2,1)S(1)}, u32[]{:S(2)}, u32[]{:S(2)}) collective-permute-start(bf16[528,512]{1,0:T(8,128)(2,1)} %collective-permute-done.12), channel_id=1, source_target_pairs={{0,1},{1,2},{2,3},{3,4},{4,5},{5,6},{6,7},{7,0},{8,9},{9,10},{10,1... | collective-permute-start | bytes 1622024 | tf_op jit(solution)/shard_map/ppermute | solution.py:232
  72.7 10.3 %collective-permute-start.15 = (bf16[528,512]{1,0:T(8,128)(2,1)}, bf16[528,512]{1,0:T(8,128)(2,1)S(1)}, u32[]{:S(2)}, u32[]{:S(2)}) collective-permute-start(bf16[528,512]{1,0:T(8,128)(2,1)} %collective-permute-done.12), channel_id=1, source_target_pairs={{0,32},{32,0},{64,96},{96,64},{128,160},{160,128},{192,224},{224,1... | collective-permute-start | bytes 1622024 | tf_op jit(solution)/shard_map/ppermute | solution.py:235
  77.5 11.5 %collective-permute-start.13 = (bf16[528,512]{1,0:T(8,128)(2,1)S(1)}, bf16[528,512]{1,0:T(8,128)(2,1)S(1)}, u32[]{:S(2)}, u32[]{:S(2)}) collective-permute-start(bf16[528,512]{1,0:T(8,128)(2,1)S(1)} %collective-permute-done.10.refs_2_.refs_7_), channel_id=1, source_target_pairs={{0,1},{1,2},{2,3},{3,4},{4,5},{5,6},{6,7},{7,0},{8,9},{9,10},{10,1... | collective-permute-start | bytes 1622024 | tf_op jit(solution)/shard_map/ppermute | solution.py:232
  86.0 3.9 %collective-permute-start.16 = (bf16[528,512]{1,0:T(8,128)(2,1)S(1)}, bf16[528,512]{1,0:T(8,128)(2,1)S(1)}, u32[]{:S(2)}, u32[]{:S(2)}) collective-permute-start(bf16[528,512]{1,0:T(8,128)(2,1)S(1)} %collective-permute-done.14), channel_id=1, source_target_pairs={{0,32},{32,0},{64,96},{96,64},{128,160},{160,128},{192,224},{224,1... | collective-permute-start | bytes 1622024 | tf_op jit(solution)/shard_map/ppermute | solution.py:235
  90.7 11.3 %collective-permute-start.17 = (bf16[3,2048,128]{2,1,0:T(8,128)(2,1)}, bf16[3,2048,128]{2,1,0:T(8,128)(2,1)}, u32[]{:S(2)}, u32[]{:S(2)}) collective-permute-start(bf16[3,2048,128]{2,1,0:T(8,128)(2,1)} %collective-permute-done.3.refs_0_), channel_id=1, source_target_pairs={{0,32},{32,0},{64,96},{96,64},{128,160},{160,128},{192,224},{224,1... | collective-permute-start | bytes 4718600 | tf_op jit(solution)/shard_map/ppermute | solution.py:235
  108.0 25.6 %collective-permute-start.18 = (f32[1168,128]{1,0:T(8,128)S(1)}, f32[1168,128]{1,0:T(8,128)S(1)}, u32[]{:S(2)}, u32[]{:S(2)}) collective-permute-start(f32[1168,128]{1,0:T(8,128)S(1)} %get-tuple-element.54), channel_id=1, source_target_pairs={{0,8},{1,9},{2,10},{3,11},{4,12},{5,13},{6,14},{7,15},{8,0},{9,1},... | collective-permute-start | bytes 1794056 | tf_op jit(solution)/shard_map/ppermute | solution.py:221
  (16 other events, 24.5 us)

commit v9 on v7

--- a/solution.py
+++ b/solution.py
@@ -12,7 +12,7 @@
 TAPS = 7
 HALO = 16
 CHUNKS = 8
-UNROLL = 8
+UNROLL = 16
 LANES = 128
 RING = 8
 LINES = 4

time: 134 us -> 134 us (level)
  no operation moved by 1% of the time
where the time goes in v9:
time: 134 us; the launch traced here: 133 us
  starting transfers between devices  70.3 us (52%)
  blocking collectives  23.3 us (17%)
  Pallas kernels  15.5 us (12%)
  local copies, waits for them, and re-layouts  14.3 us (11%)
  waiting for transfers between devices  6.41 us (5%)
  other arithmetic  2.41 us (2%)
    ppermute x7, starting transfers between devices, onward(): return lax.ppermute(block, ('ctx', 'ch'), route)  29.9 us
    all_to_all x1, blocking collectives, per_device(): lax.all_to_all(sent.reshape(2 * blocks, MODES, LANES), ('ctx', 'ch'), 0,...  23.3 us
    ppermute x6, starting transfers between devices, beside(): lax.ppermute(block, 'ch', [(z * ring + y, (z ^ step) * ring + y) for z in...  16.2 us
    ppermute x5, starting transfers between devices, other_core(): return lax.ppermute(block, 'ctx', [(i, i ^ 1) for i in range(blocks)])  12.2 us
    ppermute x1, starting transfers between devices, per_device(): lax.ppermute(tokens[rows - HALO:], 'ctx', [(i, i + 1) for i in range(bloc...  12 us
    pallas_call x2, Pallas kernels, local_part(): pl.pallas_call(functools.partial(local_kernel, len(blocks), len(in_weight...  8.48 us
    unnamed x40, local copies, waits for them, and re-layouts  8.23 us
    pallas_call x3, Pallas kernels, project(): pl.pallas_call(functools.partial(project_kernel, len(blocks), len(in_weig...  4.91 us
  transfers between devices with their start and end apart: 19, of which 5 were waited for; matrix products, arithmetic and copies ran while one was open for 6% of the time, Pallas kernels for 6%

profile of v9, /device:TPU:1, one launch (start us, length us, event | category | flops | bytes accessed | tf_op | source)
XLA Modules:
  0.0 132.7 jit_solution(10939853888377383947)
XLA Ops:
  0.7 12.0 %collective-permute-start.1 = (bf16[16,128]{1,0:T(8,128)(2,1)S(1)}, bf16[16,128]{1,0:T(8,128)(2,1)S(1)}, u32[]{:S(2)}, u32[]{:S(2)}) collective-permute-start(bf16[16,128]{1,0:T(8,128)(2,1)S(1)} %slice.33), channel_id=1, source_target_pairs={{0,32},{32,64},{64,96},{96,128},{128,160},{160,192},{192,224},{224... | collective-permute-start | bytes 12296 | tf_op jit(solution)/shard_map/ppermute | solution.py:253
  14.9 3.1 %collective-permute-start = (f32[54,128]{1,0:T(8,128)S(1)}, f32[54,128]{1,0:T(8,128)S(1)}, u32[]{:S(2)}, u32[]{:S(2)}) collective-permute-start(f32[54,128]{1,0:T(8,128)S(1)} %pad_maximum_fusion.3), channel_id=1, source_target_pairs={{0,8},{1,9},{2,10},{3,11},{4,12},{5,13},{6,14},{7,15},{8,0},{9,1},... | collective-permute-start | bytes 82952 | tf_op jit(solution)/shard_map/ppermute | solution.py:221
  19.9 4.0 %collective-permute-start.5 = (bf16[528,128]{1,0:T(8,128)(2,1)S(1)}, bf16[528,128]{1,0:T(8,128)(2,1)S(1)}, u32[]{:S(2)}, u32[]{:S(2)}) collective-permute-start(bf16[528,128]{1,0:T(8,128)(2,1)S(1)} %pad_maximum_fusion.1), channel_id=1, source_target_pairs={{0,24},{1,25},{2,26},{3,27},{4,28},{5,29},{6,30},{7,31},{8,16},{9,... | collective-permute-start | bytes 405512 | tf_op jit(solution)/shard_map/ppermute | solution.py:221
  23.9 2.2 %collective-permute-start.2 = (bf16[528,128]{1,0:T(8,128)(2,1)S(1)}, bf16[528,128]{1,0:T(8,128)(2,1)S(1)}, u32[]{:S(2)}, u32[]{:S(2)}) collective-permute-start(bf16[528,128]{1,0:T(8,128)(2,1)S(1)} %pad_maximum_fusion.1), channel_id=1, source_target_pairs={{0,8},{1,9},{2,10},{3,11},{4,12},{5,13},{6,14},{7,15},{8,0},{9,1},... | collective-permute-start | bytes 405512 | tf_op jit(solution)/shard_map/ppermute | solution.py:221
  26.1 3.1 %collective-permute-start.4 = (bf16[528,128]{1,0:T(8,128)(2,1)S(1)}, bf16[528,128]{1,0:T(8,128)(2,1)S(1)}, u32[]{:S(2)}, u32[]{:S(2)}) collective-permute-start(bf16[528,128]{1,0:T(8,128)(2,1)S(1)} %pad_maximum_fusion.2), channel_id=1, source_target_pairs={{0,16},{1,17},{2,18},{3,19},{4,20},{5,21},{6,22},{7,23},{8,24},{9,... | collective-permute-start | bytes 405512 | tf_op jit(solution)/shard_map/ppermute | solution.py:221
  29.2 2.8 %constant_dynamic-slice_fusion = bf16[3,2048,128]{2,1,0:T(8,128)(2,1)} fusion(bf16[3,4096,128]{2,1,0:T(8,128)(2,1)} %refs_1_.1, s32[]{:T(128)S(6)} %select_n.56), kind=kLoop, calls=%fused_computation.14 | loop fusion | bytes 3145732 | tf_op jit(solution)/shard_map/dynamic_slice | solution.py:261
  32.1 2.2 %collective-permute-done.4 = bf16[528,128]{1,0:T(8,128)(2,1)S(1)} collective-permute-done((bf16[528,128]{1,0:T(8,128)(2,1)S(1)}, bf16[528,128]{1,0:T(8,128)(2,1)S(1)}, u32[]{:S(2)}, u32[]{:S(2)}) %collective-permute-start.4) | collective-permute-done | bytes 135200 | tf_op jit(solution)/shard_map/ppermute | solution.py:221
  34.3 1.9 %collective-permute-start.7 = (bf16[528,512]{1,0:T(8,128)(2,1)S(1)}, bf16[528,512]{1,0:T(8,128)(2,1)S(1)}, u32[]{:S(2)}, u32[]{:S(2)}) collective-permute-start(bf16[528,512]{1,0:T(8,128)(2,1)S(1)} %pad_maximum_fusion.refs_1_.refs_2_), channel_id=1, source_target_pairs={{0,32},{32,0},{64,96},{96,64},{128,160},{160,128},{192,224},{224,1... | collective-permute-start | bytes 1622024 | tf_op jit(solution)/shard_map/ppermute | solution.py:235
  36.3 5.1 %collective-permute-start.6 = (bf16[528,512]{1,0:T(8,128)(2,1)S(1)}, bf16[528,512]{1,0:T(8,128)(2,1)}, u32[]{:S(2)}, u32[]{:S(2)}) collective-permute-start(bf16[528,512]{1,0:T(8,128)(2,1)S(1)} %pad_maximum_fusion.refs_1_.refs_2_), channel_id=1, source_target_pairs={{0,1},{1,2},{2,3},{3,4},{4,5},{5,6},{6,7},{7,0},{8,9},{9,10},{10,1... | collective-permute-start | bytes 1622024 | tf_op jit(solution)/shard_map/ppermute | solution.py:232
  42.2 3.0 %collective-permute-start.9 = (bf16[528,512]{1,0:T(8,128)(2,1)S(1)}, bf16[528,512]{1,0:T(8,128)(2,1)}, u32[]{:S(2)}, u32[]{:S(2)}) collective-permute-start(bf16[528,512]{1,0:T(8,128)(2,1)S(1)} %collective-permute-done.7), channel_id=1, source_target_pairs={{0,1},{1,2},{2,3},{3,4},{4,5},{5,6},{6,7},{7,0},{8,9},{9,10},{10,1... | collective-permute-start | bytes 1622024 | tf_op jit(solution)/shard_map/ppermute | solution.py:232
  45.2 1.9 %collective-permute-start.3 = (bf16[3,2048,128]{2,1,0:T(8,128)(2,1)}, bf16[3,2048,128]{2,1,0:T(8,128)(2,1)}, u32[]{:S(2)}, u32[]{:S(2)}) collective-permute-start(bf16[3,2048,128]{2,1,0:T(8,128)(2,1)} %constant_dynamic-slice_fusion), channel_id=1, source_target_pairs={{0,8},{1,9},{2,10},{3,11},{4,12},{5,13},{6,14},{7,15},{8,0},{9,1},... | collective-permute-start | bytes 4718600 | tf_op jit(solution)/shard_map/ppermute | solution.py:221
  47.6 5.1 %collective-permute-start.8 = (bf16[528,512]{1,0:T(8,128)(2,1)}, bf16[528,512]{1,0:T(8,128)(2,1)}, u32[]{:S(2)}, u32[]{:S(2)}) collective-permute-start(bf16[528,512]{1,0:T(8,128)(2,1)} %collective-permute-done.6.refs_1_.refs_3_), channel_id=1, source_target_pairs={{0,1},{1,2},{2,3},{3,4},{4,5},{5,6},{6,7},{7,0},{8,9},{9,10},{10,1... | collective-permute-start | bytes 1622024 | tf_op jit(solution)/shard_map/ppermute | solution.py:232
  53.4 5.1 %collective-permute-start.12 = (bf16[528,512]{1,0:T(8,128)(2,1)}, bf16[528,512]{1,0:T(8,128)(2,1)}, u32[]{:S(2)}, u32[]{:S(2)}) collective-permute-start(bf16[528,512]{1,0:T(8,128)(2,1)} %collective-permute-done.9), channel_id=1, source_target_pairs={{0,1},{1,2},{2,3},{3,4},{4,5},{5,6},{6,7},{7,0},{8,9},{9,10},{10,1... | collective-permute-start | bytes 1622024 | tf_op jit(solution)/shard_map/ppermute | solution.py:232
  63.3 3.6 %collective-permute-start.10 = (bf16[528,512]{1,0:T(8,128)(2,1)}, bf16[528,512]{1,0:T(8,128)(2,1)S(1)}, u32[]{:S(2)}, u32[]{:S(2)}) collective-permute-start(bf16[528,512]{1,0:T(8,128)(2,1)} %collective-permute-done.8.refs_1_.refs_5_), channel_id=1, source_target_pairs={{0,1},{1,2},{2,3},{3,4},{4,5},{5,6},{6,7},{7,0},{8,9},{9,10},{10,1... | collective-permute-start | bytes 1622024 | tf_op jit(solution)/shard_map/ppermute | solution.py:232
  66.8 3.3 %collective-permute-start.14 = (bf16[528,512]{1,0:T(8,128)(2,1)}, bf16[528,512]{1,0:T(8,128)(2,1)S(1)}, u32[]{:S(2)}, u32[]{:S(2)}) collective-permute-start(bf16[528,512]{1,0:T(8,128)(2,1)} %collective-permute-done.12), channel_id=1, source_target_pairs={{0,1},{1,2},{2,3},{3,4},{4,5},{5,6},{6,7},{7,0},{8,9},{9,10},{10,1... | collective-permute-start | bytes 1622024 | tf_op jit(solution)/shard_map/ppermute | solution.py:232
  72.1 2.0 %shard_map.74.refs_3_ = f32[3,528,128]{2,1,0:T(8,128)S(1)} custom-call(s32[64]{0:T(128)S(1)} %dynamic-slice_bitcast_fusion.ids, bf16[3,4096,128]{2,1,0:T(8,128)(2,1)S(1)} %copy-done, bf16[528,512]{1,0:T(8,128)(2,1)} %collective-permute-done.6.refs_1_.refs_3_, ...), custom_call_target="tpu_custom_call", output_to_operand_aliasing={{}: (4, {})} | custom-call | flops 528 | bytes 528 | tf_op jit(solution)/shard_map/pallas_call | solution.py:62
  75.0 4.7 %collective-permute-start.13 = (bf16[528,512]{1,0:T(8,128)(2,1)S(1)}, bf16[528,512]{1,0:T(8,128)(2,1)S(1)}, u32[]{:S(2)}, u32[]{:S(2)}) collective-permute-start(bf16[528,512]{1,0:T(8,128)(2,1)S(1)} %collective-permute-done.10.refs_2_.refs_7_), channel_id=1, source_target_pairs={{0,1},{1,2},{2,3},{3,4},{4,5},{5,6},{6,7},{7,0},{8,9},{9,10},{10,1... | collective-permute-start | bytes 1622024 | tf_op jit(solution)/shard_map/ppermute | solution.py:232
  81.3 2.2 %collective-permute-done.3.refs_0_ = bf16[3,2048,128]{2,1,0:T(8,128)(2,1)} collective-permute-done((bf16[3,2048,128]{2,1,0:T(8,128)(2,1)}, bf16[3,2048,128]{2,1,0:T(8,128)(2,1)}, u32[]{:S(2)}, u32[]{:S(2)}) %collective-permute-start.3) | collective-permute-done | bytes 1572896 | tf_op jit(solution)/shard_map/ppermute | solution.py:221
  83.5 2.2 %collective-permute-start.16 = (bf16[528,512]{1,0:T(8,128)(2,1)S(1)}, bf16[528,512]{1,0:T(8,128)(2,1)S(1)}, u32[]{:S(2)}, u32[]{:S(2)}) collective-permute-start(bf16[528,512]{1,0:T(8,128)(2,1)S(1)} %collective-permute-done.14), channel_id=1, source_target_pairs={{0,32},{32,0},{64,96},{96,64},{128,160},{160,128},{192,224},{224,1... | collective-permute-start | bytes 1622024 | tf_op jit(solution)/shard_map/ppermute | solution.py:235
  88.3 4.2 %collective-permute-start.17 = (bf16[3,2048,128]{2,1,0:T(8,128)(2,1)}, bf16[3,2048,128]{2,1,0:T(8,128)(2,1)}, u32[]{:S(2)}, u32[]{:S(2)}) collective-permute-start(bf16[3,2048,128]{2,1,0:T(8,128)(2,1)} %collective-permute-done.3.refs_0_), channel_id=1, source_target_pairs={{0,32},{32,0},{64,96},{96,64},{128,160},{160,128},{192,224},{224,1... | collective-permute-start | bytes 4718600 | tf_op jit(solution)/shard_map/ppermute | solution.py:235
  96.9 2.7 %shard_map.76 = (f32[1168,128]{1,0:T(8,128)S(1)}, f32[2,16,16,128]{3,2,1,0:T(8,128)S(1)}) custom-call(s32[3]{0:T(128)S(1)} %pad_add_fusion.seat, s32[64]{0:T(128)S(1)} %dynamic-slice_bitcast_fusion.ids, f32[3,7,128]{2,1,0:T(8,128)S(1)} %copy-done.18, f32[16,128]{1,0:T(8,128)S(1)} %multiply_bitcast_fusion.weights, f32[16,128]{1,0:T(8,128)S(1)} %bitcast.20, ...), custom_call_target="tpu_custom_call" | custom-call | flops 7208960 | bytes 1310720 | tf_op jit(solution)/shard_map/pallas_call | solution.py:136
  99.7 5.8 %shard_map.77 = (f32[1168,128]{1,0:T(8,128)S(1)}, f32[2,16,16,128]{3,2,1,0:T(8,128)S(1)}) custom-call(s32[3]{0:T(128)S(1)} %pad_add_fusion.2.seat, s32[64]{0:T(128)S(1)} %dynamic-slice_bitcast_fusion.ids, f32[3,7,128]{2,1,0:T(8,128)S(1)} %reshape.22.taps, f32[16,128]{1,0:T(8,128)S(1)} %get-tuple-element.58.weights, ...), custom_call_target="tpu_custom_call", output_to_operand_aliasing={{1}: (16, {})} | custom-call | flops 7208960 | bytes 1310720 | tf_op jit(solution)/shard_map/pallas_call | solution.py:136
  107.4 23.3 %all_to_all.5.arrived = f32[32,16,128]{2,1,0:T(8,128)S(1)} all-to-all(f32[32,16,128]{2,1,0:T(8,128)S(1)} %bitcast.18), channel_id=1, replica_groups={{0,32,64,96,128,160,192,224,256,288,320,352,384,416,448,480,8,40,72,104..., dimensions={0} | all-to-all | bytes 524288 | tf_op jit(solution)/shard_map/all_to_all | solution.py:307
  130.6 2.1 %shard_map.78 = f32[1024,128]{1,0:T(8,128)} custom-call(s32[3]{0:T(128)S(1)} %pad_add_fusion.seat, f32[32,16,128]{2,1,0:T(8,128)S(1)} %all_to_all.5.arrived, f32[1168,128]{1,0:T(8,128)S(1)} %get-tuple-element.51.mine, f32[1168,128]{1,0:T(8,128)S(1)} %collective-permute-done.18.other, f32[16,128]{1,0:T(8,128)S(1)} %multiply_bitcast_fusion.weights, ...), custom_call_target="tpu_custom_call" | custom-call | flops 4718592 | bytes 1572864 | tf_op jit(solution)/shard_map/pallas_call | solution.py:196
  (79 shorter events, 24.6 us)
Async XLA Ops:
  0.7 18.5 %collective-permute-start.1 = (bf16[16,128]{1,0:T(8,128)(2,1)S(1)}, bf16[16,128]{1,0:T(8,128)(2,1)S(1)}, u32[]{:S(2)}, u32[]{:S(2)}) collective-permute-start(bf16[16,128]{1,0:T(8,128)(2,1)S(1)} %slice.33), channel_id=1, source_target_pairs={{0,32},{32,64},{64,96},{96,128},{128,160},{160,192},{192,224},{224... | collective-permute-start | bytes 12296 | tf_op jit(solution)/shard_map/ppermute | solution.py:253
  14.9 19.4 %collective-permute-start = (f32[54,128]{1,0:T(8,128)S(1)}, f32[54,128]{1,0:T(8,128)S(1)}, u32[]{:S(2)}, u32[]{:S(2)}) collective-permute-start(f32[54,128]{1,0:T(8,128)S(1)} %pad_maximum_fusion.3), channel_id=1, source_target_pairs={{0,8},{1,9},{2,10},{3,11},{4,12},{5,13},{6,14},{7,15},{8,0},{9,1},... | collective-permute-start | bytes 82952 | tf_op jit(solution)/shard_map/ppermute | solution.py:221
  19.9 14.3 %collective-permute-start.5 = (bf16[528,128]{1,0:T(8,128)(2,1)S(1)}, bf16[528,128]{1,0:T(8,128)(2,1)S(1)}, u32[]{:S(2)}, u32[]{:S(2)}) collective-permute-start(bf16[528,128]{1,0:T(8,128)(2,1)S(1)} %pad_maximum_fusion.1), channel_id=1, source_target_pairs={{0,24},{1,25},{2,26},{3,27},{4,28},{5,29},{6,30},{7,31},{8,16},{9,... | collective-permute-start | bytes 405512 | tf_op jit(solution)/shard_map/ppermute | solution.py:221
  23.9 10.3 %collective-permute-start.2 = (bf16[528,128]{1,0:T(8,128)(2,1)S(1)}, bf16[528,128]{1,0:T(8,128)(2,1)S(1)}, u32[]{:S(2)}, u32[]{:S(2)}) collective-permute-start(bf16[528,128]{1,0:T(8,128)(2,1)S(1)} %pad_maximum_fusion.1), channel_id=1, source_target_pairs={{0,8},{1,9},{2,10},{3,11},{4,12},{5,13},{6,14},{7,15},{8,0},{9,1},... | collective-permute-start | bytes 405512 | tf_op jit(solution)/shard_map/ppermute | solution.py:221
  26.1 8.1 %collective-permute-start.4 = (bf16[528,128]{1,0:T(8,128)(2,1)S(1)}, bf16[528,128]{1,0:T(8,128)(2,1)S(1)}, u32[]{:S(2)}, u32[]{:S(2)}) collective-permute-start(bf16[528,128]{1,0:T(8,128)(2,1)S(1)} %pad_maximum_fusion.2), channel_id=1, source_target_pairs={{0,16},{1,17},{2,18},{3,19},{4,20},{5,21},{6,22},{7,23},{8,24},{9,... | collective-permute-start | bytes 405512 | tf_op jit(solution)/shard_map/ppermute | solution.py:221
  29.2 30.1 %copy-start = (bf16[3,4096,128]{2,1,0:T(8,128)(2,1)S(1)}, bf16[3,4096,128]{2,1,0:T(8,128)(2,1)}, u32[]{:S(2)}) copy-start(bf16[3,4096,128]{2,1,0:T(8,128)(2,1)} %refs_1_.1) | copy-start | bytes 9437188
  34.3 7.8 %collective-permute-start.7 = (bf16[528,512]{1,0:T(8,128)(2,1)S(1)}, bf16[528,512]{1,0:T(8,128)(2,1)S(1)}, u32[]{:S(2)}, u32[]{:S(2)}) collective-permute-start(bf16[528,512]{1,0:T(8,128)(2,1)S(1)} %pad_maximum_fusion.refs_1_.refs_2_), channel_id=1, source_target_pairs={{0,32},{32,0},{64,96},{96,64},{128,160},{160,128},{192,224},{224,1... | collective-permute-start | bytes 1622024 | tf_op jit(solution)/shard_map/ppermute | solution.py:235
  36.3 11.4 %collective-permute-start.6 = (bf16[528,512]{1,0:T(8,128)(2,1)S(1)}, bf16[528,512]{1,0:T(8,128)(2,1)}, u32[]{:S(2)}, u32[]{:S(2)}) collective-permute-start(bf16[528,512]{1,0:T(8,128)(2,1)S(1)} %pad_maximum_fusion.refs_1_.refs_2_), channel_id=1, source_target_pairs={{0,1},{1,2},{2,3},{3,4},{4,5},{5,6},{6,7},{7,0},{8,9},{9,10},{10,1... | collective-permute-start | bytes 1622024 | tf_op jit(solution)/shard_map/ppermute | solution.py:232
  42.2 11.3 %collective-permute-start.9 = (bf16[528,512]{1,0:T(8,128)(2,1)S(1)}, bf16[528,512]{1,0:T(8,128)(2,1)}, u32[]{:S(2)}, u32[]{:S(2)}) collective-permute-start(bf16[528,512]{1,0:T(8,128)(2,1)S(1)} %collective-permute-done.7), channel_id=1, source_target_pairs={{0,1},{1,2},{2,3},{3,4},{4,5},{5,6},{6,7},{7,0},{8,9},{9,10},{10,1... | collective-permute-start | bytes 1622024 | tf_op jit(solution)/shard_map/ppermute | solution.py:232
  45.2 38.4 %collective-permute-start.3 = (bf16[3,2048,128]{2,1,0:T(8,128)(2,1)}, bf16[3,2048,128]{2,1,0:T(8,128)(2,1)}, u32[]{:S(2)}, u32[]{:S(2)}) collective-permute-start(bf16[3,2048,128]{2,1,0:T(8,128)(2,1)} %constant_dynamic-slice_fusion), channel_id=1, source_target_pairs={{0,8},{1,9},{2,10},{3,11},{4,12},{5,13},{6,14},{7,15},{8,0},{9,1},... | collective-permute-start | bytes 4718600 | tf_op jit(solution)/shard_map/ppermute | solution.py:221
  47.6 15.6 %collective-permute-start.8 = (bf16[528,512]{1,0:T(8,128)(2,1)}, bf16[528,512]{1,0:T(8,128)(2,1)}, u32[]{:S(2)}, u32[]{:S(2)}) collective-permute-start(bf16[528,512]{1,0:T(8,128)(2,1)} %collective-permute-done.6.refs_1_.refs_3_), channel_id=1, source_target_pairs={{0,1},{1,2},{2,3},{3,4},{4,5},{5,6},{6,7},{7,0},{8,9},{9,10},{10,1... | collective-permute-start | bytes 1622024 | tf_op jit(solution)/shard_map/ppermute | solution.py:232
  53.4 13.4 %collective-permute-start.12 = (bf16[528,512]{1,0:T(8,128)(2,1)}, bf16[528,512]{1,0:T(8,128)(2,1)}, u32[]{:S(2)}, u32[]{:S(2)}) collective-permute-start(bf16[528,512]{1,0:T(8,128)(2,1)} %collective-permute-done.9), channel_id=1, source_target_pairs={{0,1},{1,2},{2,3},{3,4},{4,5},{5,6},{6,7},{7,0},{8,9},{9,10},{10,1... | collective-permute-start | bytes 1622024 | tf_op jit(solution)/shard_map/ppermute | solution.py:232
  61.3 10.8 %collective-permute-start.11 = (bf16[528,512]{1,0:T(8,128)(2,1)}, bf16[528,512]{1,0:T(8,128)(2,1)S(1)}, u32[]{:S(2)}, u32[]{:S(2)}) collective-permute-start(bf16[528,512]{1,0:T(8,128)(2,1)} %collective-permute-done.9), channel_id=1, source_target_pairs={{0,32},{32,0},{64,96},{96,64},{128,160},{160,128},{192,224},{224,1... | collective-permute-start | bytes 1622024 | tf_op jit(solution)/shard_map/ppermute | solution.py:235
  63.3 11.8 %collective-permute-start.10 = (bf16[528,512]{1,0:T(8,128)(2,1)}, bf16[528,512]{1,0:T(8,128)(2,1)S(1)}, u32[]{:S(2)}, u32[]{:S(2)}) collective-permute-start(bf16[528,512]{1,0:T(8,128)(2,1)} %collective-permute-done.8.refs_1_.refs_5_), channel_id=1, source_target_pairs={{0,1},{1,2},{2,3},{3,4},{4,5},{5,6},{6,7},{7,0},{8,9},{9,10},{10,1... | collective-permute-start | bytes 1622024 | tf_op jit(solution)/shard_map/ppermute | solution.py:232
  66.8 13.7 %collective-permute-start.14 = (bf16[528,512]{1,0:T(8,128)(2,1)}, bf16[528,512]{1,0:T(8,128)(2,1)S(1)}, u32[]{:S(2)}, u32[]{:S(2)}) collective-permute-start(bf16[528,512]{1,0:T(8,128)(2,1)} %collective-permute-done.12), channel_id=1, source_target_pairs={{0,1},{1,2},{2,3},{3,4},{4,5},{5,6},{6,7},{7,0},{8,9},{9,10},{10,1... | collective-permute-start | bytes 1622024 | tf_op jit(solution)/shard_map/ppermute | solution.py:232
  70.2 10.3 %collective-permute-start.15 = (bf16[528,512]{1,0:T(8,128)(2,1)}, bf16[528,512]{1,0:T(8,128)(2,1)S(1)}, u32[]{:S(2)}, u32[]{:S(2)}) collective-permute-start(bf16[528,512]{1,0:T(8,128)(2,1)} %collective-permute-done.12), channel_id=1, source_target_pairs={{0,32},{32,0},{64,96},{96,64},{128,160},{160,128},{192,224},{224,1... | collective-permute-start | bytes 1622024 | tf_op jit(solution)/shard_map/ppermute | solution.py:235
  72.1 2.0 %copy-start.6 = (bf16[528,512]{1,0:T(8,128)(2,1)}, bf16[528,512]{1,0:T(8,128)(2,1)S(1)}, u32[]{:S(2)}) copy-start(bf16[528,512]{1,0:T(8,128)(2,1)S(1)} %collective-permute-done.11.refs_2_.refs_4_) | copy-start | bytes 1622020
  75.0 11.5 %collective-permute-start.13 = (bf16[528,512]{1,0:T(8,128)(2,1)S(1)}, bf16[528,512]{1,0:T(8,128)(2,1)S(1)}, u32[]{:S(2)}, u32[]{:S(2)}) collective-permute-start(bf16[528,512]{1,0:T(8,128)(2,1)S(1)} %collective-permute-done.10.refs_2_.refs_7_), channel_id=1, source_target_pairs={{0,1},{1,2},{2,3},{3,4},{4,5},{5,6},{6,7},{7,0},{8,9},{9,10},{10,1... | collective-permute-start | bytes 1622024 | tf_op jit(solution)/shard_map/ppermute | solution.py:232
  83.5 3.9 %collective-permute-start.16 = (bf16[528,512]{1,0:T(8,128)(2,1)S(1)}, bf16[528,512]{1,0:T(8,128)(2,1)S(1)}, u32[]{:S(2)}, u32[]{:S(2)}) collective-permute-start(bf16[528,512]{1,0:T(8,128)(2,1)S(1)} %collective-permute-done.14), channel_id=1, source_target_pairs={{0,32},{32,0},{64,96},{96,64},{128,160},{160,128},{192,224},{224,1... | collective-permute-start | bytes 1622024 | tf_op jit(solution)/shard_map/ppermute | solution.py:235
  88.3 11.4 %collective-permute-start.17 = (bf16[3,2048,128]{2,1,0:T(8,128)(2,1)}, bf16[3,2048,128]{2,1,0:T(8,128)(2,1)}, u32[]{:S(2)}, u32[]{:S(2)}) collective-permute-start(bf16[3,2048,128]{2,1,0:T(8,128)(2,1)} %collective-permute-done.3.refs_0_), channel_id=1, source_target_pairs={{0,32},{32,0},{64,96},{96,64},{128,160},{160,128},{192,224},{224,1... | collective-permute-start | bytes 4718600 | tf_op jit(solution)/shard_map/ppermute | solution.py:235
  96.9 2.8 %copy-start.5 = (bf16[528,512]{1,0:T(8,128)(2,1)S(1)}, bf16[528,512]{1,0:T(8,128)(2,1)}, u32[]{:S(2)}) copy-start(bf16[528,512]{1,0:T(8,128)(2,1)} %copy-done.3) | copy-start | bytes 1622020
  96.9 2.8 %copy-start.7 = (bf16[528,512]{1,0:T(8,128)(2,1)S(1)}, bf16[528,512]{1,0:T(8,128)(2,1)}, u32[]{:S(2)}) copy-start(bf16[528,512]{1,0:T(8,128)(2,1)} %copy-done.6) | copy-start | bytes 1622020
  96.9 2.8 %copy-start.10 = (bf16[528,512]{1,0:T(8,128)(2,1)S(1)}, bf16[528,512]{1,0:T(8,128)(2,1)}, u32[]{:S(2)}) copy-start(bf16[528,512]{1,0:T(8,128)(2,1)} %copy-done.8) | copy-start | bytes 1622020
  105.4 25.2 %collective-permute-start.18 = (f32[1168,128]{1,0:T(8,128)S(1)}, f32[1168,128]{1,0:T(8,128)S(1)}, u32[]{:S(2)}, u32[]{:S(2)}) collective-permute-start(f32[1168,128]{1,0:T(8,128)S(1)} %get-tuple-element.52), channel_id=1, source_target_pairs={{0,8},{1,9},{2,10},{3,11},{4,12},{5,13},{6,14},{7,15},{8,0},{9,1},... | collective-permute-start | bytes 1794056 | tf_op jit(solution)/shard_map/ppermute | solution.py:221
  (15 other events, 20.1 us)
